TPU v7x, 32 devices: a whole 2x2x4 slice. The times are simulated.
32 devices in a mesh: req: 4 (over y, x), seq: 8 (over z, core).
Axes of the slice: x: 2, y: 2, z: 4, core: 2. Of those that a mesh axis runs over, the one named last changes fastest.
Arguments:
- hidden_in: bfloat16 [4, 1024, 1600], P('req', 'seq'), may hold values from -6 to 6
- mamba_in: bfloat16 [4, 1024, 3200], P('req', 'seq'), may hold values from -6 to 6
- conv_weight: float32 [4, 3200], replicated, may hold values from -3 to 3
- conv_bias: float32 [3200], replicated, may hold values from -3 to 3
- x_proj: bfloat16 [3200, 132], replicated, may hold values from -0.109375 to 0.109375
- dt_proj: bfloat16 [100, 3200], replicated, may hold values from -0.625 to 0.625
- dt_bias: float32 [3200], replicated, may hold values from -2 to 0.5
- decay_rate: float32 [3200], replicated, may hold values from 9.765625e-05 to 0.05
- skip_gain: float32 [3200], replicated, may hold values from 0.5 to 1.5
- out_proj: bfloat16 [3200, 1600], replicated, may hold values from -0.109375 to 0.109375
- norm_gain: float32 [1600], replicated, may hold values from 0.3 to 1.7
- mlp_gate: bfloat16 [1600, 5504], P(None, 'req'), may hold values from -0.15625 to 0.15625
- mlp_up: bfloat16 [1600, 5504], P(None, 'req'), may hold values from -0.15625 to 0.15625
- mlp_down: bfloat16 [5504, 1600], P('req'), may hold values from -0.078125 to 0.078125
- cache_state: float32 [4, 8, 16, 3200], P('req', 'seq'), may hold values from -6 to 6
- cache_edge: bfloat16 [4, 8, 3, 3200], P('req', 'seq'), may hold values from -6 to 6
- req_lengths: int32 [4, 4], P('req'), may hold values from 1 to 768, 1024 in all within a row
- cont_flag: int32 [4, 4], P('req'), may hold values from 0 to 1, as said below
- cache_source: int32 [4, 4], P('req'), may hold values from 0 to 7, as said below
- owner_slot: int32 [4, 4], P('req'), may hold values from 0 to 7, as said below
Outputs:
- block_out: bfloat16 [4, 1024, 1600], P('req', 'seq')
- new_state: float32 [4, 8, 16, 3200], P('req', 'seq')
- new_edge: bfloat16 [4, 8, 3, 3200], P('req', 'seq')
Inputs may be any that keep to these rules, and one draw needn't show every extreme that they name: `req_lengths`: each row sums to 1024; its largest entry is exactly 768. `owner_slot`: the 4 entries of a row are distinct; slots 0 and 7 each own a request of every group. `cont_flag`: request 0 of every group continues; request 1 of group 0 does not; the others continue with probability one half. `cache_source`: request 0 reads slot 4 in groups 0, 4, 8 ..., slot 7 in groups 1, 5 ..., slot 0 in groups 2, 6 ..., slot 1 in groups 3, 7 ...; other requests read any slot.
All inputs are finite; a program needn't handle non-finite values.
Results may differ from a plain program's by a relative error of at most 0.007.
Values may be sent and summed in bfloat16 or wider, within the bound.
No kernel may reach another device: no remote copies, remote signals or barrier semaphores. Data moves between devices by JAX's collectives and lax.ppermute only.
A program may use at most 256 MiB of HBM per device.

v0:
```python
import functools

import jax
import jax.numpy as jnp
from jax import lax
from jax.experimental import pallas as pl
from jax.experimental.pallas import tpu as pltpu
from jax.sharding import PartitionSpec as P

STATE = 16
NORM_EPS = 1e-06
LANE = 128
FAR = 1e30
OFFER = 24
LOG2E = 1.4426950408889634
F32 = jnp.float32
BF16 = jnp.bfloat16


def request_marks(lens_ref, first_pos):
    marks = []
    begin = -first_pos
    for r in range(lens_ref.shape[1]):
        end = begin + lens_ref[0, r]
        marks.append((begin, end))
        begin = end
    return marks


def segment_of(index, marks):
    total = jnp.zeros(index.shape, jnp.int32)
    for begin, _ in marks:
        total = total + (index >= begin).astype(jnp.int32)
    return total


def segment_masks(row_count, marks):
    row = lax.broadcasted_iota(jnp.int32, (row_count, row_count), 0)
    col = lax.broadcasted_iota(jnp.int32, (row_count, row_count), 1)
    same = segment_of(row, marks) == segment_of(col, marks)
    return row, col, same


def three_parts(values):
    high = values.astype(BF16)
    rest = values - high.astype(F32)
    middle = rest.astype(BF16)
    low = (rest - middle.astype(F32)).astype(BF16)
    return jnp.concatenate([high, middle, low], axis=0)


def tripled(mask):
    one = mask.astype(F32).astype(BF16)
    return jnp.concatenate([one, one, one], axis=1)


def rate_block(rate_row):
    power = lax.broadcasted_iota(jnp.int32, (STATE, rate_row.shape[1]), 0) + 1
    return power.astype(F32) * rate_row


def row_of(vec_ref, tile):
    return vec_ref[pl.ds(tile, 1), :]


def wide_row(vec_ref, first, count):
    return jnp.concatenate([vec_ref[first + k : first + k + 1, :] for k in range(count)], axis=1)


def sums_of_eight(parts):
    sub = lax.broadcasted_iota(jnp.int32, parts[0].shape, 0)
    stride = 1
    while len(parts) > 1:
        first = jnp.bitwise_and(sub, stride) == 0
        parts = [
            jnp.where(first, a, b) + pltpu.roll(jnp.where(first, b, a), stride, 0)
            for a, b in zip(parts[0::2], parts[1::2])
        ]
        stride = 2 * stride
    return parts[0]


def softplus(v):
    return jnp.maximum(v, 0.0) + jnp.log1p(jnp.exp(-jnp.abs(v)))


def sum_layout(tiles):
    groups = -(-tiles // STATE)
    return groups, 2 * groups * LANE


def read_sum(ext_ref, tile, inner):
    groups, _ = sum_layout(inner // LANE)
    group, row = divmod(tile, STATE)
    high = inner + group * LANE
    low = high + groups * LANE
    return ext_ref[row : row + 1, high : high + LANE].astype(F32) + ext_ref[
        row : row + 1, low : low + LANE
    ].astype(F32)


def write_sums(ext_ref, sums, inner):
    groups, _ = sum_layout(inner // LANE)
    for group in range(groups):
        part = sums[group * STATE : (group + 1) * STATE, :]
        high = part.astype(BF16)
        low = (part - high.astype(F32)).astype(BF16)
        at = inner + group * LANE
        ext_ref[:, at : at + LANE] = high
        ext_ref[:, at + groups * LANE : at + (groups + 1) * LANE] = low


NT = (((1,), (1,)), ((), ()))
SIDE = 5 * LANE


def start_all(pairs, sems):
    copies = [pltpu.make_async_copy(src, dst, sems.at[k]) for k, (src, dst) in enumerate(pairs)]
    for copy in copies:
        copy.start()
    return copies


def lane_blocks(size, width):
    return [slice(at, min(at + width, size)) for at in range(0, size, width)]


def offer_kernel(state_hbm, edge_hbm, x_hbm, out_ref, state_s, edge_s, tail_s, sems):
    rows = tail_s.shape[0]
    last = x_hbm.at[pl.ds(x_hbm.shape[0] - rows, rows)]
    for copy in start_all([(state_hbm, state_s), (edge_hbm, edge_s), (last, tail_s)], sems):
        copy.wait()
    lags = edge_s.shape[0]
    tail = tail_s[...].astype(F32)[rows - lags :]
    spare = jnp.zeros((OFFER - STATE - 2 * lags, tail.shape[1]), F32)
    whole = jnp.concatenate([state_s[...], edge_s[...].astype(F32), tail, spare], axis=0)
    out_ref[...] = whole.astype(BF16)


def edges_kernel(*refs):
    for k, ref in enumerate(refs[:-1]):
        refs[-1][k] = ref[...].astype(F32)[STATE:].astype(BF16)


def terms_kernel(lags, seed_count, *refs):
    scalar_hbm = refs[:4]
    x_hbm, taps_hbm, x_proj_hbm, dt_proj_hbm, out_proj_hbm = refs[4:9]
    vec_hbm = refs[9:12]
    edge_mine_ref, edge_other_ref = refs[12:14]
    seed_refs = refs[14 : 14 + seed_count]
    refs = refs[14 + seed_count :]
    (
        mixed_ref, step_ref, push_ref, decay_ref, proj_ref, slot_edge_ref, weight_ref, bundle_ref
    ) = refs[:8]
    scalars = refs[8:12]
    ext_ref = bundle_ref.at[0]
    (x_s, taps_ref, x_proj_ref, dt_proj_ref, bias_s, dt_bias_s, rate_s, rows_s, conv_s, edge_s, b_s,
     sums_s, sems) = refs[12:]
    lens_ref, cont_ref, source_ref, owner_ref = scalars
    row_count, inner = x_s.shape
    request_count = lens_ref.shape[1]
    chips = edge_mine_ref.shape[0]
    blocks = lane_blocks(inner, SIDE)
    side = SIDE // LANE
    pairs = list(zip(scalar_hbm, scalars))
    pairs += [(taps_hbm, taps_ref)]
    pairs += list(zip(vec_hbm, (bias_s, dt_bias_s, rate_s)))
    pairs += [(x_hbm.at[:, cols], x_s.at[:, cols]) for cols in blocks]
    pairs += [(x_proj_hbm, x_proj_ref), (dt_proj_hbm, dt_proj_ref), (out_proj_hbm, weight_ref)]
    copies = start_all(pairs, sems)
    for copy in copies[:8]:
        copy.wait()
    me = lax.axis_index("seq")
    core = lax.rem(me, 2)
    marks = request_marks(lens_ref, me * row_count)
    row = lax.broadcasted_iota(jnp.int32, (row_count, 1), 0)
    near = []
    for lag in range(1, lags + 1):
        hit = jnp.zeros((row_count, 1), jnp.int32)
        for begin, _ in marks:
            hit = hit + jnp.logical_and(row >= begin, row < begin + lag).astype(jnp.int32)
        near.append((hit == 0).astype(F32))
    rows_s[0:8, :] = jnp.zeros((8, inner), F32)
    before = edge_other_ref[1 - core].astype(F32)
    rows_s[8 - lags : 8, :] = before[lags : 2 * lags, :]
    for k, ref in enumerate(seed_refs):
        bundle_ref[1 + k, :, 0:inner] = ref[...].astype(F32)[:STATE].astype(BF16)
    for k, cols in enumerate(blocks):
        copies[8 + k].wait()
        here = x_s[:, cols].astype(F32)
        rows_s[8 : 8 + row_count, cols] = here
        total = wide_row(bias_s, k * side, side) + taps_ref[lags : lags + 1, cols] * here
        for lag in range(1, lags + 1):
            back = rows_s[8 - lag : 8 - lag + row_count, cols]
            total = total + taps_ref[lags - lag : lags - lag + 1, cols] * (near[lag - 1] * back)
        conv_s[:, cols] = total
    slot_edge_ref[...] = jnp.zeros(slot_edge_ref.shape, F32)
    for r in range(request_count):
        begin, end = marks[r]
        length = lens_ref[0, r]

        @pl.when(jnp.logical_and(begin > -lags, begin < row_count))
        def _(r=r, begin=begin, end=end, length=length):
            keep = cont_ref[0, r].astype(F32)
            source = source_ref[0, r]
            away = lax.rem(me // 2 - source // 2 + chips, chips)
            for ref, parity in ((edge_mine_ref, core), (edge_other_ref, 1 - core)):
                @pl.when(lax.rem(source, 2) == parity)
                def _(ref=ref):
                    edge_s[0:lags, :] = keep * ref[away].astype(F32)[0:lags, :]

            for p in range(lags):
                at = begin + p

                @pl.when(jnp.logical_and(jnp.logical_and(at >= 0, at < row_count), p < length))
                def _():
                    extra = jnp.zeros((1, inner), F32)
                    for lag in range(p + 1, lags + 1):
                        extra = extra + taps_ref[lags - lag : lags - lag + 1, :] * edge_s[
                            lags + p - lag : lags + p - lag + 1, :
                        ]
                    conv_s[pl.ds(at, 1), :] = conv_s[pl.ds(at, 1), :] + extra

        @pl.when(jnp.logical_and(end > 0, end <= row_count))
        def _(r=r, end=end, length=length):
            owner = owner_ref[0, r]
            for lag in range(lags):
                @pl.when(length > lag)
                def _():
                    slot_edge_ref[owner, lags - 1 - lag : lags - lag, :] = rows_s[
                        pl.ds(end + 7 - lag, 1), :
                    ]

                @pl.when(length <= lag)
                def _():
                    slot_edge_ref[owner, lags - 1 - lag : lags - lag, :] = edge_s[
                        pl.ds(lags + length - 1 - lag, 1), :
                    ]

    for cols in blocks:
        v = conv_s[:, cols]
        mixed_ref[:, cols] = (v / (1.0 + jnp.exp(-v))).astype(BF16)
    copies[-3].wait()
    projected = lax.dot_general(
        mixed_ref[...], x_proj_ref[...], NT, preferred_element_type=F32
    )
    proj_ref[...] = projected
    rank = dt_proj_ref.shape[0]
    dt_low = projected[:, :rank].astype(BF16)
    last_begin = jnp.int32(0)
    for begin, _ in marks:
        last_begin = jnp.where(
            jnp.logical_and(begin >= 0, begin < row_count), jnp.maximum(last_begin, begin), last_begin
        )
    in_last = (row >= last_begin).astype(F32)
    for s in range(STATE):
        b_s[s] = jnp.broadcast_to(
            projected[:, rank + s : rank + s + 1] * in_last, (row_count, LANE)
        )
    m_row, m_col, same = segment_masks(row_count, marks)
    later = tripled(jnp.logical_and(m_col > m_row, same))
    copies[-2].wait()
    for k, cols in enumerate(blocks):
        step_ref[:, cols] = softplus(
            jnp.dot(dt_low, dt_proj_ref[:, cols], preferred_element_type=F32)
            + wide_row(dt_bias_s, k * side, side)
        )
    for k, cols in enumerate(blocks):
        step = step_ref[:, cols]
        suffix = jnp.dot(later, three_parts(step), preferred_element_type=F32)
        decay_ref[:, cols] = jnp.exp(-wide_row(rate_s, k * side, side) * suffix)
        push_ref[:, cols] = step * mixed_ref[:, cols].astype(F32)

    def tile_step(i, carry):
        at = pl.multiple_of(i * LANE, LANE)
        cols = pl.ds(at, LANE)
        ext_ref[:, cols] = weighted_sum(push_ref[:, cols], decay_ref[:, cols], b_s).astype(BF16)
        sums_s[pl.ds(i, 1), :] = jnp.sum(step_ref[:, cols] * in_last, axis=0, keepdims=True)
        return carry

    sums_s[...] = jnp.zeros(sums_s.shape, F32)
    lax.fori_loop(0, inner // LANE, tile_step, 0)
    write_sums(ext_ref, sums_s[...], inner)
    copies[-1].wait()


def weighted_sum(push, decay, b_ref):
    weight = push * decay
    totals = []
    for s in range(STATE):
        product = weight * b_ref[s]
        total = product[0:8, :]
        for k in range(8, push.shape[0], 8):
            total = total + product[k : k + 8, :]
        totals.append(total)
        if s + 1 < STATE:
            weight = weight * decay
    return jnp.concatenate(
        [sums_of_eight(totals[k : k + 8]) for k in range(0, STATE, 8)], axis=0
    )


def pair_kernel(tokens, *refs):
    lens_hbm, rate_hbm, mine_ref, other_ref = refs[:4]
    mine_ref, other_ref = mine_ref.at[0], other_ref.at[0]
    out_ref, lens_ref, rate_s, sems = refs[4:]
    for copy in start_all([(lens_hbm, lens_ref), (rate_hbm, rate_s)], sems):
        copy.wait()
    inner = LANE * rate_s.shape[0]
    me = lax.axis_index("seq")
    core = lax.rem(me, 2)
    second = me - core + 1
    marks = request_marks(lens_ref, second * tokens)
    whole = jnp.float32(1.0)
    for begin, _ in marks:
        whole = jnp.where(jnp.logical_and(begin >= 0, begin < tokens), 0.0, whole)
    sums = []
    for i in range(inner // LANE):
        cols = slice(i * LANE, (i + 1) * LANE)
        mine, other = mine_ref[:, cols].astype(F32), other_ref[:, cols].astype(F32)
        e0 = jnp.where(core == 0, mine, other)
        e1 = jnp.where(core == 0, other, mine)
        my_sum, other_sum = read_sum(mine_ref, i, inner), read_sum(other_ref, i, inner)
        s0 = jnp.where(core == 0, my_sum, other_sum)
        s1 = jnp.where(core == 0, other_sum, my_sum)
        rate = rate_block(rate_s[i : i + 1, :])
        out_ref[:, cols] = (e1 + whole * jnp.exp(-rate * s1) * e0).astype(BF16)
        sums.append(s1 + whole * s0)
    groups, _ = sum_layout(inner // LANE)
    sums.append(jnp.zeros((groups * STATE - len(sums), LANE), F32))
    write_sums(out_ref, jnp.concatenate(sums, axis=0), inner)


def scan_kernel(
    lens_hbm, gate_hbm, up_hbm, down_hbm, rate_hbm, skip_hbm, mixed_ref, step_ref, push_ref, proj_ref,
    y_ref, q_ref, gate_ref, up_ref, down_ref, lens_ref, rate_s, skip_s, jump_s, b_s, c_s, sems,
):
    row_count, inner = mixed_ref.shape
    copies = start_all(
        [
            (lens_hbm, lens_ref), (rate_hbm, rate_s), (skip_hbm, skip_s),
            (gate_hbm, gate_ref), (up_hbm, up_ref), (down_hbm, down_ref),
        ],
        sems,
    )
    rank = proj_ref.shape[1] - 2 * STATE
    coefs = proj_ref[:, rank : rank + 2 * STATE]
    coefs = jnp.concatenate([coefs, jnp.zeros((row_count, LANE - 2 * STATE), F32)], axis=1)
    flipped = jnp.transpose(coefs)
    for t in range(row_count):
        b_s[t] = jnp.broadcast_to(flipped[0:STATE, t : t + 1], (STATE, LANE))
        c_s[t] = jnp.broadcast_to(flipped[STATE : 2 * STATE, t : t + 1], (STATE, LANE))
    for copy in copies[:3]:
        copy.wait()
    me = lax.axis_index("seq")
    marks = request_marks(lens_ref, me * row_count)
    m_row, m_col, same = segment_masks(row_count, marks)
    earlier = tripled(jnp.logical_and(m_col <= m_row, same))
    row = lax.broadcasted_iota(jnp.int32, (row_count, 1), 0)
    jump = jnp.zeros((row_count, 1), F32)
    for begin, _ in marks:
        jump = jump + (row == begin).astype(F32) * FAR
    tiles = 5
    width = tiles * LANE
    for k, cols in enumerate(lane_blocks(inner, width)):
        step = step_ref[:, cols]
        prefix = jnp.dot(earlier, three_parts(step), preferred_element_type=F32)
        q_ref[:, cols] = jnp.exp(-wide_row(rate_s, k * tiles, tiles) * prefix)
        jump_s[:, cols] = step + jump
        y_ref[:, cols] = wide_row(skip_s, k * tiles, tiles) * mixed_ref[:, cols].astype(F32)

    def chunk_step(i, carry):
        at = pl.multiple_of(i * width, LANE)
        rates = [-LOG2E * rate_block(row_of(rate_s, i * tiles + k)) for k in range(tiles)]

        def row_step(j, held):
            first = pl.multiple_of(j * 8, 8)
            rows = pl.ds(first, 8)
            held = list(held)
            for k in range(tiles):
                lanes = pl.ds(pl.multiple_of(at + k * LANE, LANE), LANE)
                jumps, pushes = jump_s.at[rows, lanes], push_ref.at[rows, lanes]
                h = held[k]
                outs = []
                for t in range(8):
                    decay = jnp.exp2(rates[k] * jumps[t : t + 1, :])
                    h = decay * h + b_s[first + t] * pushes[t : t + 1, :]
                    product = c_s[first + t] * h
                    outs.append(product[0:8] + product[8:16])
                held[k] = h
                y_ref[rows, lanes] = y_ref[rows, lanes] + sums_of_eight(outs)
            return tuple(held)

        lax.fori_loop(
            0, row_count // 8, row_step, tuple(jnp.zeros((STATE, LANE), F32) for _ in range(tiles))
        )
        return carry

    lax.fori_loop(0, inner // width, chunk_step, 0)
    for copy in copies[3:]:
        copy.wait()


def close_kernel(stage_count, *refs):
    scalar_hbm = refs[:3]
    rate_hbm, hidden_hbm = refs[3:5]
    stage_refs = refs[5 : 5 + stage_count]
    (mine_ref, other_ref, proj_ref, y_ref, q_ref, gain_ref, weight_ref) = refs[
        5 + stage_count : 12 + stage_count
    ]
    middle_ref, normed_ref, begins_ref = refs[12 + stage_count : 15 + stage_count]
    scalars = refs[15 + stage_count : 18 + stage_count]
    rate_s, hidden_s, c_s, ssm_s, sems = refs[18 + stage_count :]
    pair_ref = other_ref.at[0]
    lens_ref, cont_ref, source_ref = scalars
    row_count, inner = y_ref.shape
    width = middle_ref.shape[1]
    chips = mine_ref.shape[0] - 1
    copies = start_all(
        list(zip(scalar_hbm, scalars)) + [(rate_hbm, rate_s), (hidden_hbm, hidden_s)], sems
    )
    me = lax.axis_index("seq")
    core = lax.rem(me, 2)
    rank = proj_ref.shape[1] - 2 * STATE
    for s in range(STATE):
        c_s[s] = jnp.broadcast_to(
            proj_ref[:, rank + STATE + s : rank + STATE + s + 1], (row_count, LANE)
        )
    ssm_s[...] = y_ref[...]
    for copy in copies:
        copy.wait()
    marks = request_marks(lens_ref, me * row_count)
    tiles = 5
    side = tiles * LANE
    block = 16
    for r in range(lens_ref.shape[1]):
        begin, end = marks[r]
        low, high = jnp.maximum(begin, 0), jnp.minimum(end, row_count)

        @pl.when(high > low)
        def _(r=r, begin=begin, low=low, high=high):
            keep = cont_ref[0, r].astype(F32)
            source = source_ref[0, r]
            away = lax.rem(me // 2 - source // 2 + chips, chips)
            for ref, parity in ((mine_ref, core), (other_ref, 1 - core)):
                @pl.when(lax.rem(source, 2) == parity)
                def _(ref=ref):
                    begins_ref[r] = keep * ref[1 + away, :, 0:inner].astype(F32)

            for k in range(stage_count + 1):
                if k < stage_count:
                    chip_first = me - core - 2 * (stage_count - k)
                    ref = stage_refs[stage_count - 1 - k]
                    stage_end = -(core + 2 * (stage_count - 1 - k)) * row_count
                    valid = jnp.logical_and(chip_first >= 0, begin < stage_end)
                else:
                    ref = pair_ref
                    valid = jnp.logical_and(core == 1, begin < 0)

                @pl.when(valid)
                def _(ref=ref):
                    for i in range(inner // LANE):
                        cols = slice(i * LANE, (i + 1) * LANE)
                        decay = jnp.exp(-rate_block(rate_s[i : i + 1, :]) * read_sum(ref, i, inner))
                        begins_ref[r, :, cols] = (
                            ref[:, cols].astype(F32) + decay * begins_ref[r, :, cols]
                        )

            def block_step(j, carry):
                first = pl.multiple_of(j * block, block)
                rows = pl.ds(first, block)
                at_row = lax.broadcasted_iota(jnp.int32, (block, 1), 0) + first
                inside = jnp.logical_and(at_row >= low, at_row < high)

                def lane_step(i, inner_carry):
                    at = pl.multiple_of(i * side, LANE)
                    cols = pl.ds(at, side)
                    q = q_ref[rows, cols]
                    total = jnp.zeros((block, side), F32)
                    for s in range(STATE - 1, -1, -1):
                        c = c_s[s, rows, :]
                        c = jnp.concatenate([c] * tiles, axis=1)
                        total = (total + c * begins_ref[r, s : s + 1, cols]) * q
                    ssm_s[rows, cols] = ssm_s[rows, cols] + jnp.where(inside, total, 0.0)
                    return inner_carry

                lax.fori_loop(0, inner // side, lane_step, 0, unroll=True)
                return carry

            lax.fori_loop(low // block, (high + block - 1) // block, block_step, 0)

    total = lax.dot_general(
        ssm_s[...].astype(BF16), weight_ref[...], NT, preferred_element_type=F32
    )
    residual = [
        jnp.transpose(hidden_s[cols, :].astype(F32)) for cols in lane_blocks(width, LANE)
    ]
    total = total + jnp.concatenate(residual, axis=1)
    middle_ref[...] = total
    scale = lax.rsqrt(jnp.mean(total * total, axis=1, keepdims=True) + NORM_EPS)
    normed_ref[...] = (total * scale * gain_ref[...]).astype(BF16)


def final_kernel(
    lens_hbm, owner_hbm, rate_hbm, step_ref, push_ref, decay_ref, proj_ref, begins_ref,
    slot_edge_ref, keep_ref, send_ref, lens_ref, owner_ref, rate_s, b_s, held_s, edge_s, sems,
):
    pairs = [(lens_hbm, lens_ref), (owner_hbm, owner_ref), (rate_hbm, rate_s)]
    for copy in start_all(pairs, sems):
        copy.wait()
    row_count, inner = step_ref.shape
    block = 32
    me = lax.axis_index("seq")
    core = lax.rem(me, 2)
    chips = keep_ref.shape[0]
    marks = request_marks(lens_ref, me * row_count)
    rank = proj_ref.shape[1] - 2 * STATE
    lags = slot_edge_ref.shape[1]
    row = lax.broadcasted_iota(jnp.int32, (row_count, 1), 0)
    keep_ref[...] = jnp.zeros(keep_ref.shape, BF16)
    send_ref[...] = jnp.zeros(send_ref.shape, BF16)
    tiles = inner // LANE
    edge_groups = (keep_ref.shape[2] - inner) // LANE
    for r in range(lens_ref.shape[1]):
        begin, end = marks[r]

        @pl.when(jnp.logical_and(end > 0, end <= row_count))
        def _(r=r, begin=begin, end=end):
            owner = owner_ref[0, r]
            there = lax.rem(owner // 2 - me // 2 + chips, chips)
            mine = lax.rem(owner, 2) == core
            inside = jnp.logical_and(row >= begin, row < end).astype(F32)
            for s in range(STATE):
                b_s[s] = jnp.broadcast_to(
                    proj_ref[:, rank + s : rank + s + 1] * inside, (row_count, LANE)
                )

            def put(cols, block):
                @pl.when(mine)
                def _():
                    keep_ref[there, :, cols] = block

                @pl.when(jnp.logical_not(mine))
                def _():
                    send_ref[there, :, cols] = block

            held_s[...] = jnp.zeros(held_s.shape, F32)

            def block_step(j, carry):
                rows = pl.ds(pl.multiple_of(j * block, block), block)

                def add_tile(i, inner_carry):
                    cols = pl.ds(pl.multiple_of(i * LANE, LANE), LANE)
                    held_s[:, cols] = held_s[:, cols] + weighted_sum(
                        push_ref[rows, cols], decay_ref[rows, cols], b_s.at[:, rows, :]
                    )
                    return inner_carry

                lax.fori_loop(0, tiles, add_tile, 0, unroll=5)
                return carry

            lax.fori_loop(
                jnp.maximum(begin, 0) // block, (end + block - 1) // block, block_step, 0
            )

            def tile_step(i, carry):
                cols = pl.ds(pl.multiple_of(i * LANE, LANE), LANE)
                span = jnp.sum(step_ref[:, cols] * inside, axis=0, keepdims=True)
                carried = jnp.exp(-rate_block(row_of(rate_s, i)) * span) * begins_ref[r, :, cols]
                put(cols, (held_s[:, cols] + carried).astype(BF16))
                return carry

            lax.fori_loop(0, tiles, tile_step, 0)
            edge_s[...] = jnp.zeros(edge_s.shape, F32)
            for lag in range(lags):
                for i in range(tiles):
                    at = lag * tiles + i
                    edge_s[at : at + 1, :] = slot_edge_ref[
                        owner, lag : lag + 1, i * LANE : (i + 1) * LANE
                    ]
            for g in range(edge_groups):
                put(
                    slice(inner + g * LANE, inner + (g + 1) * LANE),
                    edge_s[g * STATE : (g + 1) * STATE, :].astype(BF16),
                )


def unpack_kernel(lags, *refs):
    got_refs, (state_ref, edge_ref, edge_s) = refs[:-3], refs[-3:]
    inner = state_ref.shape[1]
    tiles = inner // LANE

    def whole(cols):
        total = got_refs[0][:, cols].astype(F32)
        for ref in got_refs[1:]:
            total = total + ref[:, cols].astype(F32)
        return total

    state_ref[...] = whole(slice(0, inner))
    groups = (got_refs[0].shape[1] - inner) // LANE
    for g in range(groups):
        edge_s[g * STATE : (g + 1) * STATE, :] = whole(
            slice(inner + g * LANE, inner + (g + 1) * LANE)
        )
    for i in range(tiles):
        edge_ref[:, i * LANE : (i + 1) * LANE] = jnp.concatenate(
            [edge_s[lag * tiles + i : lag * tiles + i + 1, :] for lag in range(lags)], axis=0
        ).astype(BF16)


def feed_forward(tokens, gate_ref, up_ref, down_ref):
    gate = jnp.dot(tokens, gate_ref[...], preferred_element_type=F32)
    up = jnp.dot(tokens, up_ref[...], preferred_element_type=F32)
    hidden = (gate / (1.0 + jnp.exp(-gate)) * up).astype(BF16)
    return lax.dot_general(hidden, down_ref[...], NT, preferred_element_type=F32)


def own_kernel(token_ref, middle_ref, gate_ref, up_ref, down_ref, out_ref):
    out_ref[...] = middle_ref[...] + feed_forward(token_ref[...], gate_ref, up_ref, down_ref)


def peer_kernel(*refs):
    count = (len(refs) - 3) // 2
    tokens = jnp.concatenate([ref[...] for ref in refs[:count]], axis=0)
    out = feed_forward(tokens, *refs[count : count + 3]).astype(BF16)
    part = out.shape[0] // count
    for k, ref in enumerate(refs[count + 3 :]):
        ref[...] = out[k * part : (k + 1) * part]


def far_kernel(low_ref, high_ref, gate_ref, up_ref, down_ref, out_ref):
    tokens = jnp.concatenate([low_ref[...], high_ref[...]], axis=0)
    out_ref[...] = feed_forward(tokens, gate_ref, up_ref, down_ref).astype(BF16)


def join_kernel(own_ref, *refs):
    whole = own_ref[...]
    for ref in refs[:-1]:
        whole = whole + ref[...].astype(F32)
    for cols in lane_blocks(whole.shape[1], LANE):
        refs[-1][cols, :] = jnp.transpose(whole[:, cols]).astype(BF16)


def call(kernel, outs, scratch, operands, hbm=0, limit=16, micros=1.0, last=False):
    spaces = [pltpu.HBM if k < hbm else pltpu.VMEM for k in range(len(operands))]
    operands = [pltpu.with_memory_space_constraint(a, space) for a, space in zip(operands, spaces)]
    out_kind = jax.ShapeDtypeStruct if last else pltpu.VMEM
    return pl.pallas_call(
        kernel,
        out_shape=tuple(out_kind(shape, dtype) for shape, dtype in outs),
        in_specs=[pl.BlockSpec(memory_space=space) for space in spaces],
        out_specs=tuple(pl.BlockSpec(memory_space=pltpu.VMEM) for _ in outs),
        scratch_shapes=scratch,
        compiler_params=pltpu.CompilerParams(vmem_limit_bytes=limit * 1024 * 1024),
        cost_estimate=pl.CostEstimate(
            flops=int(micros * 1.15e9), bytes_accessed=int(micros * 3.6e6), transcendentals=0
        ),
    )(*operands)


def shifted(block, axis, distance):
    size = lax.axis_size(axis)
    return lax.ppermute(block, axis, [(i, (i + distance) % size) for i in range(size)])


def passed_up(block, axis, distance):
    size = lax.axis_size(axis)
    return lax.ppermute(block, axis, [(i, i + distance) for i in range(size - distance)])


def swapped(block, axis, mask):
    return lax.ppermute(block, axis, [(i, i ^ mask) for i in range(lax.axis_size(axis))])


def shards(
    hidden_in,
    mamba_in,
    conv_weight,
    conv_bias,
    x_proj,
    dt_proj,
    dt_bias,
    decay_rate,
    skip_gain,
    out_proj,
    norm_gain,
    mlp_gate,
    mlp_up,
    mlp_down,
    cache_state,
    cache_edge,
    req_lengths,
    cont_flag,
    cache_source,
    owner_slot,
):
    x = mamba_in[0]
    row_count, inner = x.shape
    width = hidden_in.shape[2]
    lags = cache_edge.shape[2]
    peers = lax.axis_size("seq")
    tiles = inner // LANE
    scalars = (req_lengths, cont_flag, cache_source, owner_slot)
    request_count = req_lengths.shape[1]
    chips = peers // 2
    dma = pltpu.SemaphoreType.DMA
    (offer,) = call(
        offer_kernel,
        [((OFFER, inner), BF16)],
        [
            pltpu.VMEM((STATE, inner), F32),
            pltpu.VMEM((lags, inner), BF16),
            pltpu.VMEM((STATE, inner), BF16),
            dma((3,)),
        ],
        (cache_state[0, 0], cache_edge[0, 0], x),
        hbm=3,
        limit=4,
    )
    offers = [offer] + [shifted(offer, "seq", 2 * k) for k in range(1, chips)]
    (edge_mine,) = call(
        edges_kernel, [((chips, OFFER - STATE, inner), BF16)], [], tuple(offers), limit=4
    )
    edge_other = swapped(edge_mine, "seq", 1)
    bias, dt_bias, rate, skip = [
        v.reshape(tiles, LANE) for v in (conv_bias, dt_bias, decay_rate, skip_gain)
    ]
    groups, extra = sum_layout(tiles)
    ext_shape = (STATE, inner + extra)
    scalar_s = pltpu.SMEM((1, request_count), jnp.int32)
    vec_s = pltpu.VMEM((tiles, LANE), F32)
    rank = x_proj.shape[1]
    full = ((row_count, inner), F32)
    bundle_shape = ((chips + 1, *ext_shape), BF16)
    mixed, step, push, decay, proj, slot_edge, weight, bundle = call(
        functools.partial(terms_kernel, lags, chips),
        [
            ((row_count, inner), BF16),
            full,
            full,
            full,
            ((row_count, rank), F32),
            ((peers, lags, inner), F32),
            ((width, inner), BF16),
            bundle_shape,
        ],
        [
            scalar_s, scalar_s, scalar_s, scalar_s,
            pltpu.VMEM((row_count, inner), BF16),
            pltpu.VMEM(conv_weight.shape, F32),
            pltpu.VMEM((rank, inner), BF16),
            pltpu.VMEM(dt_proj.shape, BF16),
            vec_s, vec_s, vec_s,
            pltpu.VMEM((8 + row_count, inner), F32),
            pltpu.VMEM((row_count, inner), F32),
            pltpu.VMEM((8, inner), F32),
            pltpu.VMEM((STATE, row_count, LANE), F32),
            pltpu.VMEM((groups * STATE, LANE), F32),
            dma((11 + len(lane_blocks(inner, SIDE)),)),
        ],
        (
            *scalars, x, conv_weight, x_proj.T, dt_proj, out_proj.T, bias, dt_bias, rate,
            edge_mine, edge_other, *offers,
        ),
        hbm=12,
        micros=10,
    )
    other = swapped(bundle, "seq", 1)
    (chip,) = call(
        functools.partial(pair_kernel, row_count),
        [(ext_shape, BF16)],
        [scalar_s, vec_s, dma((2,))],
        (req_lengths, rate, bundle, other),
        hbm=2,
        limit=4,
    )
    stages = [passed_up(chip, "seq", 2 * k) for k in range(1, chips)]
    y, q, gate, up, down = call(
        scan_kernel,
        [full, full, (mlp_gate.shape, BF16), (mlp_up.shape, BF16), (mlp_down.shape[::-1], BF16)],
        [
            scalar_s, vec_s, vec_s,
            pltpu.VMEM((row_count, inner), F32),
            pltpu.VMEM((row_count, STATE, LANE), F32),
            pltpu.VMEM((row_count, STATE, LANE), F32),
            dma((6,)),
        ],
        (req_lengths, mlp_gate, mlp_up, mlp_down.T, rate, skip, mixed, step, push, proj),
        hbm=6,
        limit=8,
        micros=8,
    )
    middle, normed, begins = call(
        functools.partial(close_kernel, len(stages)),
        [
            ((row_count, width), F32),
            ((row_count, width), BF16),
            ((request_count, STATE, inner), F32),
        ],
        [
            scalar_s, scalar_s, scalar_s,
            vec_s,
            pltpu.VMEM((width, row_count), BF16),
            pltpu.VMEM((STATE, row_count, LANE), F32),
            pltpu.VMEM((row_count, inner), F32),
            dma((5,)),
        ],
        (
            *scalars[:3], rate, hidden_in[0].T, *stages, bundle, other, proj, y, q,
            norm_gain.reshape(1, width), weight,
        ),
        hbm=5,
        limit=12,
        micros=6,
    )
    weights = (gate, up, down)
    tokens_out = ((row_count, width), BF16)
    from_x, from_y = swapped(normed, "req", 1), swapped(normed, "req", 2)
    (own,) = call(
        own_kernel, [((row_count, width), F32)], [], (normed, middle, *weights), limit=4, micros=3
    )
    edge_groups = -(-lags * tiles // STATE)
    packed = ((chips, STATE, inner + edge_groups * LANE), BF16)
    keep, send = call(
        final_kernel,
        [packed, packed],
        [
            scalar_s, scalar_s, vec_s,
            pltpu.VMEM((STATE, row_count, LANE), F32),
            pltpu.VMEM((STATE, inner), F32),
            pltpu.VMEM((edge_groups * STATE, LANE), F32),
            dma((3,)),
        ],
        (req_lengths, owner_slot, rate, step, push, decay, proj, begins, slot_edge),
        hbm=3,
        limit=4,
        micros=4,
    )
    from_x, from_y, send = lax.optimization_barrier((from_x, from_y, send))
    got = swapped(send, "seq", 1)
    half = row_count // 2
    far_high = swapped(from_x[half:], "req", 2)
    far_low = swapped(from_y[:half], "req", 1)
    at_x, at_y = call(
        peer_kernel, [tokens_out] * 2, [], (from_x, from_y, *weights), limit=6, micros=4.5
    )
    got = lax.optimization_barrier((got, at_x))[0]
    parts = [keep[k] + got[k] for k in range(chips)]
    far_low, far_high, parts = lax.optimization_barrier((far_low, far_high, parts))
    back_x, back_y = swapped(at_x, "req", 1), swapped(at_y, "req", 2)
    (at_far,) = call(far_kernel, [tokens_out], [], (far_low, far_high, *weights), limit=4, micros=3)
    back_far = swapped(at_far, "req", 3)
    parts = [parts[0]] + [shifted(parts[k], "seq", 2 * k) for k in range(1, chips)]
    new_state, new_edge = call(
        functools.partial(unpack_kernel, lags),
        [((STATE, inner), F32), ((lags, inner), BF16)],
        [pltpu.VMEM((edge_groups * STATE, LANE), F32)],
        tuple(parts),
        limit=4,
        last=True,
    )
    (block_rows,) = call(
        join_kernel, [((width, row_count), BF16)], [], (own, back_x, back_y, back_far), limit=4,
        last=True,
    )
    return (block_rows.T[None], new_state[None, None], new_edge[None, None])


def solution(mesh):
    return jax.shard_map(
        shards,
        mesh=mesh,
        in_specs=(
            P("req", "seq", None),
            P("req", "seq", None),
            P(),
            P(),
            P(),
            P(),
            P(),
            P(),
            P(),
            P(),
            P(),
            P(None, "req"),
            P(None, "req"),
            P("req", None),
            P("req", "seq", None, None),
            P("req", "seq", None, None),
            P("req", None),
            P("req", None),
            P("req", None),
            P("req", None),
        ),
        out_specs=(P("req", "seq", None), P("req", "seq", None, None), P("req", "seq", None, None)),
        check_vma=False,
    )
```

profile of v0, /device:TPU:0, one launch (start us, length us, event | category | flops | bytes accessed | tf_op | source)
XLA Modules:
  0.0 104.1 jit_solution(16594853279247827057)
XLA Ops:
  0.6 1.1 %shard_map.211.refs_0_.refs_14_ = bf16[24,3200]{1,0:T(8,128)(2,1)S(1)} custom-call(f32[16,3200]{1,0:T(8,128)} %bitcast.32, bf16[3,3200]{1,0:T(4,128)(2,1)} %bitcast.33, bf16[128,3200]{1,0:T(8,128)(2,1)} %bitcast.29), custom_call_target="tpu_custom_call" | custom-call | flops 1150000000 | bytes 3600000 | tf_op jit(solution)/shard_map/pallas_call | solution.py:648
  1.7 5.1 %collective-permute-start.2 = (bf16[24,3200]{1,0:T(8,128)(2,1)S(1)}, bf16[24,3200]{1,0:T(8,128)(2,1)S(1)}, u32[]{:S(2)}, u32[]{:S(2)}) collective-permute-start(bf16[24,3200]{1,0:T(8,128)(2,1)S(1)} %shard_map.211.refs_0_.refs_14_), channel_id=1, source_target_pairs={{0,6},{1,7},{2,0},{3,1},{4,2},{5,3},{6,4},{7,5},{8,14},{9,15},{10,... | collective-permute-start | bytes 460808 | tf_op jit(solution)/shard_map/ppermute | solution.py:663
  6.8 0.0 collective-permute-start.1
  6.8 1.0 collective-permute-start
  7.8 3.4 %collective-permute-done.2.refs_3_.refs_17_ = bf16[24,3200]{1,0:T(8,128)(2,1)S(1)} collective-permute-done((bf16[24,3200]{1,0:T(8,128)(2,1)S(1)}, bf16[24,3200]{1,0:T(8,128)(2,1)S(1)}, u32[]{:S(2)}, u32[]{:S(2)}) %collective-permute-start.2) | collective-permute-done | bytes 153632 | tf_op jit(solution)/shard_map/ppermute | solution.py:663
  11.2 8.6 %collective-permute-done.1.refs_2_.refs_16_ = bf16[24,3200]{1,0:T(8,128)(2,1)S(1)} collective-permute-done((bf16[24,3200]{1,0:T(8,128)(2,1)S(1)}, bf16[24,3200]{1,0:T(8,128)(2,1)S(1)}, u32[]{:S(2)}, u32[]{:S(2)}) %collective-permute-start.1) | collective-permute-done | bytes 153632 | tf_op jit(solution)/shard_map/ppermute | solution.py:663
  19.8 0.0 collective-permute-done.refs_1_.refs_15_
  19.8 0.1 collective-permute-start.3
  19.9 1.4 %collective-permute-done.3.refs_13_ = bf16[4,8,3200]{2,1,0:T(8,128)(2,1)S(1)} collective-permute-done((bf16[4,8,3200]{2,1,0:T(8,128)(2,1)S(1)}, bf16[4,8,3200]{2,1,0:T(8,128)(2,1)S(1)}, u32[]{:S(2)}, u32[]{:S(2)}) %collective-permute-start.3) | collective-permute-done | bytes 204832 | tf_op jit(solution)/shard_map/ppermute | solution.py:672
  21.4 0.0 copy-start
  21.4 9.7 %shard_map.213 = (bf16[128,3200]{1,0:T(8,128)(2,1)S(1)}, f32[128,3200]{1,0:T(8,128)S(1)}, f32[128,3200]{1,0:T(8,128)S(1)}, f32[128,3200]{1,0:T(8,128)S(1)}, f32[...) custom-call(s32[1,4]{1,0:T(1,128)} %lens_hbm.3, ...), custom_call_target="tpu_custom_call" | custom-call | flops 11500000256 | bytes 36000000 | tf_op jit(solution)/shard_map/pallas_call | solution.py:648
  31.1 0.4 collective-permute-start.4
  31.4 0.0 copy-done
  31.5 1.7 %collective-permute-done.4.refs_3_.refs_9_ = bf16[5,16,3712]{2,1,0:T(8,128)(2,1)S(1)} collective-permute-done((bf16[5,16,3712]{2,1,0:T(8,128)(2,1)S(1)}, bf16[5,16,3712]{2,1,0:T(8,128)(2,1)S(1)}, u32[]{:S(2)}, u32[]{:S(2)}) %collective-permute-start.4) | collective-permute-done | bytes 593952 | tf_op jit(solution)/shard_map/ppermute | solution.py:672
  33.2 0.9 shard_map.214
  34.0 3.1 %collective-permute-start.7 = (bf16[16,3712]{1,0:T(8,128)(2,1)S(1)}, bf16[16,3712]{1,0:T(8,128)(2,1)S(1)}, u32[]{:S(2)}, u32[]{:S(2)}) collective-permute-start(bf16[16,3712]{1,0:T(8,128)(2,1)S(1)} %shard_map.214), channel_id=1, source_target_pairs={{0,6},{1,7},{8,14},{9,15},{16,22},{17,23},{24,30},{25,31}} | collective-permute-start | bytes 356360 | tf_op jit(solution)/shard_map/ppermute | solution.py:668
  37.2 2.2 %collective-permute-start.6 = (bf16[16,3712]{1,0:T(8,128)(2,1)S(1)}, bf16[16,3712]{1,0:T(8,128)(2,1)S(1)}, u32[]{:S(2)}, u32[]{:S(2)}) collective-permute-start(bf16[16,3712]{1,0:T(8,128)(2,1)S(1)} %shard_map.214), channel_id=1, source_target_pairs={{0,4},{1,5},{2,6},{3,7},{8,12},{9,13},{10,14},{11,15},{16,20},{17,... | collective-permute-start | bytes 356360 | tf_op jit(solution)/shard_map/ppermute | solution.py:668
  39.4 1.6 %collective-permute-start.5 = (bf16[16,3712]{1,0:T(8,128)(2,1)S(1)}, bf16[16,3712]{1,0:T(8,128)(2,1)S(1)}, u32[]{:S(2)}, u32[]{:S(2)}) collective-permute-start(bf16[16,3712]{1,0:T(8,128)(2,1)S(1)} %shard_map.214), channel_id=1, source_target_pairs={{0,2},{1,3},{2,4},{3,5},{4,6},{5,7},{8,10},{9,11},{10,12},{11,13},... | collective-permute-start | bytes 356360 | tf_op jit(solution)/shard_map/ppermute | solution.py:668
  41.0 11.5 %shard_map.215 = (f32[128,3200]{1,0:T(8,128)S(1)}, f32[128,3200]{1,0:T(8,128)S(1)}, bf16[1600,1376]{1,0:T(8,128)(2,1)S(1)}, bf16[1600,1376]{1,0:T(8,128)(2,1)S(1)}, bf16[1600,1376]{1,0:T(8,128)(2,1)S(1)}) custom-call(s32[1,4]{1,0:T(1,128)} %lens_hbm.3, bf16[1600,1376]{1,0:T(8,128)(2,1)} %gate_hbm.1, bf16[1600,1376]{1,0:T(8,128)(2,1)} %up_hbm.1, ...), custom_call_target="tpu_custom_call" | custom-call | flops 9200000000 | bytes 28800000 | tf_op jit(solution)/shard_map/pallas_call | solution.py:648
  52.4 0.0 collective-permute-done.7.refs_7_
  52.4 0.0 collective-permute-done.6.refs_6_
  52.5 0.0 collective-permute-done.5.refs_5_
  52.5 8.7 %shard_map.216 = (f32[128,1600]{1,0:T(8,128)S(1)}, bf16[128,1600]{1,0:T(8,128)(2,1)S(1)}, f32[4,16,3200]{2,1,0:T(8,128)S(1)}) custom-call(s32[1,4]{1,0:T(1,128)} %lens_hbm.3, s32[1,4]{1,0:T(1,128)} %refs_1_.3, s32[1,4]{1,0:T(1,128)} %refs_2_.3, f32[25,128]{1,0:T(8,128)} %bitcast.40, bf16[1600,128]{1,0:T(8,128)(2,1)} %bitcast.31, ...), custom_call_target="tpu_custom_call" | custom-call | flops 6899999744 | bytes 21600000 | tf_op jit(solution)/shard_map/pallas_call | solution.py:648
  61.1 1.8 %collective-permute-start.9 = (bf16[128,1600]{1,0:T(8,128)(2,1)S(1)}, bf16[128,1600]{1,0:T(8,128)(2,1)S(1)}, u32[]{:S(2)}, u32[]{:S(2)}) collective-permute-start(bf16[128,1600]{1,0:T(8,128)(2,1)S(1)} %get-tuple-element.43.token_ref), channel_id=1, source_target_pairs={{0,16},{8,24},{16,0},{24,8},{1,17},{9,25},{17,1},{25,9},{2,18},{10... | collective-permute-start | bytes 1228808 | tf_op jit(solution)/shard_map/ppermute | solution.py:672
  62.9 1.5 %collective-permute-start.8 = (bf16[128,1600]{1,0:T(8,128)(2,1)S(1)}, bf16[128,1600]{1,0:T(8,128)(2,1)S(1)}, u32[]{:S(2)}, u32[]{:S(2)}) collective-permute-start(bf16[128,1600]{1,0:T(8,128)(2,1)S(1)} %get-tuple-element.43.token_ref), channel_id=1, source_target_pairs={{0,8},{8,0},{16,24},{24,16},{1,9},{9,1},{17,25},{25,17},{2,10},{10... | collective-permute-start | bytes 1228808 | tf_op jit(solution)/shard_map/ppermute | solution.py:672
  64.4 0.8 shard_map.218
  65.2 8.6 %collective-permute-done.9.refs_1_ = bf16[128,1600]{1,0:T(8,128)(2,1)S(1)} collective-permute-done((bf16[128,1600]{1,0:T(8,128)(2,1)S(1)}, bf16[128,1600]{1,0:T(8,128)(2,1)S(1)}, u32[]{:S(2)}, u32[]{:S(2)}) %collective-permute-start.9) | collective-permute-done | bytes 409632 | tf_op jit(solution)/shard_map/ppermute | solution.py:672
  73.8 0.2 collective-permute-done.8.refs_0_
  74.0 0.0 collective-permute-start.14
  74.0 1.6 %collective-permute-start.12 = (bf16[64,1600]{1,0:T(8,128)(2,1)S(1)}, bf16[64,1600]{1,0:T(8,128)(2,1)S(1)}, u32[]{:S(2)}, u32[]{:S(2)}) collective-permute-start(bf16[64,1600]{1,0:T(8,128)(2,1)S(1)} %slice.30), channel_id=1, source_target_pairs={{0,8},{8,0},{16,24},{24,16},{1,9},{9,1},{17,25},{25,17},{2,10},{10... | collective-permute-start | bytes 614408 | tf_op jit(solution)/shard_map/ppermute | solution.py:672
  75.6 0.9 collective-permute-start.13
  76.5 4.6 %shard_map.219 = (bf16[128,1600]{1,0:T(8,128)(2,1)S(1)}, bf16[128,1600]{1,0:T(8,128)(2,1)S(1)}) custom-call(bf16[128,1600]{1,0:T(8,128)(2,1)S(1)} %collective-permute-done.8.refs_0_, bf16[128,1600]{1,0:T(8,128)(2,1)S(1)} %collective-permute-done.9.refs_1_, bf16[1600,1376]{1,0:T(8,128)(2,1)S(1)} %get-tuple-element.45.gate_ref.refs_2_, ...), custom_call_target="tpu_custom_call" | custom-call | flops 5175000064 | bytes 16200000 | tf_op jit(solution)/shard_map/pallas_call | solution.py:648
  81.0 1.2 %collective-permute-start.11 = (bf16[128,1600]{1,0:T(8,128)(2,1)S(1)}, bf16[128,1600]{1,0:T(8,128)(2,1)S(1)}, u32[]{:S(2)}, u32[]{:S(2)}) collective-permute-start(bf16[128,1600]{1,0:T(8,128)(2,1)S(1)} %get-tuple-element.55), channel_id=1, source_target_pairs={{0,16},{8,24},{16,0},{24,8},{1,17},{9,25},{17,1},{25,9},{2,18},{10... | collective-permute-start | bytes 1228808 | tf_op jit(solution)/shard_map/ppermute | solution.py:672
  82.2 0.5 collective-permute-start.10
  82.8 0.0 collective-permute-done.14
  82.8 0.1 add_bitcast_fusion
  82.9 0.0 collective-permute-done.12.low_ref
  82.9 0.1 collective-permute-done.13.high_ref
  83.0 0.5 collective-permute-start.16
  83.4 0.0 collective-permute-start.17
  83.5 3.4 %collective-permute-start.18 = (bf16[16,3840]{1,0:T(8,128)(2,1)S(1)}, bf16[16,3840]{1,0:T(8,128)(2,1)S(1)}, u32[]{:S(2)}, u32[]{:S(2)}) collective-permute-start(bf16[16,3840]{1,0:T(8,128)(2,1)S(1)} %get-tuple-element.64), channel_id=1, source_target_pairs={{0,6},{1,7},{2,0},{3,1},{4,2},{5,3},{6,4},{7,5},{8,14},{9,15},{10,... | collective-permute-start | bytes 368648 | tf_op jit(solution)/shard_map/ppermute | solution.py:663
  86.8 2.9 %shard_map.220 = bf16[128,1600]{1,0:T(8,128)(2,1)S(1)} custom-call(bf16[64,1600]{1,0:T(8,128)(2,1)S(1)} %collective-permute-done.12.low_ref, bf16[64,1600]{1,0:T(8,128)(2,1)S(1)} %collective-permute-done.13.high_ref, bf16[1600,1376]{1,0:T(8,128)(2,1)S(1)} %get-tuple-element.45.gate_ref.refs_2_, bf16[1600,1376]{1,0:T(8,128)(2,1)S(1)} %get-tuple-element.46.up_ref.refs_3_, ...), custom_call_target="tpu_custom_call" | custom-call | flops 3449999872 | bytes 10800000 | tf_op jit(solution)/shard_map/pallas_call | solution.py:648
  89.7 1.4 %collective-permute-done.16.refs_1_ = bf16[16,3840]{1,0:T(8,128)(2,1)S(1)} collective-permute-done((bf16[16,3840]{1,0:T(8,128)(2,1)S(1)}, bf16[16,3840]{1,0:T(8,128)(2,1)S(1)}, u32[]{:S(2)}, u32[]{:S(2)}) %collective-permute-start.16) | collective-permute-done | bytes 122912 | tf_op jit(solution)/shard_map/ppermute | solution.py:663
  91.1 1.8 %collective-permute-start.15 = (bf16[128,1600]{1,0:T(8,128)(2,1)S(1)}, bf16[128,1600]{1,0:T(8,128)(2,1)S(1)}, u32[]{:S(2)}, u32[]{:S(2)}) collective-permute-start(bf16[128,1600]{1,0:T(8,128)(2,1)S(1)} %shard_map.220), channel_id=1, source_target_pairs={{0,24},{8,16},{16,8},{24,0},{1,25},{9,17},{17,9},{25,1},{2,26},{10... | collective-permute-start | bytes 1228808 | tf_op jit(solution)/shard_map/ppermute | solution.py:672
  92.9 2.9 %shard_map.217.own_ref = f32[128,1600]{1,0:T(8,128)S(1)} custom-call(bf16[128,1600]{1,0:T(8,128)(2,1)S(1)} %get-tuple-element.43.token_ref, f32[128,1600]{1,0:T(8,128)S(1)} %get-tuple-element.44.middle_ref, bf16[1600,1376]{1,0:T(8,128)(2,1)S(1)} %get-tuple-element.45.gate_ref.refs_2_, bf16[1600,1376]{1,0:T(8,128)(2,1)S(1)} %get-tuple-element.46.up_ref.refs_3_, ...), custom_call_target="tpu_custom_call" | custom-call | flops 3449999872 | bytes 10800000 | tf_op jit(solution)/shard_map/pallas_call | solution.py:648
  95.8 0.0 collective-permute-done.17.refs_2_
  95.8 0.0 collective-permute-done.18.refs_3_
  95.8 0.8 shard_map.222
  96.5 0.0 collective-permute-done.11.refs_1_
  96.6 0.0 collective-permute-done.10.refs_0_
  96.6 6.5 %collective-permute-done.15.refs_2_ = bf16[128,1600]{1,0:T(8,128)(2,1)S(1)} collective-permute-done((bf16[128,1600]{1,0:T(8,128)(2,1)S(1)}, bf16[128,1600]{1,0:T(8,128)(2,1)S(1)}, u32[]{:S(2)}, u32[]{:S(2)}) %collective-permute-start.15) | collective-permute-done | bytes 409632 | tf_op jit(solution)/shard_map/ppermute | solution.py:672
  103.1 1.0 %shard_map.221 = bf16[1600,128]{1,0:T(8,128)(2,1)} custom-call(f32[128,1600]{1,0:T(8,128)S(1)} %shard_map.217.own_ref, bf16[128,1600]{1,0:T(8,128)(2,1)S(1)} %collective-permute-done.10.refs_0_, bf16[128,1600]{1,0:T(8,128)(2,1)S(1)} %collective-permute-done.11.refs_1_, bf16[128,1600]{1,0:T(8,128)(2,1)S(1)} %collective-permute-done.15.refs_2_), custom_call_target="tpu_custom_call" | custom-call | flops 1150000000 | bytes 3600000 | tf_op jit(solution)/shard_map/pallas_call | solution.py:648
  (4 shorter events, 0.1 us)
Async XLA Ops:
  1.7 9.5 %collective-permute-start.2 = (bf16[24,3200]{1,0:T(8,128)(2,1)S(1)}, bf16[24,3200]{1,0:T(8,128)(2,1)S(1)}, u32[]{:S(2)}, u32[]{:S(2)}) collective-permute-start(bf16[24,3200]{1,0:T(8,128)(2,1)S(1)} %shard_map.211.refs_0_.refs_14_), channel_id=1, source_target_pairs={{0,6},{1,7},{2,0},{3,1},{4,2},{5,3},{6,4},{7,5},{8,14},{9,15},{10,... | collective-permute-start | bytes 460808 | tf_op jit(solution)/shard_map/ppermute | solution.py:663
  6.8 13.0 %collective-permute-start.1 = (bf16[24,3200]{1,0:T(8,128)(2,1)S(1)}, bf16[24,3200]{1,0:T(8,128)(2,1)S(1)}, u32[]{:S(2)}, u32[]{:S(2)}) collective-permute-start(bf16[24,3200]{1,0:T(8,128)(2,1)S(1)} %shard_map.211.refs_0_.refs_14_), channel_id=1, source_target_pairs={{0,4},{1,5},{2,6},{3,7},{4,0},{5,1},{6,2},{7,3},{8,12},{9,13},{10,... | collective-permute-start | bytes 460808 | tf_op jit(solution)/shard_map/ppermute | solution.py:663
  6.8 13.0 %collective-permute-start = (bf16[24,3200]{1,0:T(8,128)(2,1)S(1)}, bf16[24,3200]{1,0:T(8,128)(2,1)S(1)}, u32[]{:S(2)}, u32[]{:S(2)}) collective-permute-start(bf16[24,3200]{1,0:T(8,128)(2,1)S(1)} %shard_map.211.refs_0_.refs_14_), channel_id=1, source_target_pairs={{0,2},{1,3},{2,4},{3,5},{4,6},{5,7},{6,0},{7,1},{8,10},{9,11},{10,... | collective-permute-start | bytes 460808 | tf_op jit(solution)/shard_map/ppermute | solution.py:663
  19.8 1.5 %collective-permute-start.3 = (bf16[4,8,3200]{2,1,0:T(8,128)(2,1)S(1)}, bf16[4,8,3200]{2,1,0:T(8,128)(2,1)S(1)}, u32[]{:S(2)}, u32[]{:S(2)}) collective-permute-start(bf16[4,8,3200]{2,1,0:T(8,128)(2,1)S(1)} %shard_map.212.refs_12_), channel_id=1, source_target_pairs={{0,1},{1,0},{2,3},{3,2},{4,5},{5,4},{6,7},{7,6},{8,9},{9,8},{10,11... | collective-permute-start | bytes 614408 | tf_op jit(solution)/shard_map/ppermute | solution.py:672
  21.4 10.1 %copy-start = (f32[1600]{0:T(1024)S(1)}, f32[1600]{0:T(1024)}, u32[]{:S(2)}) copy-start(f32[1600]{0:T(1024)} %param.30) | copy-start | bytes 19204
  31.1 2.1 %collective-permute-start.4 = (bf16[5,16,3712]{2,1,0:T(8,128)(2,1)S(1)}, bf16[5,16,3712]{2,1,0:T(8,128)(2,1)S(1)}, u32[]{:S(2)}, u32[]{:S(2)}) collective-permute-start(bf16[5,16,3712]{2,1,0:T(8,128)(2,1)S(1)} %get-tuple-element.35.refs_2_.refs_8_), channel_id=1, source_target_pairs={{0,1},{1,0},{2,3},{3,2},{4,5},{5,4},{6,7},{7,6},{8,9},{9,8},{10,11... | collective-permute-start | bytes 1781768 | tf_op jit(solution)/shard_map/ppermute | solution.py:672
  34.0 18.4 %collective-permute-start.7 = (bf16[16,3712]{1,0:T(8,128)(2,1)S(1)}, bf16[16,3712]{1,0:T(8,128)(2,1)S(1)}, u32[]{:S(2)}, u32[]{:S(2)}) collective-permute-start(bf16[16,3712]{1,0:T(8,128)(2,1)S(1)} %shard_map.214), channel_id=1, source_target_pairs={{0,6},{1,7},{8,14},{9,15},{16,22},{17,23},{24,30},{25,31}} | collective-permute-start | bytes 356360 | tf_op jit(solution)/shard_map/ppermute | solution.py:668
  37.2 15.3 %collective-permute-start.6 = (bf16[16,3712]{1,0:T(8,128)(2,1)S(1)}, bf16[16,3712]{1,0:T(8,128)(2,1)S(1)}, u32[]{:S(2)}, u32[]{:S(2)}) collective-permute-start(bf16[16,3712]{1,0:T(8,128)(2,1)S(1)} %shard_map.214), channel_id=1, source_target_pairs={{0,4},{1,5},{2,6},{3,7},{8,12},{9,13},{10,14},{11,15},{16,20},{17,... | collective-permute-start | bytes 356360 | tf_op jit(solution)/shard_map/ppermute | solution.py:668
  39.4 13.1 %collective-permute-start.5 = (bf16[16,3712]{1,0:T(8,128)(2,1)S(1)}, bf16[16,3712]{1,0:T(8,128)(2,1)S(1)}, u32[]{:S(2)}, u32[]{:S(2)}) collective-permute-start(bf16[16,3712]{1,0:T(8,128)(2,1)S(1)} %shard_map.214), channel_id=1, source_target_pairs={{0,2},{1,3},{2,4},{3,5},{4,6},{5,7},{8,10},{9,11},{10,12},{11,13},... | collective-permute-start | bytes 356360 | tf_op jit(solution)/shard_map/ppermute | solution.py:668
  61.1 12.7 %collective-permute-start.9 = (bf16[128,1600]{1,0:T(8,128)(2,1)S(1)}, bf16[128,1600]{1,0:T(8,128)(2,1)S(1)}, u32[]{:S(2)}, u32[]{:S(2)}) collective-permute-start(bf16[128,1600]{1,0:T(8,128)(2,1)S(1)} %get-tuple-element.43.token_ref), channel_id=1, source_target_pairs={{0,16},{8,24},{16,0},{24,8},{1,17},{9,25},{17,1},{25,9},{2,18},{10... | collective-permute-start | bytes 1228808 | tf_op jit(solution)/shard_map/ppermute | solution.py:672
  62.9 11.1 %collective-permute-start.8 = (bf16[128,1600]{1,0:T(8,128)(2,1)S(1)}, bf16[128,1600]{1,0:T(8,128)(2,1)S(1)}, u32[]{:S(2)}, u32[]{:S(2)}) collective-permute-start(bf16[128,1600]{1,0:T(8,128)(2,1)S(1)} %get-tuple-element.43.token_ref), channel_id=1, source_target_pairs={{0,8},{8,0},{16,24},{24,16},{1,9},{9,1},{17,25},{25,17},{2,10},{10... | collective-permute-start | bytes 1228808 | tf_op jit(solution)/shard_map/ppermute | solution.py:672
  74.0 8.8 %collective-permute-start.14 = (bf16[4,16,3840]{2,1,0:T(8,128)(2,1)S(1)}, bf16[4,16,3840]{2,1,0:T(8,128)(2,1)S(1)}, u32[]{:S(2)}, u32[]{:S(2)}) collective-permute-start(bf16[4,16,3840]{2,1,0:T(8,128)(2,1)S(1)} %get-tuple-element.57), channel_id=1, source_target_pairs={{0,1},{1,0},{2,3},{3,2},{4,5},{5,4},{6,7},{7,6},{8,9},{9,8},{10,11... | collective-permute-start | bytes 1474568 | tf_op jit(solution)/shard_map/ppermute | solution.py:672
  74.0 8.8 %collective-permute-start.12 = (bf16[64,1600]{1,0:T(8,128)(2,1)S(1)}, bf16[64,1600]{1,0:T(8,128)(2,1)S(1)}, u32[]{:S(2)}, u32[]{:S(2)}) collective-permute-start(bf16[64,1600]{1,0:T(8,128)(2,1)S(1)} %slice.30), channel_id=1, source_target_pairs={{0,8},{8,0},{16,24},{24,16},{1,9},{9,1},{17,25},{25,17},{2,10},{10... | collective-permute-start | bytes 614408 | tf_op jit(solution)/shard_map/ppermute | solution.py:672
  75.6 7.4 %collective-permute-start.13 = (bf16[64,1600]{1,0:T(8,128)(2,1)S(1)}, bf16[64,1600]{1,0:T(8,128)(2,1)S(1)}, u32[]{:S(2)}, u32[]{:S(2)}) collective-permute-start(bf16[64,1600]{1,0:T(8,128)(2,1)S(1)} %slice.31), channel_id=1, source_target_pairs={{0,16},{8,24},{16,0},{24,8},{1,17},{9,25},{17,1},{25,9},{2,18},{10... | collective-permute-start | bytes 614408 | tf_op jit(solution)/shard_map/ppermute | solution.py:672
  81.0 15.5 %collective-permute-start.11 = (bf16[128,1600]{1,0:T(8,128)(2,1)S(1)}, bf16[128,1600]{1,0:T(8,128)(2,1)S(1)}, u32[]{:S(2)}, u32[]{:S(2)}) collective-permute-start(bf16[128,1600]{1,0:T(8,128)(2,1)S(1)} %get-tuple-element.55), channel_id=1, source_target_pairs={{0,16},{8,24},{16,0},{24,8},{1,17},{9,25},{17,1},{25,9},{2,18},{10... | collective-permute-start | bytes 1228808 | tf_op jit(solution)/shard_map/ppermute | solution.py:672
  82.2 14.3 %collective-permute-start.10 = (bf16[128,1600]{1,0:T(8,128)(2,1)S(1)}, bf16[128,1600]{1,0:T(8,128)(2,1)S(1)}, u32[]{:S(2)}, u32[]{:S(2)}) collective-permute-start(bf16[128,1600]{1,0:T(8,128)(2,1)S(1)} %get-tuple-element.54), channel_id=1, source_target_pairs={{0,8},{8,0},{16,24},{24,16},{1,9},{9,1},{17,25},{25,17},{2,10},{10... | collective-permute-start | bytes 1228808 | tf_op jit(solution)/shard_map/ppermute | solution.py:672
  83.0 8.1 %collective-permute-start.16 = (bf16[16,3840]{1,0:T(8,128)(2,1)S(1)}, bf16[16,3840]{1,0:T(8,128)(2,1)S(1)}, u32[]{:S(2)}, u32[]{:S(2)}) collective-permute-start(bf16[16,3840]{1,0:T(8,128)(2,1)S(1)} %get-tuple-element.62), channel_id=1, source_target_pairs={{0,2},{1,3},{2,4},{3,5},{4,6},{5,7},{6,0},{7,1},{8,10},{9,11},{10,... | collective-permute-start | bytes 368648 | tf_op jit(solution)/shard_map/ppermute | solution.py:663
  83.4 12.3 %collective-permute-start.17 = (bf16[16,3840]{1,0:T(8,128)(2,1)S(1)}, bf16[16,3840]{1,0:T(8,128)(2,1)S(1)}, u32[]{:S(2)}, u32[]{:S(2)}) collective-permute-start(bf16[16,3840]{1,0:T(8,128)(2,1)S(1)} %get-tuple-element.63), channel_id=1, source_target_pairs={{0,4},{1,5},{2,6},{3,7},{4,0},{5,1},{6,2},{7,3},{8,12},{9,13},{10,... | collective-permute-start | bytes 368648 | tf_op jit(solution)/shard_map/ppermute | solution.py:663
  83.5 12.3 %collective-permute-start.18 = (bf16[16,3840]{1,0:T(8,128)(2,1)S(1)}, bf16[16,3840]{1,0:T(8,128)(2,1)S(1)}, u32[]{:S(2)}, u32[]{:S(2)}) collective-permute-start(bf16[16,3840]{1,0:T(8,128)(2,1)S(1)} %get-tuple-element.64), channel_id=1, source_target_pairs={{0,6},{1,7},{2,0},{3,1},{4,2},{5,3},{6,4},{7,5},{8,14},{9,15},{10,... | collective-permute-start | bytes 368648 | tf_op jit(solution)/shard_map/ppermute | solution.py:663
  91.1 12.0 %collective-permute-start.15 = (bf16[128,1600]{1,0:T(8,128)(2,1)S(1)}, bf16[128,1600]{1,0:T(8,128)(2,1)S(1)}, u32[]{:S(2)}, u32[]{:S(2)}) collective-permute-start(bf16[128,1600]{1,0:T(8,128)(2,1)S(1)} %shard_map.220), channel_id=1, source_target_pairs={{0,24},{8,16},{16,8},{24,0},{1,25},{9,17},{17,9},{25,1},{2,26},{10... | collective-permute-start | bytes 1228808 | tf_op jit(solution)/shard_map/ppermute | solution.py:672
where the time goes:
time: 104 us
  Pallas kernels  44.8 us (43%)
  waiting for transfers between devices  32 us (31%)
  starting transfers between devices  26.5 us (25%)
    pallas_call x12, Pallas kernels, call(): pl.pallas_call(kernel, out_shape=tuple((out_kind(shape, dtype) for shape,...  44.8 us
    ppermute x10, waiting for transfers between devices, swapped(): lax.ppermute(block, axis, [(i, i ^ mask) for i in range(lax.axis_size(axi...  18.6 us
    ppermute x6, waiting for transfers between devices, shifted(): lax.ppermute(block, axis, [(i, (i + distance) % size) for i in range(size)])  13.4 us
    ppermute x6, starting transfers between devices, shifted(): lax.ppermute(block, axis, [(i, (i + distance) % size) for i in range(size)])  9.94 us
    ppermute x10, starting transfers between devices, swapped(): lax.ppermute(block, axis, [(i, i ^ mask) for i in range(lax.axis_size(axi...  9.64 us
    ppermute x3, starting transfers between devices, passed_up(): lax.ppermute(block, axis, [(i, i + distance) for i in range(size - distan...  6.9 us
  transfers between devices with their start and end apart: 19, of which 9 were waited for; matrix products, arithmetic and copies ran while one was open for 0% of the time, Pallas kernels for 22%

commit v1 on v0

--- a/solution.py
+++ b/solution.py
@@ -142,37 +142,24 @@
         refs[-1][k] = ref[...].astype(F32)[STATE:].astype(BF16)
 
 
-def terms_kernel(lags, seed_count, *refs):
-    scalar_hbm = refs[:4]
-    x_hbm, taps_hbm, x_proj_hbm, dt_proj_hbm, out_proj_hbm = refs[4:9]
-    vec_hbm = refs[9:12]
-    edge_mine_ref, edge_other_ref = refs[12:14]
-    seed_refs = refs[14 : 14 + seed_count]
-    refs = refs[14 + seed_count :]
-    (
-        mixed_ref, step_ref, push_ref, decay_ref, proj_ref, slot_edge_ref, weight_ref, bundle_ref
-    ) = refs[:8]
-    scalars = refs[8:12]
-    ext_ref = bundle_ref.at[0]
-    (x_s, taps_ref, x_proj_ref, dt_proj_ref, bias_s, dt_bias_s, rate_s, rows_s, conv_s, edge_s, b_s,
-     sums_s, sems) = refs[12:]
-    lens_ref, cont_ref, source_ref, owner_ref = scalars
+def conv_kernel(
+    lens_hbm, x_hbm, taps_hbm, bias_hbm, dt_bias_hbm, rate_hbm, skip_hbm, x_proj_hbm, dt_proj_hbm,
+    out_proj_hbm, conv_ref, rows_ref, taps_ref, dt_bias_ref, rate_ref, skip_ref, x_proj_ref,
+    dt_proj_ref, weight_ref, lens_ref, x_s, bias_s, sems,
+):
     row_count, inner = x_s.shape
-    request_count = lens_ref.shape[1]
-    chips = edge_mine_ref.shape[0]
+    lags = taps_ref.shape[0] - 1
     blocks = lane_blocks(inner, SIDE)
-    side = SIDE // LANE
-    pairs = list(zip(scalar_hbm, scalars))
-    pairs += [(taps_hbm, taps_ref)]
-    pairs += list(zip(vec_hbm, (bias_s, dt_bias_s, rate_s)))
+    pairs = [(lens_hbm, lens_ref), (taps_hbm, taps_ref), (bias_hbm, bias_s)]
     pairs += [(x_hbm.at[:, cols], x_s.at[:, cols]) for cols in blocks]
-    pairs += [(x_proj_hbm, x_proj_ref), (dt_proj_hbm, dt_proj_ref), (out_proj_hbm, weight_ref)]
+    pairs += [
+        (dt_bias_hbm, dt_bias_ref), (rate_hbm, rate_ref), (skip_hbm, skip_ref),
+        (x_proj_hbm, x_proj_ref), (dt_proj_hbm, dt_proj_ref), (out_proj_hbm, weight_ref),
+    ]
     copies = start_all(pairs, sems)
-    for copy in copies[:8]:
+    for copy in copies[:3]:
         copy.wait()
-    me = lax.axis_index("seq")
-    core = lax.rem(me, 2)
-    marks = request_marks(lens_ref, me * row_count)
+    marks = request_marks(lens_ref, lax.axis_index("seq") * row_count)
     row = lax.broadcasted_iota(jnp.int32, (row_count, 1), 0)
     near = []
     for lag in range(1, lags + 1):
@@ -180,21 +167,62 @@
         for begin, _ in marks:
             hit = hit + jnp.logical_and(row >= begin, row < begin + lag).astype(jnp.int32)
         near.append((hit == 0).astype(F32))
-    rows_s[0:8, :] = jnp.zeros((8, inner), F32)
-    before = edge_other_ref[1 - core].astype(F32)
-    rows_s[8 - lags : 8, :] = before[lags : 2 * lags, :]
+    rows_ref[0:8, :] = jnp.zeros((8, inner), F32)
+    for k, cols in enumerate(blocks):
+        copies[3 + k].wait()
+        here = x_s[:, cols].astype(F32)
+        rows_ref[8 : 8 + row_count, cols] = here
+        total = wide_row(bias_s, k * (SIDE // LANE), SIDE // LANE) + taps_ref[
+            lags : lags + 1, cols
+        ] * here
+        for lag in range(1, lags + 1):
+            back = rows_ref[8 - lag : 8 - lag + row_count, cols]
+            total = total + taps_ref[lags - lag : lags - lag + 1, cols] * (near[lag - 1] * back)
+        conv_ref[:, cols] = total
+    for copy in copies[3 + len(blocks) :]:
+        copy.wait()
+
+
+def terms_kernel(lags, seed_count, *refs):
+    scalar_hbm = refs[:4]
+    (conv_ref, rows_ref, taps_ref, dt_bias_s, rate_s, skip_s, x_proj_ref, dt_proj_ref,
+     edge_mine_ref, edge_other_ref) = refs[4:14]
+    seed_refs = refs[14 : 14 + seed_count]
+    refs = refs[14 + seed_count :]
+    (step_ref, jump_ref, push_ref, base_ref, decay_ref, b_s, c_s, coef_ref, slot_edge_ref,
+     bundle_ref) = refs[:10]
+    scalars = refs[10:14]
+    mixed_s, conv_s, edge_s, tail_s, sums_s, sems = refs[14:]
+    ext_ref = bundle_ref.at[0]
+    lens_ref, cont_ref, source_ref, owner_ref = scalars
+    row_count, inner = conv_s.shape
+    request_count = lens_ref.shape[1]
+    chips = edge_mine_ref.shape[0]
+    blocks = lane_blocks(inner, SIDE)
+    side = SIDE // LANE
+    copies = start_all(list(zip(scalar_hbm, scalars)), sems)
+    me = lax.axis_index("seq")
+    core = lax.rem(me, 2)
+    row = lax.broadcasted_iota(jnp.int32, (row_count, 1), 0)
+    for cols in blocks:
+        conv_s[:, cols] = conv_ref[:, cols]
     for k, ref in enumerate(seed_refs):
         bundle_ref[1 + k, :, 0:inner] = ref[...].astype(F32)[:STATE].astype(BF16)
-    for k, cols in enumerate(blocks):
-        copies[8 + k].wait()
-        here = x_s[:, cols].astype(F32)
-        rows_s[8 : 8 + row_count, cols] = here
-        total = wide_row(bias_s, k * side, side) + taps_ref[lags : lags + 1, cols] * here
-        for lag in range(1, lags + 1):
-            back = rows_s[8 - lag : 8 - lag + row_count, cols]
-            total = total + taps_ref[lags - lag : lags - lag + 1, cols] * (near[lag - 1] * back)
-        conv_s[:, cols] = total
+    tail_s[0:lags, :] = edge_other_ref[1 - core].astype(F32)[lags : 2 * lags, :]
     slot_edge_ref[...] = jnp.zeros(slot_edge_ref.shape, F32)
+    for copy in copies:
+        copy.wait()
+    marks = request_marks(lens_ref, me * row_count)
+    for p in range(lags):
+        extra = jnp.zeros((1, inner), F32)
+        for lag in range(p + 1, lags + 1):
+            near = jnp.float32(1.0)
+            for begin, _ in marks:
+                near = jnp.where(jnp.logical_and(begin <= p, begin > p - lag), 0.0, near)
+            extra = extra + taps_ref[lags - lag : lags - lag + 1, :] * (
+                near * tail_s[lags + p - lag : lags + p - lag + 1, :]
+            )
+        conv_s[p : p + 1, :] = conv_s[p : p + 1, :] + extra
     for r in range(request_count):
         begin, end = marks[r]
         length = lens_ref[0, r]
@@ -225,10 +253,18 @@
         def _(r=r, end=end, length=length):
             owner = owner_ref[0, r]
             for lag in range(lags):
-                @pl.when(length > lag)
+                at = end - 1 - lag
+
+                @pl.when(jnp.logical_and(length > lag, at >= 0))
                 def _():
-                    slot_edge_ref[owner, lags - 1 - lag : lags - lag, :] = rows_s[
-                        pl.ds(end + 7 - lag, 1), :
+                    slot_edge_ref[owner, lags - 1 - lag : lags - lag, :] = rows_ref[
+                        pl.ds(8 + at, 1), :
+                    ]
+
+                @pl.when(jnp.logical_and(length > lag, at < 0))
+                def _():
+                    slot_edge_ref[owner, lags - 1 - lag : lags - lag, :] = tail_s[
+                        pl.ds(lags + at, 1), :
                     ]
 
                 @pl.when(length <= lag)
@@ -237,51 +273,54 @@
                         pl.ds(lags + length - 1 - lag, 1), :
                     ]
 
-    for cols in blocks:
+    for k, cols in enumerate(blocks):
         v = conv_s[:, cols]
-        mixed_ref[:, cols] = (v / (1.0 + jnp.exp(-v))).astype(BF16)
-    copies[-3].wait()
-    projected = lax.dot_general(
-        mixed_ref[...], x_proj_ref[...], NT, preferred_element_type=F32
-    )
-    proj_ref[...] = projected
+        mixed = (v / (1.0 + jnp.exp(-v))).astype(BF16)
+        mixed_s[:, cols] = mixed
+        base_ref[:, cols] = wide_row(skip_s, k * side, side) * mixed.astype(F32)
+    projected = lax.dot_general(mixed_s[...], x_proj_ref[...], NT, preferred_element_type=F32)
     rank = dt_proj_ref.shape[0]
     dt_low = projected[:, :rank].astype(BF16)
+    coef_ref[...] = projected[:, rank : rank + 2 * STATE]
+    for s in range(STATE):
+        at = rank + s
+        b_s[s] = jnp.broadcast_to(projected[:, at : at + 1], (row_count, LANE))
+        at = rank + STATE + s
+        c_s[s] = jnp.broadcast_to(projected[:, at : at + 1], (row_count, LANE))
     last_begin = jnp.int32(0)
+    jump = jnp.zeros((row_count, 1), F32)
     for begin, _ in marks:
         last_begin = jnp.where(
             jnp.logical_and(begin >= 0, begin < row_count), jnp.maximum(last_begin, begin), last_begin
         )
+        jump = jump + (row == begin).astype(F32) * FAR
     in_last = (row >= last_begin).astype(F32)
-    for s in range(STATE):
-        b_s[s] = jnp.broadcast_to(
-            projected[:, rank + s : rank + s + 1] * in_last, (row_count, LANE)
-        )
     m_row, m_col, same = segment_masks(row_count, marks)
     later = tripled(jnp.logical_and(m_col > m_row, same))
-    copies[-2].wait()
     for k, cols in enumerate(blocks):
-        step_ref[:, cols] = softplus(
+        step = softplus(
             jnp.dot(dt_low, dt_proj_ref[:, cols], preferred_element_type=F32)
             + wide_row(dt_bias_s, k * side, side)
         )
+        step_ref[:, cols] = step
+        jump_ref[:, cols] = step + jump
+        push_ref[:, cols] = step * mixed_s[:, cols].astype(F32)
     for k, cols in enumerate(blocks):
-        step = step_ref[:, cols]
-        suffix = jnp.dot(later, three_parts(step), preferred_element_type=F32)
+        suffix = jnp.dot(later, three_parts(step_ref[:, cols]), preferred_element_type=F32)
         decay_ref[:, cols] = jnp.exp(-wide_row(rate_s, k * side, side) * suffix)
-        push_ref[:, cols] = step * mixed_ref[:, cols].astype(F32)
 
     def tile_step(i, carry):
         at = pl.multiple_of(i * LANE, LANE)
         cols = pl.ds(at, LANE)
-        ext_ref[:, cols] = weighted_sum(push_ref[:, cols], decay_ref[:, cols], b_s).astype(BF16)
+        ext_ref[:, cols] = weighted_sum(
+            push_ref[:, cols] * in_last, decay_ref[:, cols], b_s
+        ).astype(BF16)
         sums_s[pl.ds(i, 1), :] = jnp.sum(step_ref[:, cols] * in_last, axis=0, keepdims=True)
         return carry
 
     sums_s[...] = jnp.zeros(sums_s.shape, F32)
-    lax.fori_loop(0, inner // LANE, tile_step, 0)
+    lax.fori_loop(0, inner // LANE, tile_step, 0, unroll=5)
     write_sums(ext_ref, sums_s[...], inner)
-    copies[-1].wait()
 
 
 def weighted_sum(push, decay, b_ref):
@@ -300,78 +339,89 @@
     )
 
 
-def pair_kernel(tokens, *refs):
-    lens_hbm, rate_hbm, mine_ref, other_ref = refs[:4]
-    mine_ref, other_ref = mine_ref.at[0], other_ref.at[0]
-    out_ref, lens_ref, rate_s, sems = refs[4:]
-    for copy in start_all([(lens_hbm, lens_ref), (rate_hbm, rate_s)], sems):
-        copy.wait()
-    inner = LANE * rate_s.shape[0]
-    me = lax.axis_index("seq")
-    core = lax.rem(me, 2)
-    second = me - core + 1
-    marks = request_marks(lens_ref, second * tokens)
+def link_spans(earlier_of, later_of, whole, rate_ref, out_ref):
+    tiles = rate_ref.shape[0]
+    inner = tiles * LANE
+    sums = []
+    for i in range(tiles):
+        cols = slice(i * LANE, (i + 1) * LANE)
+        e0, s0 = earlier_of(cols, i, inner)
+        e1, s1 = later_of(cols, i, inner)
+        rate = rate_block(rate_ref[i : i + 1, :])
+        out_ref[:, cols] = (e1 + whole * jnp.exp(-rate * s1) * e0).astype(BF16)
+        sums.append(s1 + whole * s0)
+    groups, _ = sum_layout(tiles)
+    sums.append(jnp.zeros((groups * STATE - len(sums), LANE), F32))
+    write_sums(out_ref, jnp.concatenate(sums, axis=0), inner)
+
+
+def unbroken(marks, first, stop):
     whole = jnp.float32(1.0)
     for begin, _ in marks:
-        whole = jnp.where(jnp.logical_and(begin >= 0, begin < tokens), 0.0, whole)
-    sums = []
-    for i in range(inner // LANE):
-        cols = slice(i * LANE, (i + 1) * LANE)
-        mine, other = mine_ref[:, cols].astype(F32), other_ref[:, cols].astype(F32)
-        e0 = jnp.where(core == 0, mine, other)
-        e1 = jnp.where(core == 0, other, mine)
-        my_sum, other_sum = read_sum(mine_ref, i, inner), read_sum(other_ref, i, inner)
-        s0 = jnp.where(core == 0, my_sum, other_sum)
-        s1 = jnp.where(core == 0, other_sum, my_sum)
-        rate = rate_block(rate_s[i : i + 1, :])
-        out_ref[:, cols] = (e1 + whole * jnp.exp(-rate * s1) * e0).astype(BF16)
-        sums.append(s1 + whole * s0)
-    groups, _ = sum_layout(inner // LANE)
-    sums.append(jnp.zeros((groups * STATE - len(sums), LANE), F32))
-    write_sums(out_ref, jnp.concatenate(sums, axis=0), inner)
-
-
-def scan_kernel(
-    lens_hbm, gate_hbm, up_hbm, down_hbm, rate_hbm, skip_hbm, mixed_ref, step_ref, push_ref, proj_ref,
-    y_ref, q_ref, gate_ref, up_ref, down_ref, lens_ref, rate_s, skip_s, jump_s, b_s, c_s, sems,
-):
-    row_count, inner = mixed_ref.shape
-    copies = start_all(
-        [
-            (lens_hbm, lens_ref), (rate_hbm, rate_s), (skip_hbm, skip_s),
-            (gate_hbm, gate_ref), (up_hbm, up_ref), (down_hbm, down_ref),
-        ],
-        sems,
-    )
-    rank = proj_ref.shape[1] - 2 * STATE
-    coefs = proj_ref[:, rank : rank + 2 * STATE]
-    coefs = jnp.concatenate([coefs, jnp.zeros((row_count, LANE - 2 * STATE), F32)], axis=1)
-    flipped = jnp.transpose(coefs)
+        whole = jnp.where(jnp.logical_and(begin >= first, begin < stop), 0.0, whole)
+    return whole
+
+
+def reader(ref):
+    return lambda cols, i, inner: (ref[:, cols].astype(F32), read_sum(ref, i, inner))
+
+
+def pair_kernel(tokens, lens_hbm, rate_ref, mine_ref, other_ref, out_ref, lens_ref, sems):
+    for copy in start_all([(lens_hbm, lens_ref)], sems):
+        copy.wait()
+    core = lax.rem(lax.axis_index("seq"), 2)
+    marks = request_marks(lens_ref, lax.axis_index("seq") * tokens)
+    mine, other = reader(mine_ref.at[0]), reader(other_ref.at[0])
+
+    def choose(number):
+        def read(*where):
+            return [jnp.where(core == number, a, b) for a, b in zip(mine(*where), other(*where))]
+
+        return read
+
+    second = (1 - core) * tokens
+    link_spans(choose(0), choose(1), unbroken(marks, second, second + tokens), rate_ref, out_ref)
+
+
+def span_kernel(tokens, chips, lens_hbm, rate_ref, mine_ref, before_ref, out_ref, lens_ref, sems):
+    for copy in start_all([(lens_hbm, lens_ref)], sems):
+        copy.wait()
+    core = lax.rem(lax.axis_index("seq"), 2)
+    marks = request_marks(lens_ref, lax.axis_index("seq") * tokens)
+    stop = (2 - core) * tokens
+    whole = unbroken(marks, stop - 2 * chips * tokens, stop)
+    link_spans(reader(before_ref), reader(mine_ref), whole, rate_ref, out_ref)
+
+
+def spread_kernel(lens_hbm, rate_s, step_ref, coef_ref, b_ref, c_ref, q_ref, lens_ref, sems):
+    row_count, inner = step_ref.shape
+    copies = start_all([(lens_hbm, lens_ref)], sems)
+    spare = jnp.zeros((row_count, LANE - 2 * STATE), F32)
+    flipped = jnp.transpose(jnp.concatenate([coef_ref[...], spare], axis=1))
     for t in range(row_count):
-        b_s[t] = jnp.broadcast_to(flipped[0:STATE, t : t + 1], (STATE, LANE))
-        c_s[t] = jnp.broadcast_to(flipped[STATE : 2 * STATE, t : t + 1], (STATE, LANE))
-    for copy in copies[:3]:
-        copy.wait()
-    me = lax.axis_index("seq")
-    marks = request_marks(lens_ref, me * row_count)
+        b_ref[t] = jnp.broadcast_to(flipped[0:STATE, t : t + 1], (STATE, LANE))
+        c_ref[t] = jnp.broadcast_to(flipped[STATE : 2 * STATE, t : t + 1], (STATE, LANE))
+    copies[0].wait()
+    marks = request_marks(lens_ref, lax.axis_index("seq") * row_count)
     m_row, m_col, same = segment_masks(row_count, marks)
     earlier = tripled(jnp.logical_and(m_col <= m_row, same))
-    row = lax.broadcasted_iota(jnp.int32, (row_count, 1), 0)
-    jump = jnp.zeros((row_count, 1), F32)
-    for begin, _ in marks:
-        jump = jump + (row == begin).astype(F32) * FAR
-    tiles = 5
-    width = tiles * LANE
-    for k, cols in enumerate(lane_blocks(inner, width)):
-        step = step_ref[:, cols]
-        prefix = jnp.dot(earlier, three_parts(step), preferred_element_type=F32)
-        q_ref[:, cols] = jnp.exp(-wide_row(rate_s, k * tiles, tiles) * prefix)
-        jump_s[:, cols] = step + jump
-        y_ref[:, cols] = wide_row(skip_s, k * tiles, tiles) * mixed_ref[:, cols].astype(F32)
+    side = SIDE // LANE
+    for k, cols in enumerate(lane_blocks(inner, SIDE)):
+        prefix = jnp.dot(earlier, three_parts(step_ref[:, cols]), preferred_element_type=F32)
+        q_ref[:, cols] = jnp.exp(-wide_row(rate_s, k * side, side) * prefix)
+
+
+def scan_kernel(first_side, sides, fetched, *refs):
+    fetch_hbm = refs[:fetched]
+    rate_s, jump_ref, push_ref, base_ref, b_s, c_s, y_ref = refs[fetched : fetched + 7]
+    copies = start_all(list(zip(fetch_hbm, refs[fetched + 7 :])), refs[-1])
+    row_count = jump_ref.shape[0]
+    tiles = SIDE // LANE
+    width = SIDE
 
     def chunk_step(i, carry):
-        at = pl.multiple_of(i * width, LANE)
-        rates = [-LOG2E * rate_block(row_of(rate_s, i * tiles + k)) for k in range(tiles)]
+        at = pl.multiple_of((first_side + i) * width, LANE)
+        rates = [-LOG2E * rate_block(row_of(rate_s, (first_side + i) * tiles + k)) for k in range(tiles)]
 
         def row_step(j, held):
             first = pl.multiple_of(j * 8, 8)
@@ -379,7 +429,7 @@
             held = list(held)
             for k in range(tiles):
                 lanes = pl.ds(pl.multiple_of(at + k * LANE, LANE), LANE)
-                jumps, pushes = jump_s.at[rows, lanes], push_ref.at[rows, lanes]
+                jumps, pushes = jump_ref.at[rows, lanes], push_ref.at[rows, lanes]
                 h = held[k]
                 outs = []
                 for t in range(8):
@@ -388,16 +438,18 @@
                     product = c_s[first + t] * h
                     outs.append(product[0:8] + product[8:16])
                 held[k] = h
-                y_ref[rows, lanes] = y_ref[rows, lanes] + sums_of_eight(outs)
+                out_lanes = pl.ds(pl.multiple_of(i * width + k * LANE, LANE), LANE)
+                y_ref[rows, out_lanes] = base_ref[rows, lanes] + sums_of_eight(outs)
             return tuple(held)
 
         lax.fori_loop(
-            0, row_count // 8, row_step, tuple(jnp.zeros((STATE, LANE), F32) for _ in range(tiles))
+            0, row_count // 8, row_step, tuple(jnp.zeros((STATE, LANE), F32) for _ in range(tiles)),
+            unroll=2,
         )
         return carry
 
-    lax.fori_loop(0, inner // width, chunk_step, 0)
-    for copy in copies[3:]:
+    lax.fori_loop(0, sides, chunk_step, 0)
+    for copy in copies:
         copy.wait()
 
 
@@ -405,34 +457,32 @@
     scalar_hbm = refs[:3]
     rate_hbm, hidden_hbm = refs[3:5]
     stage_refs = refs[5 : 5 + stage_count]
-    (mine_ref, other_ref, proj_ref, y_ref, q_ref, gain_ref, weight_ref) = refs[
-        5 + stage_count : 12 + stage_count
+    (mine_ref, other_ref, c_s, y_first_ref, y_rest_ref, q_ref, gain_ref, weight_ref) = refs[
+        5 + stage_count : 13 + stage_count
     ]
+    refs = refs[1:]
     middle_ref, normed_ref, begins_ref = refs[12 + stage_count : 15 + stage_count]
     scalars = refs[15 + stage_count : 18 + stage_count]
-    rate_s, hidden_s, c_s, ssm_s, sems = refs[18 + stage_count :]
+    rate_s, hidden_s, ssm_s, sems = refs[18 + stage_count :]
     pair_ref = other_ref.at[0]
     lens_ref, cont_ref, source_ref = scalars
-    row_count, inner = y_ref.shape
-    width = middle_ref.shape[1]
+    row_count, inner = q_ref.shape
+    width = middle_ref.shape[0]
     chips = mine_ref.shape[0] - 1
     copies = start_all(
         list(zip(scalar_hbm, scalars)) + [(rate_hbm, rate_s), (hidden_hbm, hidden_s)], sems
     )
     me = lax.axis_index("seq")
     core = lax.rem(me, 2)
-    rank = proj_ref.shape[1] - 2 * STATE
-    for s in range(STATE):
-        c_s[s] = jnp.broadcast_to(
-            proj_ref[:, rank + STATE + s : rank + STATE + s + 1], (row_count, LANE)
-        )
-    ssm_s[...] = y_ref[...]
+    parting = y_first_ref.shape[1]
+    ssm_s[:, 0:parting] = y_first_ref[...]
+    ssm_s[:, parting:inner] = y_rest_ref[...]
     for copy in copies:
         copy.wait()
     marks = request_marks(lens_ref, me * row_count)
     tiles = 5
     side = tiles * LANE
-    block = 16
+    block = 32
     for r in range(lens_ref.shape[1]):
         begin, end = marks[r]
         low, high = jnp.maximum(begin, 0), jnp.minimum(end, row_count)
@@ -449,9 +499,10 @@
 
             for k in range(stage_count + 1):
                 if k < stage_count:
-                    chip_first = me - core - 2 * (stage_count - k)
+                    away = 1 << (stage_count - 1 - k)
+                    chip_first = me - core - 2 * away
                     ref = stage_refs[stage_count - 1 - k]
-                    stage_end = -(core + 2 * (stage_count - 1 - k)) * row_count
+                    stage_end = -(core + 2 * (away - 1)) * row_count
                     valid = jnp.logical_and(chip_first >= 0, begin < stage_end)
                 else:
                     ref = pair_ref
@@ -489,21 +540,18 @@
 
             lax.fori_loop(low // block, (high + block - 1) // block, block_step, 0)
 
-    total = lax.dot_general(
-        ssm_s[...].astype(BF16), weight_ref[...], NT, preferred_element_type=F32
-    )
-    residual = [
-        jnp.transpose(hidden_s[cols, :].astype(F32)) for cols in lane_blocks(width, LANE)
-    ]
-    total = total + jnp.concatenate(residual, axis=1)
+    total = hidden_s[...].astype(F32) + lax.dot_general(
+        weight_ref[...], ssm_s[...].astype(BF16), NT, preferred_element_type=F32
+    )
     middle_ref[...] = total
-    scale = lax.rsqrt(jnp.mean(total * total, axis=1, keepdims=True) + NORM_EPS)
-    normed_ref[...] = (total * scale * gain_ref[...]).astype(BF16)
+    total = total * lax.rsqrt(jnp.mean(total * total, axis=0, keepdims=True) + NORM_EPS)
+    for cols in lane_blocks(width, LANE):
+        normed_ref[:, cols] = (jnp.transpose(total[cols, :]) * gain_ref[:, cols]).astype(BF16)
 
 
 def final_kernel(
-    lens_hbm, owner_hbm, rate_hbm, step_ref, push_ref, decay_ref, proj_ref, begins_ref,
-    slot_edge_ref, keep_ref, send_ref, lens_ref, owner_ref, rate_s, b_s, held_s, edge_s, sems,
+    lens_hbm, owner_hbm, rate_hbm, step_ref, push_ref, decay_ref, b_ref, begins_ref,
+    slot_edge_ref, keep_ref, send_ref, lens_ref, owner_ref, rate_s, held_s, edge_s, sems,
 ):
     pairs = [(lens_hbm, lens_ref), (owner_hbm, owner_ref), (rate_hbm, rate_s)]
     for copy in start_all(pairs, sems):
@@ -514,7 +562,6 @@
     core = lax.rem(me, 2)
     chips = keep_ref.shape[0]
     marks = request_marks(lens_ref, me * row_count)
-    rank = proj_ref.shape[1] - 2 * STATE
     lags = slot_edge_ref.shape[1]
     row = lax.broadcasted_iota(jnp.int32, (row_count, 1), 0)
     keep_ref[...] = jnp.zeros(keep_ref.shape, BF16)
@@ -530,11 +577,6 @@
             there = lax.rem(owner // 2 - me // 2 + chips, chips)
             mine = lax.rem(owner, 2) == core
             inside = jnp.logical_and(row >= begin, row < end).astype(F32)
-            for s in range(STATE):
-                b_s[s] = jnp.broadcast_to(
-                    proj_ref[:, rank + s : rank + s + 1] * inside, (row_count, LANE)
-                )
-
             def put(cols, block):
                 @pl.when(mine)
                 def _():
@@ -547,12 +589,15 @@
             held_s[...] = jnp.zeros(held_s.shape, F32)
 
             def block_step(j, carry):
-                rows = pl.ds(pl.multiple_of(j * block, block), block)
+                first = pl.multiple_of(j * block, block)
+                rows = pl.ds(first, block)
+                at_row = lax.broadcasted_iota(jnp.int32, (block, 1), 0) + first
+                here = jnp.logical_and(at_row >= begin, at_row < end).astype(F32)
 
                 def add_tile(i, inner_carry):
                     cols = pl.ds(pl.multiple_of(i * LANE, LANE), LANE)
                     held_s[:, cols] = held_s[:, cols] + weighted_sum(
-                        push_ref[rows, cols], decay_ref[rows, cols], b_s.at[:, rows, :]
+                        push_ref[rows, cols] * here, decay_ref[rows, cols], b_ref.at[:, rows, :]
                     )
                     return inner_carry
 
@@ -615,8 +660,8 @@
     return lax.dot_general(hidden, down_ref[...], NT, preferred_element_type=F32)
 
 
-def own_kernel(token_ref, middle_ref, gate_ref, up_ref, down_ref, out_ref):
-    out_ref[...] = middle_ref[...] + feed_forward(token_ref[...], gate_ref, up_ref, down_ref)
+def own_kernel(token_ref, gate_ref, up_ref, down_ref, out_ref):
+    out_ref[...] = feed_forward(token_ref[...], gate_ref, up_ref, down_ref)
 
 
 def peer_kernel(*refs):
@@ -633,12 +678,12 @@
     out_ref[...] = feed_forward(tokens, gate_ref, up_ref, down_ref).astype(BF16)
 
 
-def join_kernel(own_ref, *refs):
+def join_kernel(middle_ref, own_ref, *refs):
     whole = own_ref[...]
     for ref in refs[:-1]:
         whole = whole + ref[...].astype(F32)
     for cols in lane_blocks(whole.shape[1], LANE):
-        refs[-1][cols, :] = jnp.transpose(whole[:, cols]).astype(BF16)
+        refs[-1][cols, :] = (middle_ref[cols, :] + jnp.transpose(whole[:, cols])).astype(BF16)
 
 
 def call(kernel, outs, scratch, operands, hbm=0, limit=16, micros=1.0, last=False):
@@ -718,10 +763,6 @@
         limit=4,
     )
     offers = [offer] + [shifted(offer, "seq", 2 * k) for k in range(1, chips)]
-    (edge_mine,) = call(
-        edges_kernel, [((chips, OFFER - STATE, inner), BF16)], [], tuple(offers), limit=4
-    )
-    edge_other = swapped(edge_mine, "seq", 1)
     bias, dt_bias, rate, skip = [
         v.reshape(tiles, LANE) for v in (conv_bias, dt_bias, decay_rate, skip_gain)
     ]
@@ -732,68 +773,99 @@
     rank = x_proj.shape[1]
     full = ((row_count, inner), F32)
     bundle_shape = ((chips + 1, *ext_shape), BF16)
-    mixed, step, push, decay, proj, slot_edge, weight, bundle = call(
+    wide = ((STATE, row_count, LANE), F32)
+    blocks = len(lane_blocks(inner, SIDE))
+    conv, rows, taps, dt_bias_v, rate_v, skip_v, x_proj_v, dt_proj_v, weight = call(
+        conv_kernel,
+        [
+            full,
+            ((8 + row_count, inner), F32),
+            (conv_weight.shape, F32),
+            ((tiles, LANE), F32),
+            ((tiles, LANE), F32),
+            ((tiles, LANE), F32),
+            ((rank, inner), BF16),
+            (dt_proj.shape, BF16),
+            ((width, inner), BF16),
+        ],
+        [scalar_s, pltpu.VMEM((row_count, inner), BF16), vec_s, dma((9 + blocks,))],
+        (
+            req_lengths, x, conv_weight, bias, dt_bias, rate, skip, x_proj.T, dt_proj, out_proj.T,
+        ),
+        hbm=10,
+        limit=8,
+    )
+    offers, conv = lax.optimization_barrier((offers, conv))
+    (edge_mine,) = call(
+        edges_kernel, [((chips, OFFER - STATE, inner), BF16)], [], tuple(offers), limit=4
+    )
+    edge_other = swapped(edge_mine, "seq", 1)
+    step, jump, push, base, decay, b_wide, c_wide, coefs, slot_edge, bundle = call(
         functools.partial(terms_kernel, lags, chips),
-        [
-            ((row_count, inner), BF16),
-            full,
-            full,
-            full,
-            ((row_count, rank), F32),
-            ((peers, lags, inner), F32),
-            ((width, inner), BF16),
-            bundle_shape,
-        ],
+        [full, full, full, full, full, wide, wide, ((row_count, 2 * STATE), F32),
+         ((peers, lags, inner), F32), bundle_shape],
         [
             scalar_s, scalar_s, scalar_s, scalar_s,
             pltpu.VMEM((row_count, inner), BF16),
-            pltpu.VMEM(conv_weight.shape, F32),
-            pltpu.VMEM((rank, inner), BF16),
-            pltpu.VMEM(dt_proj.shape, BF16),
-            vec_s, vec_s, vec_s,
-            pltpu.VMEM((8 + row_count, inner), F32),
             pltpu.VMEM((row_count, inner), F32),
             pltpu.VMEM((8, inner), F32),
-            pltpu.VMEM((STATE, row_count, LANE), F32),
+            pltpu.VMEM((8, inner), F32),
             pltpu.VMEM((groups * STATE, LANE), F32),
-            dma((11 + len(lane_blocks(inner, SIDE)),)),
+            dma((4,)),
         ],
         (
-            *scalars, x, conv_weight, x_proj.T, dt_proj, out_proj.T, bias, dt_bias, rate,
+            *scalars, conv, rows, taps, dt_bias_v, rate_v, skip_v, x_proj_v, dt_proj_v,
             edge_mine, edge_other, *offers,
         ),
-        hbm=12,
-        micros=10,
+        hbm=4,
+        limit=10,
     )
     other = swapped(bundle, "seq", 1)
-    (chip,) = call(
-        functools.partial(pair_kernel, row_count),
-        [(ext_shape, BF16)],
-        [scalar_s, vec_s, dma((2,))],
-        (req_lengths, rate, bundle, other),
-        hbm=2,
-        limit=4,
-    )
-    stages = [passed_up(chip, "seq", 2 * k) for k in range(1, chips)]
-    y, q, gate, up, down = call(
-        scan_kernel,
-        [full, full, (mlp_gate.shape, BF16), (mlp_up.shape, BF16), (mlp_down.shape[::-1], BF16)],
-        [
-            scalar_s, vec_s, vec_s,
-            pltpu.VMEM((row_count, inner), F32),
-            pltpu.VMEM((row_count, STATE, LANE), F32),
-            pltpu.VMEM((row_count, STATE, LANE), F32),
-            dma((6,)),
-        ],
-        (req_lengths, mlp_gate, mlp_up, mlp_down.T, rate, skip, mixed, step, push, proj),
-        hbm=6,
-        limit=8,
-        micros=8,
-    )
+    b_rows, c_rows, q = call(
+        spread_kernel,
+        [((row_count, STATE, LANE), F32), ((row_count, STATE, LANE), F32), full],
+        [scalar_s, dma((1,))],
+        (req_lengths, rate_v, step, coefs),
+        hbm=1,
+        limit=6,
+    )
+    other, b_rows, c_rows, q = lax.optimization_barrier((other, b_rows, c_rows, q))
+    span_call = functools.partial(
+        call, outs=[(ext_shape, BF16)], scratch=[scalar_s, dma((1,))], hbm=1, limit=4
+    )
+    (span,) = span_call(
+        functools.partial(pair_kernel, row_count), operands=(req_lengths, rate_v, bundle, other)
+    )
+
+    def scan_call(first_side, sides, fetch):
+        return call(
+            functools.partial(scan_kernel, first_side, sides, len(fetch)),
+            [((row_count, sides * SIDE), F32)] + [(w.shape, BF16) for w in fetch],
+            [dma((len(fetch),))],
+            (*fetch, rate_v, jump, push, base, b_rows, c_rows),
+            hbm=len(fetch),
+            limit=4,
+        )
+
+    all_sides = inner // SIDE
+    early = (2 * all_sides) // 5
+    y_first, gate = scan_call(0, early, (mlp_gate,))
+    stages = [passed_up(span, "seq", 2)]
+    first_stage, y_first, gate = lax.optimization_barrier((stages[0], y_first, gate))
+    stages = [first_stage]
+    reach = 2
+    while reach < chips:
+        (span,) = span_call(
+            functools.partial(span_kernel, row_count, reach // 2),
+            operands=(req_lengths, rate_v, span, stages[-1]),
+        )
+        stages.append(passed_up(span, "seq", 2 * reach))
+        reach = 2 * reach
+    y_rest, up, down = scan_call(early, all_sides - early, (mlp_up, mlp_down.T))
     middle, normed, begins = call(
         functools.partial(close_kernel, len(stages)),
         [
-            ((row_count, width), F32),
+            ((width, row_count), F32),
             ((row_count, width), BF16),
             ((request_count, STATE, inner), F32),
         ],
@@ -801,12 +873,11 @@
             scalar_s, scalar_s, scalar_s,
             vec_s,
             pltpu.VMEM((width, row_count), BF16),
-            pltpu.VMEM((STATE, row_count, LANE), F32),
             pltpu.VMEM((row_count, inner), F32),
             dma((5,)),
         ],
         (
-            *scalars[:3], rate, hidden_in[0].T, *stages, bundle, other, proj, y, q,
+            *scalars[:3], rate, hidden_in[0].T, *stages, bundle, other, c_wide, y_first, y_rest, q,
             norm_gain.reshape(1, width), weight,
         ),
         hbm=5,
@@ -817,7 +888,7 @@
     tokens_out = ((row_count, width), BF16)
     from_x, from_y = swapped(normed, "req", 1), swapped(normed, "req", 2)
     (own,) = call(
-        own_kernel, [((row_count, width), F32)], [], (normed, middle, *weights), limit=4, micros=3
+        own_kernel, [((row_count, width), F32)], [], (normed, *weights), limit=4, micros=3
     )
     edge_groups = -(-lags * tiles // STATE)
     packed = ((chips, STATE, inner + edge_groups * LANE), BF16)
@@ -826,12 +897,11 @@
         [packed, packed],
         [
             scalar_s, scalar_s, vec_s,
-            pltpu.VMEM((STATE, row_count, LANE), F32),
             pltpu.VMEM((STATE, inner), F32),
             pltpu.VMEM((edge_groups * STATE, LANE), F32),
             dma((3,)),
         ],
-        (req_lengths, owner_slot, rate, step, push, decay, proj, begins, slot_edge),
+        (req_lengths, owner_slot, rate, step, push, decay, b_wide, begins, slot_edge),
         hbm=3,
         limit=4,
         micros=4,
@@ -860,7 +930,7 @@
         last=True,
     )
     (block_rows,) = call(
-        join_kernel, [((width, row_count), BF16)], [], (own, back_x, back_y, back_far), limit=4,
+        join_kernel, [((width, row_count), BF16)], [], (middle, own, back_x, back_y, back_far), limit=4,
         last=True,
     )
     return (block_rows.T[None], new_state[None, None], new_edge[None, None])

time: 104 us -> 98.5 us (0.947)
  waiting for transfers between devices: 32 us -> 19.2 us
  Pallas kernels: 44.8 us -> 50.2 us
  starting transfers between devices: 26.5 us -> 28.1 us
    ppermute x6, waiting for transfers between devices: 13.4 us -> 5.22 us  [shifted(): lax.ppermute(block, axis, [(i, (i + distance) % size) for i in range(size)])]
    pallas_call x12 -> x16, Pallas kernels: 44.8 us -> 50.2 us  [call(): pl.pallas_call(kernel, out_shape=tuple((out_kind(shape, dtype) for shape,...]
    ppermute x10, waiting for transfers between devices: 18.6 us -> 14 us  [swapped(): lax.ppermute(block, axis, [(i, i ^ mask) for i in range(lax.axis_size(axi...]
    ppermute x3 -> x2, starting transfers between devices: 6.9 us -> 9.13 us  [passed_up(): lax.ppermute(block, axis, [(i, i + distance) for i in range(size - distan...]
    ppermute x10, starting transfers between devices: 9.64 us -> 8.1 us  [swapped(): lax.ppermute(block, axis, [(i, i ^ mask) for i in range(lax.axis_size(axi...]
  transfers between devices with their start and end apart: 19 -> 18, of which waited for: 9 -> 8; matrix products, arithmetic and copies ran while one was open for 0% -> 0% of each run, Pallas kernels for 22% -> 32%
where the time goes in v1:
time: 98.5 us
  Pallas kernels  50.2 us (51%)
  starting transfers between devices  28.1 us (29%)
  waiting for transfers between devices  19.2 us (19%)
    pallas_call x16, Pallas kernels, call(): pl.pallas_call(kernel, out_shape=tuple((out_kind(shape, dtype) for shape,...  50.2 us
    ppermute x10, waiting for transfers between devices, swapped(): lax.ppermute(block, axis, [(i, i ^ mask) for i in range(lax.axis_size(axi...  14 us
    ppermute x6, starting transfers between devices, shifted(): lax.ppermute(block, axis, [(i, (i + distance) % size) for i in range(size)])  10.9 us
    ppermute x2, starting transfers between devices, passed_up(): lax.ppermute(block, axis, [(i, i + distance) for i in range(size - distan...  9.13 us
    ppermute x10, starting transfers between devices, swapped(): lax.ppermute(block, axis, [(i, i ^ mask) for i in range(lax.axis_size(axi...  8.1 us
    ppermute x6, waiting for transfers between devices, shifted(): lax.ppermute(block, axis, [(i, (i + distance) % size) for i in range(size)])  5.22 us
  transfers between devices with their start and end apart: 18, of which 8 were waited for; matrix products, arithmetic and copies ran while one was open for 0% of the time, Pallas kernels for 32%

profile of v1, /device:TPU:0, one launch (start us, length us, event | category | flops | bytes accessed | tf_op | source)
XLA Modules:
  0.0 98.5 jit_solution(7594901629288459164)
XLA Ops:
  0.6 1.1 %shard_map.212.refs_0_.refs_14_ = bf16[24,3200]{1,0:T(8,128)(2,1)S(1)} custom-call(f32[16,3200]{1,0:T(8,128)} %bitcast.38, bf16[3,3200]{1,0:T(4,128)(2,1)} %bitcast.39, bf16[128,3200]{1,0:T(8,128)(2,1)} %bitcast.29), custom_call_target="tpu_custom_call" | custom-call | flops 1150000000 | bytes 3600000 | tf_op jit(solution)/shard_map/pallas_call | solution.py:693
  1.7 3.1 %collective-permute-start = (bf16[24,3200]{1,0:T(8,128)(2,1)S(1)}, bf16[24,3200]{1,0:T(8,128)(2,1)S(1)}, u32[]{:S(2)}, u32[]{:S(2)}) collective-permute-start(bf16[24,3200]{1,0:T(8,128)(2,1)S(1)} %shard_map.212.refs_0_.refs_14_), channel_id=1, source_target_pairs={{0,2},{1,3},{2,4},{3,5},{4,6},{5,7},{6,0},{7,1},{8,10},{9,11},{10,... | collective-permute-start | bytes 460808 | tf_op jit(solution)/shard_map/ppermute | solution.py:708
  4.8 2.6 %collective-permute-start.1 = (bf16[24,3200]{1,0:T(8,128)(2,1)S(1)}, bf16[24,3200]{1,0:T(8,128)(2,1)S(1)}, u32[]{:S(2)}, u32[]{:S(2)}) collective-permute-start(bf16[24,3200]{1,0:T(8,128)(2,1)S(1)} %shard_map.212.refs_0_.refs_14_), channel_id=1, source_target_pairs={{0,4},{1,5},{2,6},{3,7},{4,0},{5,1},{6,2},{7,3},{8,12},{9,13},{10,... | collective-permute-start | bytes 460808 | tf_op jit(solution)/shard_map/ppermute | solution.py:708
  7.4 1.3 %collective-permute-start.2 = (bf16[24,3200]{1,0:T(8,128)(2,1)S(1)}, bf16[24,3200]{1,0:T(8,128)(2,1)S(1)}, u32[]{:S(2)}, u32[]{:S(2)}) collective-permute-start(bf16[24,3200]{1,0:T(8,128)(2,1)S(1)} %shard_map.212.refs_0_.refs_14_), channel_id=1, source_target_pairs={{0,6},{1,7},{2,0},{3,1},{4,2},{5,3},{6,4},{7,5},{8,14},{9,15},{10,... | collective-permute-start | bytes 460808 | tf_op jit(solution)/shard_map/ppermute | solution.py:708
  8.7 4.9 %shard_map.211 = (f32[128,3200]{1,0:T(8,128)S(1)}, f32[136,3200]{1,0:T(8,128)S(1)}, f32[4,3200]{1,0:T(4,128)S(1)}, f32[25,128]{1,0:T(8,128)S(1)}, f32[25,128]{1,...) custom-call(s32[1,4]{1,0:T(1,128)} %lens_hbm.9, ...), custom_call_target="tpu_custom_call" | custom-call | flops 1150000000 | bytes 3600000 | tf_op jit(solution)/shard_map/pallas_call | solution.py:693
  13.7 0.0 collective-permute-done.refs_1_.refs_15_
  13.7 3.8 %collective-permute-done.1.refs_2_.refs_16_ = bf16[24,3200]{1,0:T(8,128)(2,1)S(1)} collective-permute-done((bf16[24,3200]{1,0:T(8,128)(2,1)S(1)}, bf16[24,3200]{1,0:T(8,128)(2,1)S(1)}, u32[]{:S(2)}, u32[]{:S(2)}) %collective-permute-start.1) | collective-permute-done | bytes 153632 | tf_op jit(solution)/shard_map/ppermute | solution.py:708
  17.5 0.0 collective-permute-done.2.refs_3_.refs_17_
  17.5 0.1 collective-permute-start.3
  17.6 1.4 %collective-permute-done.3.refs_13_ = bf16[4,8,3200]{2,1,0:T(8,128)(2,1)S(1)} collective-permute-done((bf16[4,8,3200]{2,1,0:T(8,128)(2,1)S(1)}, bf16[4,8,3200]{2,1,0:T(8,128)(2,1)S(1)}, u32[]{:S(2)}, u32[]{:S(2)}) %collective-permute-start.3) | collective-permute-done | bytes 204832 | tf_op jit(solution)/shard_map/ppermute | solution.py:717
  19.0 7.0 %shard_map.214 = (f32[128,3200]{1,0:T(8,128)S(1)}, f32[128,3200]{1,0:T(8,128)S(1)}, f32[128,3200]{1,0:T(8,128)S(1)}, f32[128,3200]{1,0:T(8,128)S(1)}, f32[128,32...) custom-call(s32[1,4]{1,0:T(1,128)} %lens_hbm.9, ...), custom_call_target="tpu_custom_call" | custom-call | flops 1150000000 | bytes 3600000 | tf_op jit(solution)/shard_map/pallas_call | solution.py:693
  26.0 0.1 collective-permute-start.4
  26.0 1.7 %shard_map.215 = (f32[128,16,128]{2,1,0:T(8,128)S(1)}, f32[128,16,128]{2,1,0:T(8,128)S(1)}, f32[128,3200]{1,0:T(8,128)S(1)}) custom-call(s32[1,4]{1,0:T(1,128)} %lens_hbm.9, f32[25,128]{1,0:T(8,128)S(1)} %get-tuple-element.61.refs_8_.rate_s.rate_ref.refs_1_.refs_2_, f32[128,3200]{1,0:T(8,128)S(1)} %get-tuple-element.75.step_ref, ...), custom_call_target="tpu_custom_call" | custom-call | flops 1150000000 | bytes 3600000 | tf_op jit(solution)/shard_map/pallas_call | solution.py:693
  27.7 0.3 collective-permute-done.4.other_ref.refs_8_
  28.0 0.8 shard_map.216.mine_ref
  28.9 5.5 %collective-permute-start.5 = (bf16[16,3712]{1,0:T(8,128)(2,1)S(1)}, bf16[16,3712]{1,0:T(8,128)(2,1)S(1)}, u32[]{:S(2)}, u32[]{:S(2)}) collective-permute-start(bf16[16,3712]{1,0:T(8,128)(2,1)S(1)} %shard_map.216.mine_ref), channel_id=1, source_target_pairs={{0,2},{1,3},{2,4},{3,5},{4,6},{5,7},{8,10},{9,11},{10,12},{11,13},... | collective-permute-start | bytes 356360 | tf_op jit(solution)/shard_map/ppermute | solution.py:713
  34.3 0.0 copy-start
  34.3 3.6 %shard_map.217 = (f32[128,1280]{1,0:T(8,128)S(1)}, bf16[1600,1376]{1,0:T(8,128)(2,1)S(1)}) custom-call(bf16[1600,1376]{1,0:T(8,128)(2,1)} %refs_0_.5, f32[25,128]{1,0:T(8,128)S(1)} %get-tuple-element.61.refs_8_.rate_s.rate_ref.refs_1_.refs_2_, f32[128,3200]{1,0:T(8,128)S(1)} %get-tuple-element.81.refs_2_.refs_3_, ...), custom_call_target="tpu_custom_call" | custom-call | flops 1150000000 | bytes 3600000 | tf_op jit(solution)/shard_map/pallas_call | solution.py:693
  38.0 0.0 collective-permute-done.5.before_ref.refs_5_
  38.0 0.8 shard_map.218
  38.8 3.7 %collective-permute-start.6 = (bf16[16,3712]{1,0:T(8,128)(2,1)S(1)}, bf16[16,3712]{1,0:T(8,128)(2,1)S(1)}, u32[]{:S(2)}, u32[]{:S(2)}) collective-permute-start(bf16[16,3712]{1,0:T(8,128)(2,1)S(1)} %shard_map.218), channel_id=1, source_target_pairs={{0,4},{1,5},{2,6},{3,7},{8,12},{9,13},{10,14},{11,15},{16,20},{17,... | collective-permute-start | bytes 356360 | tf_op jit(solution)/shard_map/ppermute | solution.py:713
  42.4 0.0 copy-done
  42.5 5.4 %shard_map.219 = (f32[128,1920]{1,0:T(8,128)S(1)}, bf16[1600,1376]{1,0:T(8,128)(2,1)S(1)}, bf16[1600,1376]{1,0:T(8,128)(2,1)S(1)}) custom-call(bf16[1600,1376]{1,0:T(8,128)(2,1)} %refs_0_.6, bf16[1600,1376]{1,0:T(8,128)(2,1)} %bitcast.27, f32[25,128]{1,0:T(8,128)S(1)} %get-tuple-element.61.refs_8_.rate_s.rate_ref.refs_1_.refs_2_, ...), custom_call_target="tpu_custom_call" | custom-call | flops 1150000000 | bytes 3600000 | tf_op jit(solution)/shard_map/pallas_call | solution.py:693
  47.9 0.0 collective-permute-done.6.refs_6_
  47.9 8.3 %shard_map.220 = (f32[1600,128]{1,0:T(8,128)S(1)}, bf16[128,1600]{1,0:T(8,128)(2,1)S(1)}, f32[4,16,3200]{2,1,0:T(8,128)S(1)}) custom-call(s32[1,4]{1,0:T(1,128)} %lens_hbm.9, s32[1,4]{1,0:T(1,128)} %refs_1_.3, s32[1,4]{1,0:T(1,128)} %refs_2_.3, f32[25,128]{1,0:T(8,128)} %bitcast.35, bf16[1600,128]{1,0:T(8,128)(2,1)} %bitcast.37, ...), custom_call_target="tpu_custom_call" | custom-call | flops 6899999744 | bytes 21600000 | tf_op jit(solution)/shard_map/pallas_call | solution.py:693
  56.2 0.6 collective-permute-start.7
  56.9 2.3 %collective-permute-start.8 = (bf16[128,1600]{1,0:T(8,128)(2,1)S(1)}, bf16[128,1600]{1,0:T(8,128)(2,1)S(1)}, u32[]{:S(2)}, u32[]{:S(2)}) collective-permute-start(bf16[128,1600]{1,0:T(8,128)(2,1)S(1)} %get-tuple-element.95.token_ref), channel_id=1, source_target_pairs={{0,16},{8,24},{16,0},{24,8},{1,17},{9,25},{17,1},{25,9},{2,18},{10... | collective-permute-start | bytes 1228808 | tf_op jit(solution)/shard_map/ppermute | solution.py:717
  59.2 4.5 %shard_map.222 = (bf16[4,16,3840]{2,1,0:T(8,128)(2,1)S(1)}, bf16[4,16,3840]{2,1,0:T(8,128)(2,1)S(1)}) custom-call(s32[1,4]{1,0:T(1,128)} %lens_hbm.9, s32[1,4]{1,0:T(1,128)} %owner_hbm.1, f32[25,128]{1,0:T(8,128)} %bitcast.36, f32[128,3200]{1,0:T(8,128)S(1)} %get-tuple-element.75.step_ref, f32[128,3200]{1,0:T(8,128)S(1)} %get-tuple-element.82.refs_3_.refs_4_.push_ref, ...), custom_call_target="tpu_custom_call" | custom-call | flops 4600000000 | bytes 14400000 | tf_op jit(solution)/shard_map/pallas_call | solution.py:693
  63.6 4.5 %collective-permute-done.7.refs_0_ = bf16[128,1600]{1,0:T(8,128)(2,1)S(1)} collective-permute-done((bf16[128,1600]{1,0:T(8,128)(2,1)S(1)}, bf16[128,1600]{1,0:T(8,128)(2,1)S(1)}, u32[]{:S(2)}, u32[]{:S(2)}) %collective-permute-start.7) | collective-permute-done | bytes 409632 | tf_op jit(solution)/shard_map/ppermute | solution.py:717
  68.2 1.5 %collective-permute-done.8.refs_1_ = bf16[128,1600]{1,0:T(8,128)(2,1)S(1)} collective-permute-done((bf16[128,1600]{1,0:T(8,128)(2,1)S(1)}, bf16[128,1600]{1,0:T(8,128)(2,1)S(1)}, u32[]{:S(2)}, u32[]{:S(2)}) %collective-permute-start.8) | collective-permute-done | bytes 409632 | tf_op jit(solution)/shard_map/ppermute | solution.py:717
  69.6 0.0 collective-permute-start.13
  69.7 0.4 collective-permute-start.11
  70.1 0.8 collective-permute-start.12
  70.9 4.5 %shard_map.223 = (bf16[128,1600]{1,0:T(8,128)(2,1)S(1)}, bf16[128,1600]{1,0:T(8,128)(2,1)S(1)}) custom-call(bf16[128,1600]{1,0:T(8,128)(2,1)S(1)} %collective-permute-done.7.refs_0_, bf16[128,1600]{1,0:T(8,128)(2,1)S(1)} %collective-permute-done.8.refs_1_, bf16[1600,1376]{1,0:T(8,128)(2,1)S(1)} %get-tuple-element.96.gate_ref.refs_2_, ...), custom_call_target="tpu_custom_call" | custom-call | flops 5175000064 | bytes 16200000 | tf_op jit(solution)/shard_map/pallas_call | solution.py:693
  75.4 1.4 %collective-permute-start.10 = (bf16[128,1600]{1,0:T(8,128)(2,1)S(1)}, bf16[128,1600]{1,0:T(8,128)(2,1)S(1)}, u32[]{:S(2)}, u32[]{:S(2)}) collective-permute-start(bf16[128,1600]{1,0:T(8,128)(2,1)S(1)} %get-tuple-element.107), channel_id=1, source_target_pairs={{0,16},{8,24},{16,0},{24,8},{1,17},{9,25},{17,1},{25,9},{2,18},{10... | collective-permute-start | bytes 1228808 | tf_op jit(solution)/shard_map/ppermute | solution.py:717
  76.8 1.7 %collective-permute-start.9 = (bf16[128,1600]{1,0:T(8,128)(2,1)S(1)}, bf16[128,1600]{1,0:T(8,128)(2,1)S(1)}, u32[]{:S(2)}, u32[]{:S(2)}) collective-permute-start(bf16[128,1600]{1,0:T(8,128)(2,1)S(1)} %get-tuple-element.106), channel_id=1, source_target_pairs={{0,8},{8,0},{16,24},{24,16},{1,9},{9,1},{17,25},{25,17},{2,10},{10... | collective-permute-start | bytes 1228808 | tf_op jit(solution)/shard_map/ppermute | solution.py:717
  78.5 0.0 collective-permute-done.13
  78.5 0.1 add_bitcast_fusion
  78.5 0.0 collective-permute-done.11.low_ref
  78.5 0.0 collective-permute-done.12.high_ref
  78.5 0.1 collective-permute-start.15
  78.6 2.5 %collective-permute-start.16 = (bf16[16,3840]{1,0:T(8,128)(2,1)S(1)}, bf16[16,3840]{1,0:T(8,128)(2,1)S(1)}, u32[]{:S(2)}, u32[]{:S(2)}) collective-permute-start(bf16[16,3840]{1,0:T(8,128)(2,1)S(1)} %get-tuple-element.115), channel_id=1, source_target_pairs={{0,4},{1,5},{2,6},{3,7},{4,0},{5,1},{6,2},{7,3},{8,12},{9,13},{10,... | collective-permute-start | bytes 368648 | tf_op jit(solution)/shard_map/ppermute | solution.py:708
  81.1 1.3 %collective-permute-start.17 = (bf16[16,3840]{1,0:T(8,128)(2,1)S(1)}, bf16[16,3840]{1,0:T(8,128)(2,1)S(1)}, u32[]{:S(2)}, u32[]{:S(2)}) collective-permute-start(bf16[16,3840]{1,0:T(8,128)(2,1)S(1)} %get-tuple-element.116), channel_id=1, source_target_pairs={{0,6},{1,7},{2,0},{3,1},{4,2},{5,3},{6,4},{7,5},{8,14},{9,15},{10,... | collective-permute-start | bytes 368648 | tf_op jit(solution)/shard_map/ppermute | solution.py:708
  82.4 2.9 %shard_map.224 = bf16[128,1600]{1,0:T(8,128)(2,1)S(1)} custom-call(bf16[64,1600]{1,0:T(8,128)(2,1)S(1)} %collective-permute-done.11.low_ref, bf16[64,1600]{1,0:T(8,128)(2,1)S(1)} %collective-permute-done.12.high_ref, bf16[1600,1376]{1,0:T(8,128)(2,1)S(1)} %get-tuple-element.96.gate_ref.refs_2_, bf16[1600,1376]{1,0:T(8,128)(2,1)S(1)} %get-tuple-element.97.up_ref.refs_3_, ...), custom_call_target="tpu_custom_call" | custom-call | flops 3449999872 | bytes 10800000 | tf_op jit(solution)/shard_map/pallas_call | solution.py:693
  85.3 1.4 %collective-permute-done.15.refs_1_ = bf16[16,3840]{1,0:T(8,128)(2,1)S(1)} collective-permute-done((bf16[16,3840]{1,0:T(8,128)(2,1)S(1)}, bf16[16,3840]{1,0:T(8,128)(2,1)S(1)}, u32[]{:S(2)}, u32[]{:S(2)}) %collective-permute-start.15) | collective-permute-done | bytes 122912 | tf_op jit(solution)/shard_map/ppermute | solution.py:708
  86.7 0.8 collective-permute-start.14
  87.5 2.9 %shard_map.221.own_ref = f32[128,1600]{1,0:T(8,128)S(1)} custom-call(bf16[128,1600]{1,0:T(8,128)(2,1)S(1)} %get-tuple-element.95.token_ref, bf16[1600,1376]{1,0:T(8,128)(2,1)S(1)} %get-tuple-element.96.gate_ref.refs_2_, bf16[1600,1376]{1,0:T(8,128)(2,1)S(1)} %get-tuple-element.97.up_ref.refs_3_, bf16[1600,1376]{1,0:T(8,128)(2,1)S(1)} %get-tuple-element.98.down_ref.refs_4_), custom_call_target="tpu_custom_call" | custom-call | flops 3449999872 | bytes 10800000 | tf_op jit(solution)/shard_map/pallas_call | solution.py:693
  90.4 0.1 collective-permute-done.16.refs_2_
  90.4 0.0 collective-permute-done.17.refs_3_
  90.4 0.7 shard_map.226
  91.2 0.0 collective-permute-done.10.refs_1_
  91.2 0.0 collective-permute-done.9.refs_0_
  91.2 6.3 %collective-permute-done.14.refs_2_ = bf16[128,1600]{1,0:T(8,128)(2,1)S(1)} collective-permute-done((bf16[128,1600]{1,0:T(8,128)(2,1)S(1)}, bf16[128,1600]{1,0:T(8,128)(2,1)S(1)}, u32[]{:S(2)}, u32[]{:S(2)}) %collective-permute-start.14) | collective-permute-done | bytes 409632 | tf_op jit(solution)/shard_map/ppermute | solution.py:717
  97.5 1.0 %shard_map.225 = bf16[1600,128]{1,0:T(8,128)(2,1)} custom-call(f32[1600,128]{1,0:T(8,128)S(1)} %get-tuple-element.94.middle_ref, f32[128,1600]{1,0:T(8,128)S(1)} %shard_map.221.own_ref, bf16[128,1600]{1,0:T(8,128)(2,1)S(1)} %collective-permute-done.9.refs_0_, bf16[128,1600]{1,0:T(8,128)(2,1)S(1)} %collective-permute-done.10.refs_1_, ...), custom_call_target="tpu_custom_call" | custom-call | flops 1150000000 | bytes 3600000 | tf_op jit(solution)/shard_map/pallas_call | solution.py:693
  (4 shorter events, 0.1 us)
Async XLA Ops:
  1.7 12.0 %collective-permute-start = (bf16[24,3200]{1,0:T(8,128)(2,1)S(1)}, bf16[24,3200]{1,0:T(8,128)(2,1)S(1)}, u32[]{:S(2)}, u32[]{:S(2)}) collective-permute-start(bf16[24,3200]{1,0:T(8,128)(2,1)S(1)} %shard_map.212.refs_0_.refs_14_), channel_id=1, source_target_pairs={{0,2},{1,3},{2,4},{3,5},{4,6},{5,7},{6,0},{7,1},{8,10},{9,11},{10,... | collective-permute-start | bytes 460808 | tf_op jit(solution)/shard_map/ppermute | solution.py:708
  4.8 12.7 %collective-permute-start.1 = (bf16[24,3200]{1,0:T(8,128)(2,1)S(1)}, bf16[24,3200]{1,0:T(8,128)(2,1)S(1)}, u32[]{:S(2)}, u32[]{:S(2)}) collective-permute-start(bf16[24,3200]{1,0:T(8,128)(2,1)S(1)} %shard_map.212.refs_0_.refs_14_), channel_id=1, source_target_pairs={{0,4},{1,5},{2,6},{3,7},{4,0},{5,1},{6,2},{7,3},{8,12},{9,13},{10,... | collective-permute-start | bytes 460808 | tf_op jit(solution)/shard_map/ppermute | solution.py:708
  7.4 10.1 %collective-permute-start.2 = (bf16[24,3200]{1,0:T(8,128)(2,1)S(1)}, bf16[24,3200]{1,0:T(8,128)(2,1)S(1)}, u32[]{:S(2)}, u32[]{:S(2)}) collective-permute-start(bf16[24,3200]{1,0:T(8,128)(2,1)S(1)} %shard_map.212.refs_0_.refs_14_), channel_id=1, source_target_pairs={{0,6},{1,7},{2,0},{3,1},{4,2},{5,3},{6,4},{7,5},{8,14},{9,15},{10,... | collective-permute-start | bytes 460808 | tf_op jit(solution)/shard_map/ppermute | solution.py:708
  17.5 1.5 %collective-permute-start.3 = (bf16[4,8,3200]{2,1,0:T(8,128)(2,1)S(1)}, bf16[4,8,3200]{2,1,0:T(8,128)(2,1)S(1)}, u32[]{:S(2)}, u32[]{:S(2)}) collective-permute-start(bf16[4,8,3200]{2,1,0:T(8,128)(2,1)S(1)} %shard_map.213.refs_12_), channel_id=1, source_target_pairs={{0,1},{1,0},{2,3},{3,2},{4,5},{5,4},{6,7},{7,6},{8,9},{9,8},{10,11... | collective-permute-start | bytes 614408 | tf_op jit(solution)/shard_map/ppermute | solution.py:717
  26.0 2.1 %collective-permute-start.4 = (bf16[5,16,3712]{2,1,0:T(8,128)(2,1)S(1)}, bf16[5,16,3712]{2,1,0:T(8,128)(2,1)S(1)}, u32[]{:S(2)}, u32[]{:S(2)}) collective-permute-start(bf16[5,16,3712]{2,1,0:T(8,128)(2,1)S(1)} %get-tuple-element.74.mine_ref.refs_7_), channel_id=1, source_target_pairs={{0,1},{1,0},{2,3},{3,2},{4,5},{5,4},{6,7},{7,6},{8,9},{9,8},{10,11... | collective-permute-start | bytes 1781768 | tf_op jit(solution)/shard_map/ppermute | solution.py:717
  28.9 9.1 %collective-permute-start.5 = (bf16[16,3712]{1,0:T(8,128)(2,1)S(1)}, bf16[16,3712]{1,0:T(8,128)(2,1)S(1)}, u32[]{:S(2)}, u32[]{:S(2)}) collective-permute-start(bf16[16,3712]{1,0:T(8,128)(2,1)S(1)} %shard_map.216.mine_ref), channel_id=1, source_target_pairs={{0,2},{1,3},{2,4},{3,5},{4,6},{5,7},{8,10},{9,11},{10,12},{11,13},... | collective-permute-start | bytes 356360 | tf_op jit(solution)/shard_map/ppermute | solution.py:713
  34.3 8.1 %copy-start = (f32[1600]{0:T(1024)S(1)}, f32[1600]{0:T(1024)}, u32[]{:S(2)}) copy-start(f32[1600]{0:T(1024)} %param.30) | copy-start | bytes 19204
  38.8 9.1 %collective-permute-start.6 = (bf16[16,3712]{1,0:T(8,128)(2,1)S(1)}, bf16[16,3712]{1,0:T(8,128)(2,1)S(1)}, u32[]{:S(2)}, u32[]{:S(2)}) collective-permute-start(bf16[16,3712]{1,0:T(8,128)(2,1)S(1)} %shard_map.218), channel_id=1, source_target_pairs={{0,4},{1,5},{2,6},{3,7},{8,12},{9,13},{10,14},{11,15},{16,20},{17,... | collective-permute-start | bytes 356360 | tf_op jit(solution)/shard_map/ppermute | solution.py:713
  56.2 11.9 %collective-permute-start.7 = (bf16[128,1600]{1,0:T(8,128)(2,1)S(1)}, bf16[128,1600]{1,0:T(8,128)(2,1)S(1)}, u32[]{:S(2)}, u32[]{:S(2)}) collective-permute-start(bf16[128,1600]{1,0:T(8,128)(2,1)S(1)} %get-tuple-element.95.token_ref), channel_id=1, source_target_pairs={{0,8},{8,0},{16,24},{24,16},{1,9},{9,1},{17,25},{25,17},{2,10},{10... | collective-permute-start | bytes 1228808 | tf_op jit(solution)/shard_map/ppermute | solution.py:717
  56.9 12.8 %collective-permute-start.8 = (bf16[128,1600]{1,0:T(8,128)(2,1)S(1)}, bf16[128,1600]{1,0:T(8,128)(2,1)S(1)}, u32[]{:S(2)}, u32[]{:S(2)}) collective-permute-start(bf16[128,1600]{1,0:T(8,128)(2,1)S(1)} %get-tuple-element.95.token_ref), channel_id=1, source_target_pairs={{0,16},{8,24},{16,0},{24,8},{1,17},{9,25},{17,1},{25,9},{2,18},{10... | collective-permute-start | bytes 1228808 | tf_op jit(solution)/shard_map/ppermute | solution.py:717
  69.6 8.8 %collective-permute-start.13 = (bf16[4,16,3840]{2,1,0:T(8,128)(2,1)S(1)}, bf16[4,16,3840]{2,1,0:T(8,128)(2,1)S(1)}, u32[]{:S(2)}, u32[]{:S(2)}) collective-permute-start(bf16[4,16,3840]{2,1,0:T(8,128)(2,1)S(1)} %get-tuple-element.109), channel_id=1, source_target_pairs={{0,1},{1,0},{2,3},{3,2},{4,5},{5,4},{6,7},{7,6},{8,9},{9,8},{10,11... | collective-permute-start | bytes 1474568 | tf_op jit(solution)/shard_map/ppermute | solution.py:717
  69.7 8.9 %collective-permute-start.11 = (bf16[64,1600]{1,0:T(8,128)(2,1)S(1)}, bf16[64,1600]{1,0:T(8,128)(2,1)S(1)}, u32[]{:S(2)}, u32[]{:S(2)}) collective-permute-start(bf16[64,1600]{1,0:T(8,128)(2,1)S(1)} %slice.30), channel_id=1, source_target_pairs={{0,8},{8,0},{16,24},{24,16},{1,9},{9,1},{17,25},{25,17},{2,10},{10... | collective-permute-start | bytes 614408 | tf_op jit(solution)/shard_map/ppermute | solution.py:717
  70.1 8.4 %collective-permute-start.12 = (bf16[64,1600]{1,0:T(8,128)(2,1)S(1)}, bf16[64,1600]{1,0:T(8,128)(2,1)S(1)}, u32[]{:S(2)}, u32[]{:S(2)}) collective-permute-start(bf16[64,1600]{1,0:T(8,128)(2,1)S(1)} %slice.31), channel_id=1, source_target_pairs={{0,16},{8,24},{16,0},{24,8},{1,17},{9,25},{17,1},{25,9},{2,18},{10... | collective-permute-start | bytes 614408 | tf_op jit(solution)/shard_map/ppermute | solution.py:717
  75.4 15.8 %collective-permute-start.10 = (bf16[128,1600]{1,0:T(8,128)(2,1)S(1)}, bf16[128,1600]{1,0:T(8,128)(2,1)S(1)}, u32[]{:S(2)}, u32[]{:S(2)}) collective-permute-start(bf16[128,1600]{1,0:T(8,128)(2,1)S(1)} %get-tuple-element.107), channel_id=1, source_target_pairs={{0,16},{8,24},{16,0},{24,8},{1,17},{9,25},{17,1},{25,9},{2,18},{10... | collective-permute-start | bytes 1228808 | tf_op jit(solution)/shard_map/ppermute | solution.py:717
  76.8 14.4 %collective-permute-start.9 = (bf16[128,1600]{1,0:T(8,128)(2,1)S(1)}, bf16[128,1600]{1,0:T(8,128)(2,1)S(1)}, u32[]{:S(2)}, u32[]{:S(2)}) collective-permute-start(bf16[128,1600]{1,0:T(8,128)(2,1)S(1)} %get-tuple-element.106), channel_id=1, source_target_pairs={{0,8},{8,0},{16,24},{24,16},{1,9},{9,1},{17,25},{25,17},{2,10},{10... | collective-permute-start | bytes 1228808 | tf_op jit(solution)/shard_map/ppermute | solution.py:717
  78.5 8.2 %collective-permute-start.15 = (bf16[16,3840]{1,0:T(8,128)(2,1)S(1)}, bf16[16,3840]{1,0:T(8,128)(2,1)S(1)}, u32[]{:S(2)}, u32[]{:S(2)}) collective-permute-start(bf16[16,3840]{1,0:T(8,128)(2,1)S(1)} %get-tuple-element.114), channel_id=1, source_target_pairs={{0,2},{1,3},{2,4},{3,5},{4,6},{5,7},{6,0},{7,1},{8,10},{9,11},{10,... | collective-permute-start | bytes 368648 | tf_op jit(solution)/shard_map/ppermute | solution.py:708
  78.6 11.8 %collective-permute-start.16 = (bf16[16,3840]{1,0:T(8,128)(2,1)S(1)}, bf16[16,3840]{1,0:T(8,128)(2,1)S(1)}, u32[]{:S(2)}, u32[]{:S(2)}) collective-permute-start(bf16[16,3840]{1,0:T(8,128)(2,1)S(1)} %get-tuple-element.115), channel_id=1, source_target_pairs={{0,4},{1,5},{2,6},{3,7},{4,0},{5,1},{6,2},{7,3},{8,12},{9,13},{10,... | collective-permute-start | bytes 368648 | tf_op jit(solution)/shard_map/ppermute | solution.py:708
  81.1 9.3 %collective-permute-start.17 = (bf16[16,3840]{1,0:T(8,128)(2,1)S(1)}, bf16[16,3840]{1,0:T(8,128)(2,1)S(1)}, u32[]{:S(2)}, u32[]{:S(2)}) collective-permute-start(bf16[16,3840]{1,0:T(8,128)(2,1)S(1)} %get-tuple-element.116), channel_id=1, source_target_pairs={{0,6},{1,7},{2,0},{3,1},{4,2},{5,3},{6,4},{7,5},{8,14},{9,15},{10,... | collective-permute-start | bytes 368648 | tf_op jit(solution)/shard_map/ppermute | solution.py:708
  86.7 10.8 %collective-permute-start.14 = (bf16[128,1600]{1,0:T(8,128)(2,1)S(1)}, bf16[128,1600]{1,0:T(8,128)(2,1)S(1)}, u32[]{:S(2)}, u32[]{:S(2)}) collective-permute-start(bf16[128,1600]{1,0:T(8,128)(2,1)S(1)} %shard_map.224), channel_id=1, source_target_pairs={{0,24},{8,16},{16,8},{24,0},{1,25},{9,17},{17,9},{25,1},{2,26},{10... | collective-permute-start | bytes 1228808 | tf_op jit(solution)/shard_map/ppermute | solution.py:717

commit v2 on v1

--- a/solution.py
+++ b/solution.py
@@ -144,8 +144,8 @@
 
 def conv_kernel(
     lens_hbm, x_hbm, taps_hbm, bias_hbm, dt_bias_hbm, rate_hbm, skip_hbm, x_proj_hbm, dt_proj_hbm,
-    out_proj_hbm, conv_ref, rows_ref, taps_ref, dt_bias_ref, rate_ref, skip_ref, x_proj_ref,
-    dt_proj_ref, weight_ref, lens_ref, x_s, bias_s, sems,
+    out_proj_hbm, hidden_hbm, conv_ref, rows_ref, taps_ref, dt_bias_ref, rate_ref, skip_ref,
+    x_proj_ref, dt_proj_ref, weight_ref, hidden_ref, lens_ref, x_s, bias_s, sems,
 ):
     row_count, inner = x_s.shape
     lags = taps_ref.shape[0] - 1
@@ -155,6 +155,7 @@
     pairs += [
         (dt_bias_hbm, dt_bias_ref), (rate_hbm, rate_ref), (skip_hbm, skip_ref),
         (x_proj_hbm, x_proj_ref), (dt_proj_hbm, dt_proj_ref), (out_proj_hbm, weight_ref),
+        (hidden_hbm, hidden_ref),
     ]
     copies = start_all(pairs, sems)
     for copy in copies[:3]:
@@ -190,9 +191,9 @@
     seed_refs = refs[14 : 14 + seed_count]
     refs = refs[14 + seed_count :]
     (step_ref, jump_ref, push_ref, base_ref, decay_ref, b_s, c_s, coef_ref, slot_edge_ref,
-     bundle_ref) = refs[:10]
-    scalars = refs[10:14]
-    mixed_s, conv_s, edge_s, tail_s, sums_s, sems = refs[14:]
+     bundle_ref, whole_ref) = refs[:11]
+    scalars = refs[11:15]
+    mixed_s, conv_s, edge_s, tail_s, sums_s, sems = refs[15:]
     ext_ref = bundle_ref.at[0]
     lens_ref, cont_ref, source_ref, owner_ref = scalars
     row_count, inner = conv_s.shape
@@ -295,6 +296,13 @@
         )
         jump = jump + (row == begin).astype(F32) * FAR
     in_last = (row >= last_begin).astype(F32)
+    second = (1 - core) * row_count
+    flags = [unbroken(marks, second, second + row_count)]
+    stop = second + row_count
+    for k in range(1, whole_ref.shape[0]):
+        flags.append(unbroken(marks, stop - (row_count << k), stop))
+    for k, flag in enumerate(flags):
+        whole_ref[k : k + 1, :] = jnp.zeros((1, LANE), F32) + flag
     m_row, m_col, same = segment_masks(row_count, marks)
     later = tripled(jnp.logical_and(m_col > m_row, same))
     for k, cols in enumerate(blocks):
@@ -366,11 +374,8 @@
     return lambda cols, i, inner: (ref[:, cols].astype(F32), read_sum(ref, i, inner))
 
 
-def pair_kernel(tokens, lens_hbm, rate_ref, mine_ref, other_ref, out_ref, lens_ref, sems):
-    for copy in start_all([(lens_hbm, lens_ref)], sems):
-        copy.wait()
+def pair_kernel(rate_ref, whole_ref, mine_ref, other_ref, out_ref):
     core = lax.rem(lax.axis_index("seq"), 2)
-    marks = request_marks(lens_ref, lax.axis_index("seq") * tokens)
     mine, other = reader(mine_ref.at[0]), reader(other_ref.at[0])
 
     def choose(number):
@@ -379,17 +384,11 @@
 
         return read
 
-    second = (1 - core) * tokens
-    link_spans(choose(0), choose(1), unbroken(marks, second, second + tokens), rate_ref, out_ref)
-
-
-def span_kernel(tokens, chips, lens_hbm, rate_ref, mine_ref, before_ref, out_ref, lens_ref, sems):
-    for copy in start_all([(lens_hbm, lens_ref)], sems):
-        copy.wait()
-    core = lax.rem(lax.axis_index("seq"), 2)
-    marks = request_marks(lens_ref, lax.axis_index("seq") * tokens)
-    stop = (2 - core) * tokens
-    whole = unbroken(marks, stop - 2 * chips * tokens, stop)
+    link_spans(choose(0), choose(1), whole_ref[0:1, :], rate_ref, out_ref)
+
+
+def span_kernel(power, rate_ref, whole_ref, mine_ref, before_ref, out_ref):
+    whole = whole_ref[power : power + 1, :]
     link_spans(reader(before_ref), reader(mine_ref), whole, rate_ref, out_ref)
 
 
@@ -455,23 +454,20 @@
 
 def close_kernel(stage_count, *refs):
     scalar_hbm = refs[:3]
-    rate_hbm, hidden_hbm = refs[3:5]
+    rate_s, hidden_s = refs[3:5]
     stage_refs = refs[5 : 5 + stage_count]
     (mine_ref, other_ref, c_s, y_first_ref, y_rest_ref, q_ref, gain_ref, weight_ref) = refs[
         5 + stage_count : 13 + stage_count
     ]
-    refs = refs[1:]
-    middle_ref, normed_ref, begins_ref = refs[12 + stage_count : 15 + stage_count]
-    scalars = refs[15 + stage_count : 18 + stage_count]
-    rate_s, hidden_s, ssm_s, sems = refs[18 + stage_count :]
+    middle_ref, normed_ref, begins_ref = refs[13 + stage_count : 16 + stage_count]
+    scalars = refs[16 + stage_count : 19 + stage_count]
+    ssm_s, sems = refs[19 + stage_count :]
     pair_ref = other_ref.at[0]
     lens_ref, cont_ref, source_ref = scalars
     row_count, inner = q_ref.shape
     width = middle_ref.shape[0]
     chips = mine_ref.shape[0] - 1
-    copies = start_all(
-        list(zip(scalar_hbm, scalars)) + [(rate_hbm, rate_s), (hidden_hbm, hidden_s)], sems
-    )
+    copies = start_all(list(zip(scalar_hbm, scalars)), sems)
     me = lax.axis_index("seq")
     core = lax.rem(me, 2)
     parting = y_first_ref.shape[1]
@@ -550,10 +546,10 @@
 
 
 def final_kernel(
-    lens_hbm, owner_hbm, rate_hbm, step_ref, push_ref, decay_ref, b_ref, begins_ref,
-    slot_edge_ref, keep_ref, send_ref, lens_ref, owner_ref, rate_s, held_s, edge_s, sems,
+    lens_hbm, owner_hbm, rate_s, step_ref, push_ref, decay_ref, b_ref, begins_ref,
+    slot_edge_ref, keep_ref, send_ref, lens_ref, owner_ref, held_s, edge_s, sems,
 ):
-    pairs = [(lens_hbm, lens_ref), (owner_hbm, owner_ref), (rate_hbm, rate_s)]
+    pairs = [(lens_hbm, lens_ref), (owner_hbm, owner_ref)]
     for copy in start_all(pairs, sems):
         copy.wait()
     row_count, inner = step_ref.shape
@@ -775,7 +771,7 @@
     bundle_shape = ((chips + 1, *ext_shape), BF16)
     wide = ((STATE, row_count, LANE), F32)
     blocks = len(lane_blocks(inner, SIDE))
-    conv, rows, taps, dt_bias_v, rate_v, skip_v, x_proj_v, dt_proj_v, weight = call(
+    conv, rows, taps, dt_bias_v, rate_v, skip_v, x_proj_v, dt_proj_v, weight, hidden = call(
         conv_kernel,
         [
             full,
@@ -787,12 +783,14 @@
             ((rank, inner), BF16),
             (dt_proj.shape, BF16),
             ((width, inner), BF16),
+            ((width, row_count), BF16),
         ],
-        [scalar_s, pltpu.VMEM((row_count, inner), BF16), vec_s, dma((9 + blocks,))],
+        [scalar_s, pltpu.VMEM((row_count, inner), BF16), vec_s, dma((10 + blocks,))],
         (
             req_lengths, x, conv_weight, bias, dt_bias, rate, skip, x_proj.T, dt_proj, out_proj.T,
+            hidden_in[0].T,
         ),
-        hbm=10,
+        hbm=11,
         limit=8,
     )
     offers, conv = lax.optimization_barrier((offers, conv))
@@ -800,10 +798,10 @@
         edges_kernel, [((chips, OFFER - STATE, inner), BF16)], [], tuple(offers), limit=4
     )
     edge_other = swapped(edge_mine, "seq", 1)
-    step, jump, push, base, decay, b_wide, c_wide, coefs, slot_edge, bundle = call(
+    step, jump, push, base, decay, b_wide, c_wide, coefs, slot_edge, bundle, whole = call(
         functools.partial(terms_kernel, lags, chips),
         [full, full, full, full, full, wide, wide, ((row_count, 2 * STATE), F32),
-         ((peers, lags, inner), F32), bundle_shape],
+         ((peers, lags, inner), F32), bundle_shape, ((chips.bit_length(), LANE), F32)],
         [
             scalar_s, scalar_s, scalar_s, scalar_s,
             pltpu.VMEM((row_count, inner), BF16),
@@ -831,11 +829,9 @@
     )
     other, b_rows, c_rows, q = lax.optimization_barrier((other, b_rows, c_rows, q))
     span_call = functools.partial(
-        call, outs=[(ext_shape, BF16)], scratch=[scalar_s, dma((1,))], hbm=1, limit=4
-    )
-    (span,) = span_call(
-        functools.partial(pair_kernel, row_count), operands=(req_lengths, rate_v, bundle, other)
-    )
+        call, outs=[(ext_shape, BF16)], scratch=[], limit=4
+    )
+    (span,) = span_call(pair_kernel, operands=(rate_v, whole, bundle, other))
 
     def scan_call(first_side, sides, fetch):
         return call(
@@ -856,8 +852,8 @@
     reach = 2
     while reach < chips:
         (span,) = span_call(
-            functools.partial(span_kernel, row_count, reach // 2),
-            operands=(req_lengths, rate_v, span, stages[-1]),
+            functools.partial(span_kernel, reach.bit_length() - 1),
+            operands=(rate_v, whole, span, stages[-1]),
         )
         stages.append(passed_up(span, "seq", 2 * reach))
         reach = 2 * reach
@@ -871,17 +867,15 @@
         ],
         [
             scalar_s, scalar_s, scalar_s,
-            vec_s,
-            pltpu.VMEM((width, row_count), BF16),
             pltpu.VMEM((row_count, inner), F32),
-            dma((5,)),
+            dma((3,)),
         ],
         (
-            *scalars[:3], rate, hidden_in[0].T, *stages, bundle, other, c_wide, y_first, y_rest, q,
+            *scalars[:3], rate_v, hidden, *stages, bundle, other, c_wide, y_first, y_rest, q,
             norm_gain.reshape(1, width), weight,
         ),
-        hbm=5,
-        limit=12,
+        hbm=3,
+        limit=14,
         micros=6,
     )
     weights = (gate, up, down)
@@ -896,13 +890,13 @@
         final_kernel,
         [packed, packed],
         [
-            scalar_s, scalar_s, vec_s,
+            scalar_s, scalar_s,
             pltpu.VMEM((STATE, inner), F32),
             pltpu.VMEM((edge_groups * STATE, LANE), F32),
-            dma((3,)),
+            dma((2,)),
         ],
-        (req_lengths, owner_slot, rate, step, push, decay, b_wide, begins, slot_edge),
-        hbm=3,
+        (req_lengths, owner_slot, rate_v, step, push, decay, b_wide, begins, slot_edge),
+        hbm=2,
         limit=4,
         micros=4,
     )

time: 98.5 us -> 96.7 us (0.982)
  waiting for transfers between devices: 19.2 us -> 15.5 us
  starting transfers between devices: 28.1 us -> 30.5 us
    ppermute x10, waiting for transfers between devices: 14 us -> 10.9 us  [swapped(): lax.ppermute(block, axis, [(i, i ^ mask) for i in range(lax.axis_size(axi...]
    ppermute x10, starting transfers between devices: 8.1 us -> 9.44 us  [swapped(): lax.ppermute(block, axis, [(i, i ^ mask) for i in range(lax.axis_size(axi...]
    ppermute x6, starting transfers between devices: 10.9 us -> 12 us  [shifted(): lax.ppermute(block, axis, [(i, (i + distance) % size) for i in range(size)])]
  transfers between devices with their start and end apart: 18 -> 18, of which waited for: 8 -> 8; matrix products, arithmetic and copies ran while one was open for 0% -> 0% of each run, Pallas kernels for 32% -> 33%
where the time goes in v2:
time: 96.7 us; the launch traced here: 96.3 us
  Pallas kernels  49.4 us (51%)
  starting transfers between devices  30.5 us (32%)
  waiting for transfers between devices  15.5 us (16%)
    pallas_call x16, Pallas kernels, call(): pl.pallas_call(kernel, out_shape=tuple((out_kind(shape, dtype) for shape,...  49.4 us
    ppermute x6, starting transfers between devices, shifted(): lax.ppermute(block, axis, [(i, (i + distance) % size) for i in range(size)])  12 us
    ppermute x10, waiting for transfers between devices, swapped(): lax.ppermute(block, axis, [(i, i ^ mask) for i in range(lax.axis_size(axi...  10.9 us
    ppermute x10, starting transfers between devices, swapped(): lax.ppermute(block, axis, [(i, i ^ mask) for i in range(lax.axis_size(axi...  9.44 us
    ppermute x2, starting transfers between devices, passed_up(): lax.ppermute(block, axis, [(i, i + distance) for i in range(size - distan...  9.04 us
    ppermute x6, waiting for transfers between devices, shifted(): lax.ppermute(block, axis, [(i, (i + distance) % size) for i in range(size)])  4.61 us
  transfers between devices with their start and end apart: 18, of which 8 were waited for; matrix products, arithmetic and copies ran while one was open for 0% of the time, Pallas kernels for 33%

profile of v2, /device:TPU:0, one launch (start us, length us, event | category | flops | bytes accessed | tf_op | source)
XLA Modules:
  0.0 96.3 jit_solution(3338940044667348675)
XLA Ops:
  0.6 1.1 %shard_map.212.refs_0_.refs_14_ = bf16[24,3200]{1,0:T(8,128)(2,1)S(1)} custom-call(f32[16,3200]{1,0:T(8,128)} %bitcast.36, bf16[3,3200]{1,0:T(4,128)(2,1)} %bitcast.37, bf16[128,3200]{1,0:T(8,128)(2,1)} %bitcast.29), custom_call_target="tpu_custom_call" | custom-call | flops 1150000000 | bytes 3600000 | tf_op jit(solution)/shard_map/pallas_call | solution.py:689
  1.7 3.1 %collective-permute-start = (bf16[24,3200]{1,0:T(8,128)(2,1)S(1)}, bf16[24,3200]{1,0:T(8,128)(2,1)S(1)}, u32[]{:S(2)}, u32[]{:S(2)}) collective-permute-start(bf16[24,3200]{1,0:T(8,128)(2,1)S(1)} %shard_map.212.refs_0_.refs_14_), channel_id=1, source_target_pairs={{0,2},{1,3},{2,4},{3,5},{4,6},{5,7},{6,0},{7,1},{8,10},{9,11},{10,... | collective-permute-start | bytes 460808 | tf_op jit(solution)/shard_map/ppermute | solution.py:704
  4.8 2.6 %collective-permute-start.1 = (bf16[24,3200]{1,0:T(8,128)(2,1)S(1)}, bf16[24,3200]{1,0:T(8,128)(2,1)S(1)}, u32[]{:S(2)}, u32[]{:S(2)}) collective-permute-start(bf16[24,3200]{1,0:T(8,128)(2,1)S(1)} %shard_map.212.refs_0_.refs_14_), channel_id=1, source_target_pairs={{0,4},{1,5},{2,6},{3,7},{4,0},{5,1},{6,2},{7,3},{8,12},{9,13},{10,... | collective-permute-start | bytes 460808 | tf_op jit(solution)/shard_map/ppermute | solution.py:704
  7.4 1.3 %collective-permute-start.2 = (bf16[24,3200]{1,0:T(8,128)(2,1)S(1)}, bf16[24,3200]{1,0:T(8,128)(2,1)S(1)}, u32[]{:S(2)}, u32[]{:S(2)}) collective-permute-start(bf16[24,3200]{1,0:T(8,128)(2,1)S(1)} %shard_map.212.refs_0_.refs_14_), channel_id=1, source_target_pairs={{0,6},{1,7},{2,0},{3,1},{4,2},{5,3},{6,4},{7,5},{8,14},{9,15},{10,... | collective-permute-start | bytes 460808 | tf_op jit(solution)/shard_map/ppermute | solution.py:704
  8.7 4.9 %shard_map.211 = (f32[128,3200]{1,0:T(8,128)S(1)}, f32[136,3200]{1,0:T(8,128)S(1)}, f32[4,3200]{1,0:T(4,128)S(1)}, f32[25,128]{1,0:T(8,128)S(1)}, f32[25,128]{1,...) custom-call(s32[1,4]{1,0:T(1,128)} %lens_hbm.5, ...), custom_call_target="tpu_custom_call" | custom-call | flops 1150000000 | bytes 3600000 | tf_op jit(solution)/shard_map/pallas_call | solution.py:689
  13.7 0.0 collective-permute-done.refs_1_.refs_15_
  13.7 3.8 %collective-permute-done.1.refs_2_.refs_16_ = bf16[24,3200]{1,0:T(8,128)(2,1)S(1)} collective-permute-done((bf16[24,3200]{1,0:T(8,128)(2,1)S(1)}, bf16[24,3200]{1,0:T(8,128)(2,1)S(1)}, u32[]{:S(2)}, u32[]{:S(2)}) %collective-permute-start.1) | collective-permute-done | bytes 153632 | tf_op jit(solution)/shard_map/ppermute | solution.py:704
  17.5 0.0 collective-permute-done.2.refs_3_.refs_17_
  17.5 0.1 collective-permute-start.3
  17.6 1.4 %collective-permute-done.3.refs_13_ = bf16[4,8,3200]{2,1,0:T(8,128)(2,1)S(1)} collective-permute-done((bf16[4,8,3200]{2,1,0:T(8,128)(2,1)S(1)}, bf16[4,8,3200]{2,1,0:T(8,128)(2,1)S(1)}, u32[]{:S(2)}, u32[]{:S(2)}) %collective-permute-start.3) | collective-permute-done | bytes 204832 | tf_op jit(solution)/shard_map/ppermute | solution.py:713
  19.0 7.0 %shard_map.214 = (f32[128,3200]{1,0:T(8,128)S(1)}, f32[128,3200]{1,0:T(8,128)S(1)}, f32[128,3200]{1,0:T(8,128)S(1)}, f32[128,3200]{1,0:T(8,128)S(1)}, f32[128,32...) custom-call(s32[1,4]{1,0:T(1,128)} %lens_hbm.5, ...), custom_call_target="tpu_custom_call" | custom-call | flops 1150000000 | bytes 3600000 | tf_op jit(solution)/shard_map/pallas_call | solution.py:689
  26.0 0.1 collective-permute-start.4
  26.1 1.7 %shard_map.215 = (f32[128,16,128]{2,1,0:T(8,128)S(1)}, f32[128,16,128]{2,1,0:T(8,128)S(1)}, f32[128,3200]{1,0:T(8,128)S(1)}) custom-call(s32[1,4]{1,0:T(1,128)} %lens_hbm.5, f32[25,128]{1,0:T(8,128)S(1)} %get-tuple-element.63.refs_8_.rate_s.rate_ref.refs_1_.refs_2_.refs_3_, f32[128,3200]{1,0:T(8,128)S(1)} %get-tuple-element.79.step_ref, ...), custom_call_target="tpu_custom_call" | custom-call | flops 1150000000 | bytes 3600000 | tf_op jit(solution)/shard_map/pallas_call | solution.py:689
  27.8 0.3 collective-permute-done.4.other_ref.refs_8_
  28.1 0.1 shard_map.216.mine_ref
  28.2 5.5 %collective-permute-start.5 = (bf16[16,3712]{1,0:T(8,128)(2,1)S(1)}, bf16[16,3712]{1,0:T(8,128)(2,1)S(1)}, u32[]{:S(2)}, u32[]{:S(2)}) collective-permute-start(bf16[16,3712]{1,0:T(8,128)(2,1)S(1)} %shard_map.216.mine_ref), channel_id=1, source_target_pairs={{0,2},{1,3},{2,4},{3,5},{4,6},{5,7},{8,10},{9,11},{10,12},{11,13},... | collective-permute-start | bytes 356360 | tf_op jit(solution)/shard_map/ppermute | solution.py:709
  33.7 0.0 copy-start
  33.7 3.6 %shard_map.217 = (f32[128,1280]{1,0:T(8,128)S(1)}, bf16[1600,1376]{1,0:T(8,128)(2,1)S(1)}) custom-call(bf16[1600,1376]{1,0:T(8,128)(2,1)} %refs_0_.5, f32[25,128]{1,0:T(8,128)S(1)} %get-tuple-element.63.refs_8_.rate_s.rate_ref.refs_1_.refs_2_.refs_3_, f32[128,3200]{1,0:T(8,128)S(1)} %get-tuple-element.85.refs_2_.refs_3_, ...), custom_call_target="tpu_custom_call" | custom-call | flops 1150000000 | bytes 3600000 | tf_op jit(solution)/shard_map/pallas_call | solution.py:689
  37.2 0.0 collective-permute-done.5.before_ref.refs_5_
  37.3 0.1 shard_map.218
  37.4 3.6 %collective-permute-start.6 = (bf16[16,3712]{1,0:T(8,128)(2,1)S(1)}, bf16[16,3712]{1,0:T(8,128)(2,1)S(1)}, u32[]{:S(2)}, u32[]{:S(2)}) collective-permute-start(bf16[16,3712]{1,0:T(8,128)(2,1)S(1)} %shard_map.218), channel_id=1, source_target_pairs={{0,4},{1,5},{2,6},{3,7},{8,12},{9,13},{10,14},{11,15},{16,20},{17,... | collective-permute-start | bytes 356360 | tf_op jit(solution)/shard_map/ppermute | solution.py:709
  41.0 0.0 copy-done
  41.0 5.3 %shard_map.219 = (f32[128,1920]{1,0:T(8,128)S(1)}, bf16[1600,1376]{1,0:T(8,128)(2,1)S(1)}, bf16[1600,1376]{1,0:T(8,128)(2,1)S(1)}) custom-call(bf16[1600,1376]{1,0:T(8,128)(2,1)} %refs_0_.6, bf16[1600,1376]{1,0:T(8,128)(2,1)} %bitcast.27, f32[25,128]{1,0:T(8,128)S(1)} %get-tuple-element.63.refs_8_.rate_s.rate_ref.refs_1_.refs_2_.refs_3_, ...), custom_call_target="tpu_custom_call" | custom-call | flops 1150000000 | bytes 3600000 | tf_op jit(solution)/shard_map/pallas_call | solution.py:689
  46.3 0.0 collective-permute-done.6.refs_6_
  46.3 8.1 %shard_map.220 = (f32[1600,128]{1,0:T(8,128)S(1)}, bf16[128,1600]{1,0:T(8,128)(2,1)S(1)}, f32[4,16,3200]{2,1,0:T(8,128)S(1)}) custom-call(s32[1,4]{1,0:T(1,128)} %lens_hbm.5, s32[1,4]{1,0:T(1,128)} %refs_1_.3, s32[1,4]{1,0:T(1,128)} %refs_2_.3, f32[25,128]{1,0:T(8,128)S(1)} %get-tuple-element.63.refs_8_.rate_s.rate_ref.refs_1_.refs_2_.refs_3_, ...), custom_call_target="tpu_custom_call" | custom-call | flops 6899999744 | bytes 21600000 | tf_op jit(solution)/shard_map/pallas_call | solution.py:689
  54.5 2.3 %collective-permute-start.7 = (bf16[128,1600]{1,0:T(8,128)(2,1)S(1)}, bf16[128,1600]{1,0:T(8,128)(2,1)S(1)}, u32[]{:S(2)}, u32[]{:S(2)}) collective-permute-start(bf16[128,1600]{1,0:T(8,128)(2,1)S(1)} %get-tuple-element.99.token_ref), channel_id=1, source_target_pairs={{0,8},{8,0},{16,24},{24,16},{1,9},{9,1},{17,25},{25,17},{2,10},{10... | collective-permute-start | bytes 1228808 | tf_op jit(solution)/shard_map/ppermute | solution.py:713
  56.8 0.8 collective-permute-start.8
  57.6 5.3 %shard_map.222 = (bf16[4,16,3840]{2,1,0:T(8,128)(2,1)S(1)}, bf16[4,16,3840]{2,1,0:T(8,128)(2,1)S(1)}) custom-call(s32[1,4]{1,0:T(1,128)} %lens_hbm.5, s32[1,4]{1,0:T(1,128)} %owner_hbm.1, f32[25,128]{1,0:T(8,128)S(1)} %get-tuple-element.63.refs_8_.rate_s.rate_ref.refs_1_.refs_2_.refs_3_, f32[128,3200]{1,0:T(8,128)S(1)} %get-tuple-element.79.step_ref, ...), custom_call_target="tpu_custom_call" | custom-call | flops 4600000000 | bytes 14400000 | tf_op jit(solution)/shard_map/pallas_call | solution.py:689
  62.9 3.1 %collective-permute-done.7.refs_0_ = bf16[128,1600]{1,0:T(8,128)(2,1)S(1)} collective-permute-done((bf16[128,1600]{1,0:T(8,128)(2,1)S(1)}, bf16[128,1600]{1,0:T(8,128)(2,1)S(1)}, u32[]{:S(2)}, u32[]{:S(2)}) %collective-permute-start.7) | collective-permute-done | bytes 409632 | tf_op jit(solution)/shard_map/ppermute | solution.py:713
  66.0 0.3 collective-permute-done.8.refs_1_
  66.3 0.0 collective-permute-start.13
  66.3 1.5 %collective-permute-start.11 = (bf16[64,1600]{1,0:T(8,128)(2,1)S(1)}, bf16[64,1600]{1,0:T(8,128)(2,1)S(1)}, u32[]{:S(2)}, u32[]{:S(2)}) collective-permute-start(bf16[64,1600]{1,0:T(8,128)(2,1)S(1)} %slice.30), channel_id=1, source_target_pairs={{0,8},{8,0},{16,24},{24,16},{1,9},{9,1},{17,25},{25,17},{2,10},{10... | collective-permute-start | bytes 614408 | tf_op jit(solution)/shard_map/ppermute | solution.py:713
  67.9 0.8 collective-permute-start.12
  68.7 4.5 %shard_map.223 = (bf16[128,1600]{1,0:T(8,128)(2,1)S(1)}, bf16[128,1600]{1,0:T(8,128)(2,1)S(1)}) custom-call(bf16[128,1600]{1,0:T(8,128)(2,1)S(1)} %collective-permute-done.7.refs_0_, bf16[128,1600]{1,0:T(8,128)(2,1)S(1)} %collective-permute-done.8.refs_1_, bf16[1600,1376]{1,0:T(8,128)(2,1)S(1)} %get-tuple-element.100.gate_ref.refs_2_, ...), custom_call_target="tpu_custom_call" | custom-call | flops 5175000064 | bytes 16200000 | tf_op jit(solution)/shard_map/pallas_call | solution.py:689
  73.2 1.4 %collective-permute-start.10 = (bf16[128,1600]{1,0:T(8,128)(2,1)S(1)}, bf16[128,1600]{1,0:T(8,128)(2,1)S(1)}, u32[]{:S(2)}, u32[]{:S(2)}) collective-permute-start(bf16[128,1600]{1,0:T(8,128)(2,1)S(1)} %get-tuple-element.111), channel_id=1, source_target_pairs={{0,16},{8,24},{16,0},{24,8},{1,17},{9,25},{17,1},{25,9},{2,18},{10... | collective-permute-start | bytes 1228808 | tf_op jit(solution)/shard_map/ppermute | solution.py:713
  74.6 0.5 collective-permute-start.9
  75.1 0.0 collective-permute-done.13
  75.2 0.1 add_bitcast_fusion
  75.2 0.0 collective-permute-done.11.low_ref
  75.2 0.1 collective-permute-done.12.high_ref
  75.3 1.2 %collective-permute-start.15 = (bf16[16,3840]{1,0:T(8,128)(2,1)S(1)}, bf16[16,3840]{1,0:T(8,128)(2,1)S(1)}, u32[]{:S(2)}, u32[]{:S(2)}) collective-permute-start(bf16[16,3840]{1,0:T(8,128)(2,1)S(1)} %get-tuple-element.118), channel_id=1, source_target_pairs={{0,2},{1,3},{2,4},{3,5},{4,6},{5,7},{6,0},{7,1},{8,10},{9,11},{10,... | collective-permute-start | bytes 368648 | tf_op jit(solution)/shard_map/ppermute | solution.py:704
  76.5 3.9 %collective-permute-start.16 = (bf16[16,3840]{1,0:T(8,128)(2,1)S(1)}, bf16[16,3840]{1,0:T(8,128)(2,1)S(1)}, u32[]{:S(2)}, u32[]{:S(2)}) collective-permute-start(bf16[16,3840]{1,0:T(8,128)(2,1)S(1)} %get-tuple-element.119), channel_id=1, source_target_pairs={{0,4},{1,5},{2,6},{3,7},{4,0},{5,1},{6,2},{7,3},{8,12},{9,13},{10,... | collective-permute-start | bytes 368648 | tf_op jit(solution)/shard_map/ppermute | solution.py:704
  80.4 0.0 collective-permute-start.17
  80.4 2.9 %shard_map.224 = bf16[128,1600]{1,0:T(8,128)(2,1)S(1)} custom-call(bf16[64,1600]{1,0:T(8,128)(2,1)S(1)} %collective-permute-done.11.low_ref, bf16[64,1600]{1,0:T(8,128)(2,1)S(1)} %collective-permute-done.12.high_ref, bf16[1600,1376]{1,0:T(8,128)(2,1)S(1)} %get-tuple-element.100.gate_ref.refs_2_, bf16[1600,1376]{1,0:T(8,128)(2,1)S(1)} %get-tuple-element.101.up_ref.refs_3_, ...), custom_call_target="tpu_custom_call" | custom-call | flops 3449999872 | bytes 10800000 | tf_op jit(solution)/shard_map/pallas_call | solution.py:689
  83.3 0.8 collective-permute-done.15.refs_1_
  84.1 1.8 %collective-permute-start.14 = (bf16[128,1600]{1,0:T(8,128)(2,1)S(1)}, bf16[128,1600]{1,0:T(8,128)(2,1)S(1)}, u32[]{:S(2)}, u32[]{:S(2)}) collective-permute-start(bf16[128,1600]{1,0:T(8,128)(2,1)S(1)} %shard_map.224), channel_id=1, source_target_pairs={{0,24},{8,16},{16,8},{24,0},{1,25},{9,17},{17,9},{25,1},{2,26},{10... | collective-permute-start | bytes 1228808 | tf_op jit(solution)/shard_map/ppermute | solution.py:713
  85.9 2.9 %shard_map.221.own_ref = f32[128,1600]{1,0:T(8,128)S(1)} custom-call(bf16[128,1600]{1,0:T(8,128)(2,1)S(1)} %get-tuple-element.99.token_ref, bf16[1600,1376]{1,0:T(8,128)(2,1)S(1)} %get-tuple-element.100.gate_ref.refs_2_, bf16[1600,1376]{1,0:T(8,128)(2,1)S(1)} %get-tuple-element.101.up_ref.refs_3_, bf16[1600,1376]{1,0:T(8,128)(2,1)S(1)} %get-tuple-element.102.down_ref.refs_4_), custom_call_target="tpu_custom_call" | custom-call | flops 3449999872 | bytes 10800000 | tf_op jit(solution)/shard_map/pallas_call | solution.py:689
  88.8 0.0 collective-permute-done.16.refs_2_
  88.8 0.0 collective-permute-done.17.refs_3_
  88.9 0.8 shard_map.226
  89.6 0.0 collective-permute-done.10.refs_1_
  89.6 0.0 collective-permute-done.9.refs_0_
  89.6 5.7 %collective-permute-done.14.refs_2_ = bf16[128,1600]{1,0:T(8,128)(2,1)S(1)} collective-permute-done((bf16[128,1600]{1,0:T(8,128)(2,1)S(1)}, bf16[128,1600]{1,0:T(8,128)(2,1)S(1)}, u32[]{:S(2)}, u32[]{:S(2)}) %collective-permute-start.14) | collective-permute-done | bytes 409632 | tf_op jit(solution)/shard_map/ppermute | solution.py:713
  95.3 1.1 %shard_map.225 = bf16[1600,128]{1,0:T(8,128)(2,1)} custom-call(f32[1600,128]{1,0:T(8,128)S(1)} %get-tuple-element.98.middle_ref, f32[128,1600]{1,0:T(8,128)S(1)} %shard_map.221.own_ref, bf16[128,1600]{1,0:T(8,128)(2,1)S(1)} %collective-permute-done.9.refs_0_, bf16[128,1600]{1,0:T(8,128)(2,1)S(1)} %collective-permute-done.10.refs_1_, ...), custom_call_target="tpu_custom_call" | custom-call | flops 1150000000 | bytes 3600000 | tf_op jit(solution)/shard_map/pallas_call | solution.py:689
  (4 shorter events, 0.1 us)
Async XLA Ops:
  1.7 12.0 %collective-permute-start = (bf16[24,3200]{1,0:T(8,128)(2,1)S(1)}, bf16[24,3200]{1,0:T(8,128)(2,1)S(1)}, u32[]{:S(2)}, u32[]{:S(2)}) collective-permute-start(bf16[24,3200]{1,0:T(8,128)(2,1)S(1)} %shard_map.212.refs_0_.refs_14_), channel_id=1, source_target_pairs={{0,2},{1,3},{2,4},{3,5},{4,6},{5,7},{6,0},{7,1},{8,10},{9,11},{10,... | collective-permute-start | bytes 460808 | tf_op jit(solution)/shard_map/ppermute | solution.py:704
  4.8 12.7 %collective-permute-start.1 = (bf16[24,3200]{1,0:T(8,128)(2,1)S(1)}, bf16[24,3200]{1,0:T(8,128)(2,1)S(1)}, u32[]{:S(2)}, u32[]{:S(2)}) collective-permute-start(bf16[24,3200]{1,0:T(8,128)(2,1)S(1)} %shard_map.212.refs_0_.refs_14_), channel_id=1, source_target_pairs={{0,4},{1,5},{2,6},{3,7},{4,0},{5,1},{6,2},{7,3},{8,12},{9,13},{10,... | collective-permute-start | bytes 460808 | tf_op jit(solution)/shard_map/ppermute | solution.py:704
  7.4 10.1 %collective-permute-start.2 = (bf16[24,3200]{1,0:T(8,128)(2,1)S(1)}, bf16[24,3200]{1,0:T(8,128)(2,1)S(1)}, u32[]{:S(2)}, u32[]{:S(2)}) collective-permute-start(bf16[24,3200]{1,0:T(8,128)(2,1)S(1)} %shard_map.212.refs_0_.refs_14_), channel_id=1, source_target_pairs={{0,6},{1,7},{2,0},{3,1},{4,2},{5,3},{6,4},{7,5},{8,14},{9,15},{10,... | collective-permute-start | bytes 460808 | tf_op jit(solution)/shard_map/ppermute | solution.py:704
  17.5 1.5 %collective-permute-start.3 = (bf16[4,8,3200]{2,1,0:T(8,128)(2,1)S(1)}, bf16[4,8,3200]{2,1,0:T(8,128)(2,1)S(1)}, u32[]{:S(2)}, u32[]{:S(2)}) collective-permute-start(bf16[4,8,3200]{2,1,0:T(8,128)(2,1)S(1)} %shard_map.213.refs_12_), channel_id=1, source_target_pairs={{0,1},{1,0},{2,3},{3,2},{4,5},{5,4},{6,7},{7,6},{8,9},{9,8},{10,11... | collective-permute-start | bytes 614408 | tf_op jit(solution)/shard_map/ppermute | solution.py:713
  26.0 2.1 %collective-permute-start.4 = (bf16[5,16,3712]{2,1,0:T(8,128)(2,1)S(1)}, bf16[5,16,3712]{2,1,0:T(8,128)(2,1)S(1)}, u32[]{:S(2)}, u32[]{:S(2)}) collective-permute-start(bf16[5,16,3712]{2,1,0:T(8,128)(2,1)S(1)} %get-tuple-element.78.mine_ref.refs_7_), channel_id=1, source_target_pairs={{0,1},{1,0},{2,3},{3,2},{4,5},{5,4},{6,7},{7,6},{8,9},{9,8},{10,11... | collective-permute-start | bytes 1781768 | tf_op jit(solution)/shard_map/ppermute | solution.py:713
  28.2 9.1 %collective-permute-start.5 = (bf16[16,3712]{1,0:T(8,128)(2,1)S(1)}, bf16[16,3712]{1,0:T(8,128)(2,1)S(1)}, u32[]{:S(2)}, u32[]{:S(2)}) collective-permute-start(bf16[16,3712]{1,0:T(8,128)(2,1)S(1)} %shard_map.216.mine_ref), channel_id=1, source_target_pairs={{0,2},{1,3},{2,4},{3,5},{4,6},{5,7},{8,10},{9,11},{10,12},{11,13},... | collective-permute-start | bytes 356360 | tf_op jit(solution)/shard_map/ppermute | solution.py:709
  33.7 7.3 %copy-start = (f32[1600]{0:T(1024)S(1)}, f32[1600]{0:T(1024)}, u32[]{:S(2)}) copy-start(f32[1600]{0:T(1024)} %param.30) | copy-start | bytes 19204
  37.4 8.9 %collective-permute-start.6 = (bf16[16,3712]{1,0:T(8,128)(2,1)S(1)}, bf16[16,3712]{1,0:T(8,128)(2,1)S(1)}, u32[]{:S(2)}, u32[]{:S(2)}) collective-permute-start(bf16[16,3712]{1,0:T(8,128)(2,1)S(1)} %shard_map.218), channel_id=1, source_target_pairs={{0,4},{1,5},{2,6},{3,7},{8,12},{9,13},{10,14},{11,15},{16,20},{17,... | collective-permute-start | bytes 356360 | tf_op jit(solution)/shard_map/ppermute | solution.py:709
  54.5 11.6 %collective-permute-start.7 = (bf16[128,1600]{1,0:T(8,128)(2,1)S(1)}, bf16[128,1600]{1,0:T(8,128)(2,1)S(1)}, u32[]{:S(2)}, u32[]{:S(2)}) collective-permute-start(bf16[128,1600]{1,0:T(8,128)(2,1)S(1)} %get-tuple-element.99.token_ref), channel_id=1, source_target_pairs={{0,8},{8,0},{16,24},{24,16},{1,9},{9,1},{17,25},{25,17},{2,10},{10... | collective-permute-start | bytes 1228808 | tf_op jit(solution)/shard_map/ppermute | solution.py:713
  56.8 9.5 %collective-permute-start.8 = (bf16[128,1600]{1,0:T(8,128)(2,1)S(1)}, bf16[128,1600]{1,0:T(8,128)(2,1)S(1)}, u32[]{:S(2)}, u32[]{:S(2)}) collective-permute-start(bf16[128,1600]{1,0:T(8,128)(2,1)S(1)} %get-tuple-element.99.token_ref), channel_id=1, source_target_pairs={{0,16},{8,24},{16,0},{24,8},{1,17},{9,25},{17,1},{25,9},{2,18},{10... | collective-permute-start | bytes 1228808 | tf_op jit(solution)/shard_map/ppermute | solution.py:713
  66.3 8.8 %collective-permute-start.13 = (bf16[4,16,3840]{2,1,0:T(8,128)(2,1)S(1)}, bf16[4,16,3840]{2,1,0:T(8,128)(2,1)S(1)}, u32[]{:S(2)}, u32[]{:S(2)}) collective-permute-start(bf16[4,16,3840]{2,1,0:T(8,128)(2,1)S(1)} %get-tuple-element.113), channel_id=1, source_target_pairs={{0,1},{1,0},{2,3},{3,2},{4,5},{5,4},{6,7},{7,6},{8,9},{9,8},{10,11... | collective-permute-start | bytes 1474568 | tf_op jit(solution)/shard_map/ppermute | solution.py:713
  66.3 8.9 %collective-permute-start.11 = (bf16[64,1600]{1,0:T(8,128)(2,1)S(1)}, bf16[64,1600]{1,0:T(8,128)(2,1)S(1)}, u32[]{:S(2)}, u32[]{:S(2)}) collective-permute-start(bf16[64,1600]{1,0:T(8,128)(2,1)S(1)} %slice.30), channel_id=1, source_target_pairs={{0,8},{8,0},{16,24},{24,16},{1,9},{9,1},{17,25},{25,17},{2,10},{10... | collective-permute-start | bytes 614408 | tf_op jit(solution)/shard_map/ppermute | solution.py:713
  67.9 7.4 %collective-permute-start.12 = (bf16[64,1600]{1,0:T(8,128)(2,1)S(1)}, bf16[64,1600]{1,0:T(8,128)(2,1)S(1)}, u32[]{:S(2)}, u32[]{:S(2)}) collective-permute-start(bf16[64,1600]{1,0:T(8,128)(2,1)S(1)} %slice.31), channel_id=1, source_target_pairs={{0,16},{8,24},{16,0},{24,8},{1,17},{9,25},{17,1},{25,9},{2,18},{10... | collective-permute-start | bytes 614408 | tf_op jit(solution)/shard_map/ppermute | solution.py:713
  73.2 16.4 %collective-permute-start.10 = (bf16[128,1600]{1,0:T(8,128)(2,1)S(1)}, bf16[128,1600]{1,0:T(8,128)(2,1)S(1)}, u32[]{:S(2)}, u32[]{:S(2)}) collective-permute-start(bf16[128,1600]{1,0:T(8,128)(2,1)S(1)} %get-tuple-element.111), channel_id=1, source_target_pairs={{0,16},{8,24},{16,0},{24,8},{1,17},{9,25},{17,1},{25,9},{2,18},{10... | collective-permute-start | bytes 1228808 | tf_op jit(solution)/shard_map/ppermute | solution.py:713
  74.6 15.0 %collective-permute-start.9 = (bf16[128,1600]{1,0:T(8,128)(2,1)S(1)}, bf16[128,1600]{1,0:T(8,128)(2,1)S(1)}, u32[]{:S(2)}, u32[]{:S(2)}) collective-permute-start(bf16[128,1600]{1,0:T(8,128)(2,1)S(1)} %get-tuple-element.110), channel_id=1, source_target_pairs={{0,8},{8,0},{16,24},{24,16},{1,9},{9,1},{17,25},{25,17},{2,10},{10... | collective-permute-start | bytes 1228808 | tf_op jit(solution)/shard_map/ppermute | solution.py:713
  75.3 8.8 %collective-permute-start.15 = (bf16[16,3840]{1,0:T(8,128)(2,1)S(1)}, bf16[16,3840]{1,0:T(8,128)(2,1)S(1)}, u32[]{:S(2)}, u32[]{:S(2)}) collective-permute-start(bf16[16,3840]{1,0:T(8,128)(2,1)S(1)} %get-tuple-element.118), channel_id=1, source_target_pairs={{0,2},{1,3},{2,4},{3,5},{4,6},{5,7},{6,0},{7,1},{8,10},{9,11},{10,... | collective-permute-start | bytes 368648 | tf_op jit(solution)/shard_map/ppermute | solution.py:704
  76.5 12.3 %collective-permute-start.16 = (bf16[16,3840]{1,0:T(8,128)(2,1)S(1)}, bf16[16,3840]{1,0:T(8,128)(2,1)S(1)}, u32[]{:S(2)}, u32[]{:S(2)}) collective-permute-start(bf16[16,3840]{1,0:T(8,128)(2,1)S(1)} %get-tuple-element.119), channel_id=1, source_target_pairs={{0,4},{1,5},{2,6},{3,7},{4,0},{5,1},{6,2},{7,3},{8,12},{9,13},{10,... | collective-permute-start | bytes 368648 | tf_op jit(solution)/shard_map/ppermute | solution.py:704
  80.4 8.5 %collective-permute-start.17 = (bf16[16,3840]{1,0:T(8,128)(2,1)S(1)}, bf16[16,3840]{1,0:T(8,128)(2,1)S(1)}, u32[]{:S(2)}, u32[]{:S(2)}) collective-permute-start(bf16[16,3840]{1,0:T(8,128)(2,1)S(1)} %get-tuple-element.120), channel_id=1, source_target_pairs={{0,6},{1,7},{2,0},{3,1},{4,2},{5,3},{6,4},{7,5},{8,14},{9,15},{10,... | collective-permute-start | bytes 368648 | tf_op jit(solution)/shard_map/ppermute | solution.py:704
  84.1 11.2 %collective-permute-start.14 = (bf16[128,1600]{1,0:T(8,128)(2,1)S(1)}, bf16[128,1600]{1,0:T(8,128)(2,1)S(1)}, u32[]{:S(2)}, u32[]{:S(2)}) collective-permute-start(bf16[128,1600]{1,0:T(8,128)(2,1)S(1)} %shard_map.224), channel_id=1, source_target_pairs={{0,24},{8,16},{16,8},{24,0},{1,25},{9,17},{17,9},{25,1},{2,26},{10... | collective-permute-start | bytes 1228808 | tf_op jit(solution)/shard_map/ppermute | solution.py:713

commit v3 on v2

--- a/solution.py
+++ b/solution.py
@@ -327,7 +327,7 @@
         return carry
 
     sums_s[...] = jnp.zeros(sums_s.shape, F32)
-    lax.fori_loop(0, inner // LANE, tile_step, 0, unroll=5)
+    lax.fori_loop(0, inner // LANE, tile_step, 0, unroll=True)
     write_sums(ext_ref, sums_s[...], inner)
 
 
@@ -443,7 +443,7 @@
 
         lax.fori_loop(
             0, row_count // 8, row_step, tuple(jnp.zeros((STATE, LANE), F32) for _ in range(tiles)),
-            unroll=2,
+            unroll=4,
         )
         return carry
 

time: 96.7 us -> 97.4 us (level)
  waiting for transfers between devices: 15.5 us -> 18.6 us
  starting transfers between devices: 30.5 us -> 28.7 us
    ppermute x10, waiting for transfers between devices: 10.9 us -> 13.8 us  [swapped(): lax.ppermute(block, axis, [(i, i ^ mask) for i in range(lax.axis_size(axi...]
    ppermute x10, starting transfers between devices: 9.44 us -> 8.04 us  [swapped(): lax.ppermute(block, axis, [(i, i ^ mask) for i in range(lax.axis_size(axi...]
  transfers between devices with their start and end apart: 18 -> 18, of which waited for: 8 -> 7; matrix products, arithmetic and copies ran while one was open for 0% -> 0% of each run, Pallas kernels for 33% -> 33%
where the time goes in v3:
time: 97.4 us; the launch traced here: 97.6 us
  Pallas kernels  49.3 us (51%)
  starting transfers between devices  28.7 us (29%)
  waiting for transfers between devices  18.6 us (19%)
    pallas_call x16, Pallas kernels, call(): pl.pallas_call(kernel, out_shape=tuple((out_kind(shape, dtype) for shape,...  49.3 us
    ppermute x10, waiting for transfers between devices, swapped(): lax.ppermute(block, axis, [(i, i ^ mask) for i in range(lax.axis_size(axi...  13.8 us
    ppermute x6, starting transfers between devices, shifted(): lax.ppermute(block, axis, [(i, (i + distance) % size) for i in range(size)])  11.3 us
    ppermute x2, starting transfers between devices, passed_up(): lax.ppermute(block, axis, [(i, i + distance) for i in range(size - distan...  9.31 us
    ppermute x10, starting transfers between devices, swapped(): lax.ppermute(block, axis, [(i, i ^ mask) for i in range(lax.axis_size(axi...  8.04 us
    ppermute x6, waiting for transfers between devices, shifted(): lax.ppermute(block, axis, [(i, (i + distance) % size) for i in range(size)])  4.79 us
  transfers between devices with their start and end apart: 18, of which 7 were waited for; matrix products, arithmetic and copies ran while one was open for 0% of the time, Pallas kernels for 33%

profile of v3, /device:TPU:0, one launch (start us, length us, event | category | flops | bytes accessed | tf_op | source)
XLA Modules:
  0.0 97.6 jit_solution(16419865965233008560)
XLA Ops:
  0.6 1.1 %shard_map.212.refs_0_.refs_14_ = bf16[24,3200]{1,0:T(8,128)(2,1)S(1)} custom-call(f32[16,3200]{1,0:T(8,128)} %bitcast.36, bf16[3,3200]{1,0:T(4,128)(2,1)} %bitcast.37, bf16[128,3200]{1,0:T(8,128)(2,1)} %bitcast.29), custom_call_target="tpu_custom_call" | custom-call | flops 1150000000 | bytes 3600000 | tf_op jit(solution)/shard_map/pallas_call | solution.py:689
  1.7 3.1 %collective-permute-start = (bf16[24,3200]{1,0:T(8,128)(2,1)S(1)}, bf16[24,3200]{1,0:T(8,128)(2,1)S(1)}, u32[]{:S(2)}, u32[]{:S(2)}) collective-permute-start(bf16[24,3200]{1,0:T(8,128)(2,1)S(1)} %shard_map.212.refs_0_.refs_14_), channel_id=1, source_target_pairs={{0,2},{1,3},{2,4},{3,5},{4,6},{5,7},{6,0},{7,1},{8,10},{9,11},{10,... | collective-permute-start | bytes 460808 | tf_op jit(solution)/shard_map/ppermute | solution.py:704
  4.8 2.6 %collective-permute-start.1 = (bf16[24,3200]{1,0:T(8,128)(2,1)S(1)}, bf16[24,3200]{1,0:T(8,128)(2,1)S(1)}, u32[]{:S(2)}, u32[]{:S(2)}) collective-permute-start(bf16[24,3200]{1,0:T(8,128)(2,1)S(1)} %shard_map.212.refs_0_.refs_14_), channel_id=1, source_target_pairs={{0,4},{1,5},{2,6},{3,7},{4,0},{5,1},{6,2},{7,3},{8,12},{9,13},{10,... | collective-permute-start | bytes 460808 | tf_op jit(solution)/shard_map/ppermute | solution.py:704
  7.4 1.3 %collective-permute-start.2 = (bf16[24,3200]{1,0:T(8,128)(2,1)S(1)}, bf16[24,3200]{1,0:T(8,128)(2,1)S(1)}, u32[]{:S(2)}, u32[]{:S(2)}) collective-permute-start(bf16[24,3200]{1,0:T(8,128)(2,1)S(1)} %shard_map.212.refs_0_.refs_14_), channel_id=1, source_target_pairs={{0,6},{1,7},{2,0},{3,1},{4,2},{5,3},{6,4},{7,5},{8,14},{9,15},{10,... | collective-permute-start | bytes 460808 | tf_op jit(solution)/shard_map/ppermute | solution.py:704
  8.7 4.9 %shard_map.211 = (f32[128,3200]{1,0:T(8,128)S(1)}, f32[136,3200]{1,0:T(8,128)S(1)}, f32[4,3200]{1,0:T(4,128)S(1)}, f32[25,128]{1,0:T(8,128)S(1)}, f32[25,128]{1,...) custom-call(s32[1,4]{1,0:T(1,128)} %lens_hbm.5, ...), custom_call_target="tpu_custom_call" | custom-call | flops 1150000000 | bytes 3600000 | tf_op jit(solution)/shard_map/pallas_call | solution.py:689
  13.7 0.0 collective-permute-done.refs_1_.refs_15_
  13.7 3.8 %collective-permute-done.1.refs_2_.refs_16_ = bf16[24,3200]{1,0:T(8,128)(2,1)S(1)} collective-permute-done((bf16[24,3200]{1,0:T(8,128)(2,1)S(1)}, bf16[24,3200]{1,0:T(8,128)(2,1)S(1)}, u32[]{:S(2)}, u32[]{:S(2)}) %collective-permute-start.1) | collective-permute-done | bytes 153632 | tf_op jit(solution)/shard_map/ppermute | solution.py:704
  17.5 0.0 collective-permute-done.2.refs_3_.refs_17_
  17.5 0.1 collective-permute-start.3
  17.6 1.4 %collective-permute-done.3.refs_13_ = bf16[4,8,3200]{2,1,0:T(8,128)(2,1)S(1)} collective-permute-done((bf16[4,8,3200]{2,1,0:T(8,128)(2,1)S(1)}, bf16[4,8,3200]{2,1,0:T(8,128)(2,1)S(1)}, u32[]{:S(2)}, u32[]{:S(2)}) %collective-permute-start.3) | collective-permute-done | bytes 204832 | tf_op jit(solution)/shard_map/ppermute | solution.py:713
  19.0 7.1 %shard_map.214 = (f32[128,3200]{1,0:T(8,128)S(1)}, f32[128,3200]{1,0:T(8,128)S(1)}, f32[128,3200]{1,0:T(8,128)S(1)}, f32[128,3200]{1,0:T(8,128)S(1)}, f32[128,32...) custom-call(s32[1,4]{1,0:T(1,128)} %lens_hbm.5, ...), custom_call_target="tpu_custom_call" | custom-call | flops 1150000000 | bytes 3600000 | tf_op jit(solution)/shard_map/pallas_call | solution.py:689
  26.1 0.1 collective-permute-start.4
  26.2 1.7 %shard_map.215 = (f32[128,16,128]{2,1,0:T(8,128)S(1)}, f32[128,16,128]{2,1,0:T(8,128)S(1)}, f32[128,3200]{1,0:T(8,128)S(1)}) custom-call(s32[1,4]{1,0:T(1,128)} %lens_hbm.5, f32[25,128]{1,0:T(8,128)S(1)} %get-tuple-element.63.refs_8_.rate_s.rate_ref.refs_1_.refs_2_.refs_3_, f32[128,3200]{1,0:T(8,128)S(1)} %get-tuple-element.79.step_ref, ...), custom_call_target="tpu_custom_call" | custom-call | flops 1150000000 | bytes 3600000 | tf_op jit(solution)/shard_map/pallas_call | solution.py:689
  27.9 0.3 collective-permute-done.4.other_ref.refs_8_
  28.1 0.1 shard_map.216.mine_ref
  28.3 5.5 %collective-permute-start.5 = (bf16[16,3712]{1,0:T(8,128)(2,1)S(1)}, bf16[16,3712]{1,0:T(8,128)(2,1)S(1)}, u32[]{:S(2)}, u32[]{:S(2)}) collective-permute-start(bf16[16,3712]{1,0:T(8,128)(2,1)S(1)} %shard_map.216.mine_ref), channel_id=1, source_target_pairs={{0,2},{1,3},{2,4},{3,5},{4,6},{5,7},{8,10},{9,11},{10,12},{11,13},... | collective-permute-start | bytes 356360 | tf_op jit(solution)/shard_map/ppermute | solution.py:709
  33.7 0.0 copy-start
  33.8 3.5 %shard_map.217 = (f32[128,1280]{1,0:T(8,128)S(1)}, bf16[1600,1376]{1,0:T(8,128)(2,1)S(1)}) custom-call(bf16[1600,1376]{1,0:T(8,128)(2,1)} %refs_0_.5, f32[25,128]{1,0:T(8,128)S(1)} %get-tuple-element.63.refs_8_.rate_s.rate_ref.refs_1_.refs_2_.refs_3_, f32[128,3200]{1,0:T(8,128)S(1)} %get-tuple-element.85.refs_2_.refs_3_, ...), custom_call_target="tpu_custom_call" | custom-call | flops 1150000000 | bytes 3600000 | tf_op jit(solution)/shard_map/pallas_call | solution.py:689
  37.2 0.0 collective-permute-done.5.before_ref.refs_5_
  37.3 0.1 shard_map.218
  37.4 3.9 %collective-permute-start.6 = (bf16[16,3712]{1,0:T(8,128)(2,1)S(1)}, bf16[16,3712]{1,0:T(8,128)(2,1)S(1)}, u32[]{:S(2)}, u32[]{:S(2)}) collective-permute-start(bf16[16,3712]{1,0:T(8,128)(2,1)S(1)} %shard_map.218), channel_id=1, source_target_pairs={{0,4},{1,5},{2,6},{3,7},{8,12},{9,13},{10,14},{11,15},{16,20},{17,... | collective-permute-start | bytes 356360 | tf_op jit(solution)/shard_map/ppermute | solution.py:709
  41.2 0.0 copy-done
  41.3 5.2 %shard_map.219 = (f32[128,1920]{1,0:T(8,128)S(1)}, bf16[1600,1376]{1,0:T(8,128)(2,1)S(1)}, bf16[1600,1376]{1,0:T(8,128)(2,1)S(1)}) custom-call(bf16[1600,1376]{1,0:T(8,128)(2,1)} %refs_0_.6, bf16[1600,1376]{1,0:T(8,128)(2,1)} %bitcast.27, f32[25,128]{1,0:T(8,128)S(1)} %get-tuple-element.63.refs_8_.rate_s.rate_ref.refs_1_.refs_2_.refs_3_, ...), custom_call_target="tpu_custom_call" | custom-call | flops 1150000000 | bytes 3600000 | tf_op jit(solution)/shard_map/pallas_call | solution.py:689
  46.5 0.0 collective-permute-done.6.refs_6_
  46.5 7.9 %shard_map.220 = (f32[1600,128]{1,0:T(8,128)S(1)}, bf16[128,1600]{1,0:T(8,128)(2,1)S(1)}, f32[4,16,3200]{2,1,0:T(8,128)S(1)}) custom-call(s32[1,4]{1,0:T(1,128)} %lens_hbm.5, s32[1,4]{1,0:T(1,128)} %refs_1_.3, s32[1,4]{1,0:T(1,128)} %refs_2_.3, f32[25,128]{1,0:T(8,128)S(1)} %get-tuple-element.63.refs_8_.rate_s.rate_ref.refs_1_.refs_2_.refs_3_, ...), custom_call_target="tpu_custom_call" | custom-call | flops 6899999744 | bytes 21600000 | tf_op jit(solution)/shard_map/pallas_call | solution.py:689
  54.5 0.6 collective-permute-start.7
  55.1 1.5 %collective-permute-start.8 = (bf16[128,1600]{1,0:T(8,128)(2,1)S(1)}, bf16[128,1600]{1,0:T(8,128)(2,1)S(1)}, u32[]{:S(2)}, u32[]{:S(2)}) collective-permute-start(bf16[128,1600]{1,0:T(8,128)(2,1)S(1)} %get-tuple-element.99.token_ref), channel_id=1, source_target_pairs={{0,16},{8,24},{16,0},{24,8},{1,17},{9,25},{17,1},{25,9},{2,18},{10... | collective-permute-start | bytes 1228808 | tf_op jit(solution)/shard_map/ppermute | solution.py:713
  56.6 5.5 %shard_map.222 = (bf16[4,16,3840]{2,1,0:T(8,128)(2,1)S(1)}, bf16[4,16,3840]{2,1,0:T(8,128)(2,1)S(1)}) custom-call(s32[1,4]{1,0:T(1,128)} %lens_hbm.5, s32[1,4]{1,0:T(1,128)} %owner_hbm.1, f32[25,128]{1,0:T(8,128)S(1)} %get-tuple-element.63.refs_8_.rate_s.rate_ref.refs_1_.refs_2_.refs_3_, f32[128,3200]{1,0:T(8,128)S(1)} %get-tuple-element.79.step_ref, ...), custom_call_target="tpu_custom_call" | custom-call | flops 4600000000 | bytes 14400000 | tf_op jit(solution)/shard_map/pallas_call | solution.py:689
  62.1 4.5 %collective-permute-done.7.refs_0_ = bf16[128,1600]{1,0:T(8,128)(2,1)S(1)} collective-permute-done((bf16[128,1600]{1,0:T(8,128)(2,1)S(1)}, bf16[128,1600]{1,0:T(8,128)(2,1)S(1)}, u32[]{:S(2)}, u32[]{:S(2)}) %collective-permute-start.7) | collective-permute-done | bytes 409632 | tf_op jit(solution)/shard_map/ppermute | solution.py:713
  66.5 1.0 %collective-permute-done.8.refs_1_ = bf16[128,1600]{1,0:T(8,128)(2,1)S(1)} collective-permute-done((bf16[128,1600]{1,0:T(8,128)(2,1)S(1)}, bf16[128,1600]{1,0:T(8,128)(2,1)S(1)}, u32[]{:S(2)}, u32[]{:S(2)}) %collective-permute-start.8) | collective-permute-done | bytes 409632 | tf_op jit(solution)/shard_map/ppermute | solution.py:713
  67.6 0.1 collective-permute-start.13
  67.7 0.7 collective-permute-start.11
  68.5 1.5 %collective-permute-start.12 = (bf16[64,1600]{1,0:T(8,128)(2,1)S(1)}, bf16[64,1600]{1,0:T(8,128)(2,1)S(1)}, u32[]{:S(2)}, u32[]{:S(2)}) collective-permute-start(bf16[64,1600]{1,0:T(8,128)(2,1)S(1)} %slice.31), channel_id=1, source_target_pairs={{0,16},{8,24},{16,0},{24,8},{1,17},{9,25},{17,1},{25,9},{2,18},{10... | collective-permute-start | bytes 614408 | tf_op jit(solution)/shard_map/ppermute | solution.py:713
  69.9 4.5 %shard_map.223 = (bf16[128,1600]{1,0:T(8,128)(2,1)S(1)}, bf16[128,1600]{1,0:T(8,128)(2,1)S(1)}) custom-call(bf16[128,1600]{1,0:T(8,128)(2,1)S(1)} %collective-permute-done.7.refs_0_, bf16[128,1600]{1,0:T(8,128)(2,1)S(1)} %collective-permute-done.8.refs_1_, bf16[1600,1376]{1,0:T(8,128)(2,1)S(1)} %get-tuple-element.100.gate_ref.refs_2_, ...), custom_call_target="tpu_custom_call" | custom-call | flops 5175000064 | bytes 16200000 | tf_op jit(solution)/shard_map/pallas_call | solution.py:689
  74.5 0.7 collective-permute-start.10
  75.2 1.4 %collective-permute-start.9 = (bf16[128,1600]{1,0:T(8,128)(2,1)S(1)}, bf16[128,1600]{1,0:T(8,128)(2,1)S(1)}, u32[]{:S(2)}, u32[]{:S(2)}) collective-permute-start(bf16[128,1600]{1,0:T(8,128)(2,1)S(1)} %get-tuple-element.110), channel_id=1, source_target_pairs={{0,8},{8,0},{16,24},{24,16},{1,9},{9,1},{17,25},{25,17},{2,10},{10... | collective-permute-start | bytes 1228808 | tf_op jit(solution)/shard_map/ppermute | solution.py:713
  76.5 0.0 collective-permute-done.13
  76.5 0.1 add_bitcast_fusion
  76.6 0.0 collective-permute-done.11.low_ref
  76.6 0.0 collective-permute-done.12.high_ref
  76.6 0.1 collective-permute-start.15
  76.7 4.2 %collective-permute-start.16 = (bf16[16,3840]{1,0:T(8,128)(2,1)S(1)}, bf16[16,3840]{1,0:T(8,128)(2,1)S(1)}, u32[]{:S(2)}, u32[]{:S(2)}) collective-permute-start(bf16[16,3840]{1,0:T(8,128)(2,1)S(1)} %get-tuple-element.119), channel_id=1, source_target_pairs={{0,4},{1,5},{2,6},{3,7},{4,0},{5,1},{6,2},{7,3},{8,12},{9,13},{10,... | collective-permute-start | bytes 368648 | tf_op jit(solution)/shard_map/ppermute | solution.py:704
  80.9 0.0 collective-permute-start.17
  80.9 2.9 %shard_map.224 = bf16[128,1600]{1,0:T(8,128)(2,1)S(1)} custom-call(bf16[64,1600]{1,0:T(8,128)(2,1)S(1)} %collective-permute-done.11.low_ref, bf16[64,1600]{1,0:T(8,128)(2,1)S(1)} %collective-permute-done.12.high_ref, bf16[1600,1376]{1,0:T(8,128)(2,1)S(1)} %get-tuple-element.100.gate_ref.refs_2_, bf16[1600,1376]{1,0:T(8,128)(2,1)S(1)} %get-tuple-element.101.up_ref.refs_3_, ...), custom_call_target="tpu_custom_call" | custom-call | flops 3449999872 | bytes 10800000 | tf_op jit(solution)/shard_map/pallas_call | solution.py:689
  83.9 1.0 %collective-permute-done.15.refs_1_ = bf16[16,3840]{1,0:T(8,128)(2,1)S(1)} collective-permute-done((bf16[16,3840]{1,0:T(8,128)(2,1)S(1)}, bf16[16,3840]{1,0:T(8,128)(2,1)S(1)}, u32[]{:S(2)}, u32[]{:S(2)}) %collective-permute-start.15) | collective-permute-done | bytes 122912 | tf_op jit(solution)/shard_map/ppermute | solution.py:704
  84.9 1.4 %collective-permute-start.14 = (bf16[128,1600]{1,0:T(8,128)(2,1)S(1)}, bf16[128,1600]{1,0:T(8,128)(2,1)S(1)}, u32[]{:S(2)}, u32[]{:S(2)}) collective-permute-start(bf16[128,1600]{1,0:T(8,128)(2,1)S(1)} %shard_map.224), channel_id=1, source_target_pairs={{0,24},{8,16},{16,8},{24,0},{1,25},{9,17},{17,9},{25,1},{2,26},{10... | collective-permute-start | bytes 1228808 | tf_op jit(solution)/shard_map/ppermute | solution.py:713
  86.3 2.9 %shard_map.221.own_ref = f32[128,1600]{1,0:T(8,128)S(1)} custom-call(bf16[128,1600]{1,0:T(8,128)(2,1)S(1)} %get-tuple-element.99.token_ref, bf16[1600,1376]{1,0:T(8,128)(2,1)S(1)} %get-tuple-element.100.gate_ref.refs_2_, bf16[1600,1376]{1,0:T(8,128)(2,1)S(1)} %get-tuple-element.101.up_ref.refs_3_, bf16[1600,1376]{1,0:T(8,128)(2,1)S(1)} %get-tuple-element.102.down_ref.refs_4_), custom_call_target="tpu_custom_call" | custom-call | flops 3449999872 | bytes 10800000 | tf_op jit(solution)/shard_map/pallas_call | solution.py:689
  89.2 0.0 collective-permute-done.16.refs_2_
  89.2 0.0 collective-permute-done.17.refs_3_
  89.2 0.8 shard_map.226
  89.9 0.0 collective-permute-done.10.refs_1_
  90.0 0.0 collective-permute-done.9.refs_0_
  90.0 6.6 %collective-permute-done.14.refs_2_ = bf16[128,1600]{1,0:T(8,128)(2,1)S(1)} collective-permute-done((bf16[128,1600]{1,0:T(8,128)(2,1)S(1)}, bf16[128,1600]{1,0:T(8,128)(2,1)S(1)}, u32[]{:S(2)}, u32[]{:S(2)}) %collective-permute-start.14) | collective-permute-done | bytes 409632 | tf_op jit(solution)/shard_map/ppermute | solution.py:713
  96.5 1.1 %shard_map.225 = bf16[1600,128]{1,0:T(8,128)(2,1)} custom-call(f32[1600,128]{1,0:T(8,128)S(1)} %get-tuple-element.98.middle_ref, f32[128,1600]{1,0:T(8,128)S(1)} %shard_map.221.own_ref, bf16[128,1600]{1,0:T(8,128)(2,1)S(1)} %collective-permute-done.9.refs_0_, bf16[128,1600]{1,0:T(8,128)(2,1)S(1)} %collective-permute-done.10.refs_1_, ...), custom_call_target="tpu_custom_call" | custom-call | flops 1150000000 | bytes 3600000 | tf_op jit(solution)/shard_map/pallas_call | solution.py:689
  (4 shorter events, 0.1 us)
Async XLA Ops:
  1.7 12.0 %collective-permute-start = (bf16[24,3200]{1,0:T(8,128)(2,1)S(1)}, bf16[24,3200]{1,0:T(8,128)(2,1)S(1)}, u32[]{:S(2)}, u32[]{:S(2)}) collective-permute-start(bf16[24,3200]{1,0:T(8,128)(2,1)S(1)} %shard_map.212.refs_0_.refs_14_), channel_id=1, source_target_pairs={{0,2},{1,3},{2,4},{3,5},{4,6},{5,7},{6,0},{7,1},{8,10},{9,11},{10,... | collective-permute-start | bytes 460808 | tf_op jit(solution)/shard_map/ppermute | solution.py:704
  4.8 12.7 %collective-permute-start.1 = (bf16[24,3200]{1,0:T(8,128)(2,1)S(1)}, bf16[24,3200]{1,0:T(8,128)(2,1)S(1)}, u32[]{:S(2)}, u32[]{:S(2)}) collective-permute-start(bf16[24,3200]{1,0:T(8,128)(2,1)S(1)} %shard_map.212.refs_0_.refs_14_), channel_id=1, source_target_pairs={{0,4},{1,5},{2,6},{3,7},{4,0},{5,1},{6,2},{7,3},{8,12},{9,13},{10,... | collective-permute-start | bytes 460808 | tf_op jit(solution)/shard_map/ppermute | solution.py:704
  7.4 10.1 %collective-permute-start.2 = (bf16[24,3200]{1,0:T(8,128)(2,1)S(1)}, bf16[24,3200]{1,0:T(8,128)(2,1)S(1)}, u32[]{:S(2)}, u32[]{:S(2)}) collective-permute-start(bf16[24,3200]{1,0:T(8,128)(2,1)S(1)} %shard_map.212.refs_0_.refs_14_), channel_id=1, source_target_pairs={{0,6},{1,7},{2,0},{3,1},{4,2},{5,3},{6,4},{7,5},{8,14},{9,15},{10,... | collective-permute-start | bytes 460808 | tf_op jit(solution)/shard_map/ppermute | solution.py:704
  17.5 1.5 %collective-permute-start.3 = (bf16[4,8,3200]{2,1,0:T(8,128)(2,1)S(1)}, bf16[4,8,3200]{2,1,0:T(8,128)(2,1)S(1)}, u32[]{:S(2)}, u32[]{:S(2)}) collective-permute-start(bf16[4,8,3200]{2,1,0:T(8,128)(2,1)S(1)} %shard_map.213.refs_12_), channel_id=1, source_target_pairs={{0,1},{1,0},{2,3},{3,2},{4,5},{5,4},{6,7},{7,6},{8,9},{9,8},{10,11... | collective-permute-start | bytes 614408 | tf_op jit(solution)/shard_map/ppermute | solution.py:713
  26.1 2.1 %collective-permute-start.4 = (bf16[5,16,3712]{2,1,0:T(8,128)(2,1)S(1)}, bf16[5,16,3712]{2,1,0:T(8,128)(2,1)S(1)}, u32[]{:S(2)}, u32[]{:S(2)}) collective-permute-start(bf16[5,16,3712]{2,1,0:T(8,128)(2,1)S(1)} %get-tuple-element.78.mine_ref.refs_7_), channel_id=1, source_target_pairs={{0,1},{1,0},{2,3},{3,2},{4,5},{5,4},{6,7},{7,6},{8,9},{9,8},{10,11... | collective-permute-start | bytes 1781768 | tf_op jit(solution)/shard_map/ppermute | solution.py:713
  28.3 9.0 %collective-permute-start.5 = (bf16[16,3712]{1,0:T(8,128)(2,1)S(1)}, bf16[16,3712]{1,0:T(8,128)(2,1)S(1)}, u32[]{:S(2)}, u32[]{:S(2)}) collective-permute-start(bf16[16,3712]{1,0:T(8,128)(2,1)S(1)} %shard_map.216.mine_ref), channel_id=1, source_target_pairs={{0,2},{1,3},{2,4},{3,5},{4,6},{5,7},{8,10},{9,11},{10,12},{11,13},... | collective-permute-start | bytes 356360 | tf_op jit(solution)/shard_map/ppermute | solution.py:709
  33.7 7.5 %copy-start = (f32[1600]{0:T(1024)S(1)}, f32[1600]{0:T(1024)}, u32[]{:S(2)}) copy-start(f32[1600]{0:T(1024)} %param.30) | copy-start | bytes 19204
  37.4 9.1 %collective-permute-start.6 = (bf16[16,3712]{1,0:T(8,128)(2,1)S(1)}, bf16[16,3712]{1,0:T(8,128)(2,1)S(1)}, u32[]{:S(2)}, u32[]{:S(2)}) collective-permute-start(bf16[16,3712]{1,0:T(8,128)(2,1)S(1)} %shard_map.218), channel_id=1, source_target_pairs={{0,4},{1,5},{2,6},{3,7},{8,12},{9,13},{10,14},{11,15},{16,20},{17,... | collective-permute-start | bytes 356360 | tf_op jit(solution)/shard_map/ppermute | solution.py:709
  54.5 12.1 %collective-permute-start.7 = (bf16[128,1600]{1,0:T(8,128)(2,1)S(1)}, bf16[128,1600]{1,0:T(8,128)(2,1)S(1)}, u32[]{:S(2)}, u32[]{:S(2)}) collective-permute-start(bf16[128,1600]{1,0:T(8,128)(2,1)S(1)} %get-tuple-element.99.token_ref), channel_id=1, source_target_pairs={{0,8},{8,0},{16,24},{24,16},{1,9},{9,1},{17,25},{25,17},{2,10},{10... | collective-permute-start | bytes 1228808 | tf_op jit(solution)/shard_map/ppermute | solution.py:713
  55.1 12.5 %collective-permute-start.8 = (bf16[128,1600]{1,0:T(8,128)(2,1)S(1)}, bf16[128,1600]{1,0:T(8,128)(2,1)S(1)}, u32[]{:S(2)}, u32[]{:S(2)}) collective-permute-start(bf16[128,1600]{1,0:T(8,128)(2,1)S(1)} %get-tuple-element.99.token_ref), channel_id=1, source_target_pairs={{0,16},{8,24},{16,0},{24,8},{1,17},{9,25},{17,1},{25,9},{2,18},{10... | collective-permute-start | bytes 1228808 | tf_op jit(solution)/shard_map/ppermute | solution.py:713
  67.6 9.0 %collective-permute-start.13 = (bf16[4,16,3840]{2,1,0:T(8,128)(2,1)S(1)}, bf16[4,16,3840]{2,1,0:T(8,128)(2,1)S(1)}, u32[]{:S(2)}, u32[]{:S(2)}) collective-permute-start(bf16[4,16,3840]{2,1,0:T(8,128)(2,1)S(1)} %get-tuple-element.113), channel_id=1, source_target_pairs={{0,1},{1,0},{2,3},{3,2},{4,5},{5,4},{6,7},{7,6},{8,9},{9,8},{10,11... | collective-permute-start | bytes 1474568 | tf_op jit(solution)/shard_map/ppermute | solution.py:713
  67.7 8.9 %collective-permute-start.11 = (bf16[64,1600]{1,0:T(8,128)(2,1)S(1)}, bf16[64,1600]{1,0:T(8,128)(2,1)S(1)}, u32[]{:S(2)}, u32[]{:S(2)}) collective-permute-start(bf16[64,1600]{1,0:T(8,128)(2,1)S(1)} %slice.30), channel_id=1, source_target_pairs={{0,8},{8,0},{16,24},{24,16},{1,9},{9,1},{17,25},{25,17},{2,10},{10... | collective-permute-start | bytes 614408 | tf_op jit(solution)/shard_map/ppermute | solution.py:713
  68.5 8.1 %collective-permute-start.12 = (bf16[64,1600]{1,0:T(8,128)(2,1)S(1)}, bf16[64,1600]{1,0:T(8,128)(2,1)S(1)}, u32[]{:S(2)}, u32[]{:S(2)}) collective-permute-start(bf16[64,1600]{1,0:T(8,128)(2,1)S(1)} %slice.31), channel_id=1, source_target_pairs={{0,16},{8,24},{16,0},{24,8},{1,17},{9,25},{17,1},{25,9},{2,18},{10... | collective-permute-start | bytes 614408 | tf_op jit(solution)/shard_map/ppermute | solution.py:713
  74.5 15.5 %collective-permute-start.10 = (bf16[128,1600]{1,0:T(8,128)(2,1)S(1)}, bf16[128,1600]{1,0:T(8,128)(2,1)S(1)}, u32[]{:S(2)}, u32[]{:S(2)}) collective-permute-start(bf16[128,1600]{1,0:T(8,128)(2,1)S(1)} %get-tuple-element.111), channel_id=1, source_target_pairs={{0,16},{8,24},{16,0},{24,8},{1,17},{9,25},{17,1},{25,9},{2,18},{10... | collective-permute-start | bytes 1228808 | tf_op jit(solution)/shard_map/ppermute | solution.py:713
  75.2 14.8 %collective-permute-start.9 = (bf16[128,1600]{1,0:T(8,128)(2,1)S(1)}, bf16[128,1600]{1,0:T(8,128)(2,1)S(1)}, u32[]{:S(2)}, u32[]{:S(2)}) collective-permute-start(bf16[128,1600]{1,0:T(8,128)(2,1)S(1)} %get-tuple-element.110), channel_id=1, source_target_pairs={{0,8},{8,0},{16,24},{24,16},{1,9},{9,1},{17,25},{25,17},{2,10},{10... | collective-permute-start | bytes 1228808 | tf_op jit(solution)/shard_map/ppermute | solution.py:713
  76.6 8.2 %collective-permute-start.15 = (bf16[16,3840]{1,0:T(8,128)(2,1)S(1)}, bf16[16,3840]{1,0:T(8,128)(2,1)S(1)}, u32[]{:S(2)}, u32[]{:S(2)}) collective-permute-start(bf16[16,3840]{1,0:T(8,128)(2,1)S(1)} %get-tuple-element.118), channel_id=1, source_target_pairs={{0,2},{1,3},{2,4},{3,5},{4,6},{5,7},{6,0},{7,1},{8,10},{9,11},{10,... | collective-permute-start | bytes 368648 | tf_op jit(solution)/shard_map/ppermute | solution.py:704
  76.7 12.4 %collective-permute-start.16 = (bf16[16,3840]{1,0:T(8,128)(2,1)S(1)}, bf16[16,3840]{1,0:T(8,128)(2,1)S(1)}, u32[]{:S(2)}, u32[]{:S(2)}) collective-permute-start(bf16[16,3840]{1,0:T(8,128)(2,1)S(1)} %get-tuple-element.119), channel_id=1, source_target_pairs={{0,4},{1,5},{2,6},{3,7},{4,0},{5,1},{6,2},{7,3},{8,12},{9,13},{10,... | collective-permute-start | bytes 368648 | tf_op jit(solution)/shard_map/ppermute | solution.py:704
  80.9 8.2 %collective-permute-start.17 = (bf16[16,3840]{1,0:T(8,128)(2,1)S(1)}, bf16[16,3840]{1,0:T(8,128)(2,1)S(1)}, u32[]{:S(2)}, u32[]{:S(2)}) collective-permute-start(bf16[16,3840]{1,0:T(8,128)(2,1)S(1)} %get-tuple-element.120), channel_id=1, source_target_pairs={{0,6},{1,7},{2,0},{3,1},{4,2},{5,3},{6,4},{7,5},{8,14},{9,15},{10,... | collective-permute-start | bytes 368648 | tf_op jit(solution)/shard_map/ppermute | solution.py:704
  84.9 11.7 %collective-permute-start.14 = (bf16[128,1600]{1,0:T(8,128)(2,1)S(1)}, bf16[128,1600]{1,0:T(8,128)(2,1)S(1)}, u32[]{:S(2)}, u32[]{:S(2)}) collective-permute-start(bf16[128,1600]{1,0:T(8,128)(2,1)S(1)} %shard_map.224), channel_id=1, source_target_pairs={{0,24},{8,16},{16,8},{24,0},{1,25},{9,17},{17,9},{25,1},{2,26},{10... | collective-permute-start | bytes 1228808 | tf_op jit(solution)/shard_map/ppermute | solution.py:713
